TPU v7x, 256 devices: a whole 4x4x8 slice. The times are simulated.
256 devices in a mesh: dp: 16 (over y_hi, x, core), tensor: 16 (over y_lo, z).
Axes of the slice: x: 4, y: 4 (y_hi: 2, y_lo: 2; y = y_hi * 2 + y_lo), z: 8, core: 2. Of those that a mesh axis runs over, the one named last changes fastest.
Arguments:
- context: bfloat16 [8192, 4096], P('dp', 'tensor'), parts along dimension 0, may hold values from -6 to 6
- residual_in: bfloat16 [8192, 4096], P(('dp', 'tensor')), parts along dimension 0, may hold values from -6 to 6
- out_weight: bfloat16 [4096, 4096], P('tensor'), may hold values from -0.09375 to 0.09375
- out_bias: float32 [4096], replicated, may hold values from -3 to 3
- norm_gain: float32 [4096], replicated, may hold values from 0.1 to 1.9
- norm_bias: float32 [4096], replicated, may hold values from -3 to 3
- gate_weight: bfloat16 [4096, 8192], P(None, 'tensor'), may hold values from -0.09375 to 0.09375
- up_weight: bfloat16 [4096, 8192], P(None, 'tensor'), may hold values from -0.09375 to 0.09375
Outputs:
- normed: bfloat16 [8192, 4096], P(('dp', 'tensor')), parts along dimension 0
- hidden: bfloat16 [8192, 8192], P('dp', 'tensor'), parts along dimension 0
There are 16 independent parts, one for each index of `dp`. A program takes and returns all parts, laid end to end along the dimension named above; an argument that names none is the same for every part. Nothing has to cross between parts.
All inputs are finite; a program needn't handle non-finite values.
Results may differ from a plain program's by a relative error of at most 0.029.
Values may be sent and summed in bfloat16 or wider, within the bound.
No kernel may reach another device: no remote copies, remote signals or barrier semaphores. Data moves between devices by JAX's collectives and lax.ppermute only.
A program may use at most 64 MiB of HBM per device.

v0:
```python
import jax
import jax.numpy as jnp
from jax import lax
from jax.sharding import PartitionSpec as P


def layer_norm(stream, norm_gain, norm_bias):
    center = jnp.mean(stream, axis=1, keepdims=True)
    spread = jnp.mean((stream - center) ** 2, axis=1, keepdims=True)
    return ((stream - center) / jnp.sqrt(spread + 1e-05) * norm_gain + norm_bias).astype(
        jnp.bfloat16
    )


def gated_units(normed_rows, gate_weight, up_weight):
    gate = jnp.dot(normed_rows, gate_weight, preferred_element_type=jnp.float32)
    up = jnp.dot(normed_rows, up_weight, preferred_element_type=jnp.float32)
    return (jax.nn.gelu(gate, approximate=False) * up).astype(jnp.bfloat16)


def shards(
    context, residual_in, out_weight, out_bias, norm_gain, norm_bias, gate_weight, up_weight
):
    attended = lax.psum_scatter(
        jnp.dot(context, out_weight, preferred_element_type=jnp.float32).astype(jnp.bfloat16),
        "tensor",
        scatter_dimension=0,
        tiled=True,
    ).astype(jnp.float32)
    stream = residual_in.astype(jnp.float32) + attended + out_bias
    normed = layer_norm(stream, norm_gain, norm_bias)
    hidden = gated_units(
        lax.all_gather(normed, "tensor", axis=0, tiled=True), gate_weight, up_weight
    )
    return (normed, hidden)


def solution(mesh):
    in_specs = (
        P("dp", "tensor"),
        P(("dp", "tensor"), None),
        P("tensor", None),
        P(),
        P(),
        P(),
        P(None, "tensor"),
        P(None, "tensor"),
    )
    out_specs = (P(("dp", "tensor"), None), P("dp", "tensor"))
    return jax.shard_map(shards, mesh=mesh, in_specs=in_specs, out_specs=out_specs, check_vma=False)
```

profile of v0, /device:TPU:6, one launch (start us, length us, event | category | flops | bytes accessed | tf_op | source)
XLA Modules:
  0.0 191.9 jit_solution(568064041384506153)
XLA Ops:
  7.2 0.0 copy-start
  7.2 0.0 copy-start.2
  7.2 0.0 copy-start.1
  7.2 0.0 reduce-scatter.2.cloned.1.call-start
  7.2 1.5 copy-done
  8.8 4.1 %convolution_convert_fusion = bf16[512,4096]{1,0:T(8,128)(2,1)} fusion(bf16[512,256]{1,0:T(8,128)(2,1)} %param.8, bf16[256,4096]{1,0:T(8,128)(2,1)S(1)} %copy-done), kind=kOutput, calls=%fused_computation | convolution fusion | flops 1075838976 | bytes 6553600 | tf_op jit(solution)/shard_map/dot_general | solution.py:25
  12.9 0.0 copy-start.3
  12.9 0.0 copy-start.4
  12.9 0.0 reduce-scatter.2.cloned.1.call-update
  12.9 0.0 all-gather.2.cloned.1.call-start
  13.0 83.6 %reduce-scatter.2.cloned.1.call-done = bf16[32,4096]{1,0:T(8,128)(2,1)} async-done(((bf16[512,4096]{1,0:T(8,128)(2,1)}), bf16[32,4096]{1,0:T(8,128)(2,1)}) %reduce-scatter.2.cloned.1.call-update) | async-done | bytes 262160 | tf_op jit(solution)/shard_map/reduce_scatter | solution.py:24
  96.6 0.0 copy-done.2
  96.6 0.0 copy-done.1
  96.6 1.1 fusion.10
  97.7 1.2 multiply_reduce_fusion
  98.9 0.0 copy-done.3
  98.9 0.0 copy-done.4
  98.9 1.8 add_convert_fusion
  100.7 0.0 all-gather.2.cloned.1.call-update
  100.8 73.2 %all-gather.2.cloned.1.call-done = bf16[512,4096]{1,0:T(8,128)(2,1)} async-done(((bf16[32,4096]{1,0:T(8,128)(2,1)}), bf16[512,4096]{1,0:T(8,128)(2,1)}) %all-gather.2.cloned.1.call-update) | async-done | bytes 4194320 | tf_op jit(solution)/shard_map/all_gather | solution.py:33
  174.0 5.9 %fusion.11 = f32[512,512]{1,0:T(8,128)S(1)} fusion(bf16[512,4096]{1,0:T(8,128)(2,1)} %all-gather.2.cloned.1.call-done, bf16[4096,512]{1,0:T(8,128)(2,1)} %param.14), kind=kOutput, calls=%fused_computation.27 | convolution fusion | flops 2147483648 | bytes 9437184 | tf_op jit(solution)/shard_map/dot_general | solution.py:16
  179.9 0.0 copy-done.5
  179.9 0.0 copy-done.6
  179.9 5.2 %fusion = bf16[512,512]{1,0:T(8,128)(2,1)} fusion(bf16[512,4096]{1,0:T(8,128)(2,1)S(1)} %copy-done.6, bf16[4096,512]{1,0:T(8,128)(2,1)S(1)} %copy-done.5, f32[512,512]{1,0:T(8,128)S(1)} %fusion.11), kind=kOutput, calls=%fused_computation.3 | convolution fusion | flops 2164785152 | bytes 9961472 | tf_op jit(solution)/shard_map/dot_general | solution.py:17
  (4 shorter events, 0.0 us)
Async XLA Ops:
  7.2 1.6 copy-start
  7.2 89.4 %copy-start.2 = (f32[4096]{0:T(1024)S(1)}, f32[4096]{0:T(1024)}, u32[]{:S(2)}) copy-start(f32[4096]{0:T(1024)} %param.11) | copy-start | bytes 49156
  7.2 89.4 %copy-start.1 = (bf16[32,4096]{1,0:T(8,128)(2,1)S(1)}, bf16[32,4096]{1,0:T(8,128)(2,1)}, u32[]{:S(2)}) copy-start(bf16[32,4096]{1,0:T(8,128)(2,1)} %param.9) | copy-start | bytes 786436
  7.2 89.4 %reduce-scatter.2.cloned.1.call-start = ((), (), s32[]{:S(2)}) async-start(), calls=%async_computation.1 | async-start | bytes 4456448 | tf_op jit(solution)/shard_map/reduce_scatter | solution.py:24
  12.9 86.0 %copy-start.3 = (f32[4096]{0:T(1024)S(1)}, f32[4096]{0:T(1024)}, u32[]{:S(2)}) copy-start(f32[4096]{0:T(1024)} %param.13) | copy-start | bytes 49156
  12.9 86.0 %copy-start.4 = (f32[4096]{0:T(1024)S(1)}, f32[4096]{0:T(1024)}, u32[]{:S(2)}) copy-start(f32[4096]{0:T(1024)} %param.12) | copy-start | bytes 49156
  12.9 161.0 %all-gather.2.cloned.1.call-start = ((), (), s32[]{:S(2)}) async-start(), calls=%async_computation.2 | async-start | bytes 4456448 | tf_op jit(solution)/shard_map/all_gather | solution.py:33
  174.0 5.9 %copy-start.5 = (bf16[4096,512]{1,0:T(8,128)(2,1)S(1)}, bf16[4096,512]{1,0:T(8,128)(2,1)}, u32[]{:S(2)}) copy-start(bf16[4096,512]{1,0:T(8,128)(2,1)} %param.15) | copy-start | bytes 12582916
  174.0 5.9 %copy-start.6 = (bf16[512,4096]{1,0:T(8,128)(2,1)S(1)}, bf16[512,4096]{1,0:T(8,128)(2,1)}, u32[]{:S(2)}) copy-start(bf16[512,4096]{1,0:T(8,128)(2,1)} %all-gather.2.cloned.1.call-done) | copy-start | bytes 12582916
Sparse Core Ops, SparseCore 0:
  13.1 83.4 reduce-scatter.1
  100.9 73.0 all-gather.1
where the time goes:
time: 192 us
  waiting for transfers between devices  157 us (82%)
  matrix products  15.2 us (8%)
  between operations  14.1 us (7%)
  other arithmetic  4.16 us (2%)
    reduce_scatter x1, waiting for transfers between devices, shards(): lax.psum_scatter(jnp.dot(context, out_weight, preferred_element_type=jnp....  83.6 us
    all_gather x1, waiting for transfers between devices, shards(): lax.all_gather(normed, 'tensor', axis=0, tiled=True)  73.2 us
    dot_general x1, matrix products, gated_units(): gate = jnp.dot(normed_rows, gate_weight, preferred_element_type=jnp.float32)  5.92 us
    dot_general x1, matrix products, gated_units(): up = jnp.dot(normed_rows, up_weight, preferred_element_type=jnp.float32)  5.16 us
    dot_general x1, matrix products, shards(): jnp.dot(context, out_weight, preferred_element_type=jnp.float32)  4.15 us
  transfers between devices with their start and end apart: 2, of which 2 were waited for; matrix products, arithmetic and copies ran while one was open for 0% of the time, Pallas kernels for 0%

commit v1 on v0

v1 whole, which is shorter than its diff:
```python
import jax
import jax.numpy as jnp
from jax import lax
from jax.sharding import PartitionSpec as P

ROWS = 32
RING = 8
HALF = ROWS // 2


def index_of(y, z):
    return (y % 2) * RING + z % RING


def ring_pairs(step):
    return [(index_of(y, z), index_of(y, z + step)) for y in range(2) for z in range(RING)]


UP, DOWN = ring_pairs(1), ring_pairs(-1)
ACROSS = [(index_of(y, z), index_of(y + 1, z)) for y in range(2) for z in range(RING)]


def send(value, pairs):
    return lax.ppermute(value, "tensor", pairs)


def shards(
    context, residual_in, out_weight, out_bias, norm_gain, norm_bias, gate_weight, up_weight
):
    me = lax.axis_index("tensor")
    y, z = me // RING, me % RING

    def start_of(other, dz):
        return (jnp.bitwise_xor(y, other) * RING + lax.rem(z + dz + RING, RING)) * ROWS

    def partial(*blocks):
        rows = [lax.dynamic_slice_in_dim(context, start_of(*b), ROWS, 0) for b in blocks]
        rows = jnp.concatenate(rows, 0) if len(rows) > 1 else rows[0]
        return jnp.dot(rows, out_weight, preferred_element_type=jnp.float32)

    def bf(value):
        return value.astype(jnp.bfloat16)

    def f32(value):
        return value.astype(jnp.float32)

    far = send(bf(partial((1, 4))), ACROSS)
    side_up = send(bf(partial((1, 2))), UP)
    side_down = send(bf(partial((1, -2))), DOWN)
    three = send(bf(partial((1, 3), (1, -3))), ACROSS)

    total = bf(partial((0, 4)) + f32(far))
    up, down = send(total[:HALF], UP), send(total[HALF:], DOWN)

    side_up = send(bf(partial((1, 1)) + f32(side_up)), UP)
    side_down = send(bf(partial((1, -1)) + f32(side_down)), DOWN)

    pad = jnp.zeros((HALF, up.shape[1]), jnp.bfloat16)
    up = jnp.concatenate([up, pad], 0)
    down = jnp.concatenate([pad, down], 0)
    up = send(bf(partial((0, 3)) + f32(three[:ROWS]) + f32(up)), UP)
    down = send(bf(partial((0, -3)) + f32(three[ROWS:]) + f32(down)), DOWN)

    side = send(bf(partial((1, 0)) + f32(side_up) + f32(side_down)), ACROSS)

    up = send(bf(partial((0, 2)) + f32(up)), UP)
    down = send(bf(partial((0, -2)) + f32(down)), DOWN)
    up = send(bf(partial((0, 1)) + f32(up)), UP)
    down = send(bf(partial((0, -1)) + f32(down)), DOWN)

    attended = partial((0, 0)) + f32(side) + f32(up) + f32(down)

    stream = f32(residual_in) + attended + out_bias
    center = jnp.mean(stream, axis=1, keepdims=True)
    spread = jnp.mean((stream - center) ** 2, axis=1, keepdims=True)
    normed = bf((stream - center) / jnp.sqrt(spread + 1e-05) * norm_gain + norm_bias)

    hidden = jnp.zeros((context.shape[0], gate_weight.shape[1]), jnp.bfloat16)

    def units(hidden, blocks):
        rows = jnp.concatenate([rows for rows, _ in blocks], 0)
        gate = jnp.dot(rows, gate_weight, preferred_element_type=jnp.float32)
        up = jnp.dot(rows, up_weight, preferred_element_type=jnp.float32)
        out = bf(jax.nn.gelu(gate, approximate=False) * up)
        for i, (_, block) in enumerate(blocks):
            hidden = lax.dynamic_update_slice_in_dim(
                hidden, out[i * ROWS : (i + 1) * ROWS], start_of(*block), 0
            )
        return hidden

    up1, down1 = send(normed, UP), send(normed, DOWN)
    other = send(normed, ACROSS)
    up2, down2 = send(up1, UP), send(down1, DOWN)
    side_up1, side_down1 = send(other, UP), send(other, DOWN)
    hidden = units(hidden, [(normed, (0, 0)), (other, (1, 0)), (up1, (0, -1)), (down1, (0, 1))])
    up3, down3 = send(up2, UP), send(down2, DOWN)
    side_up2, side_down2 = send(side_up1, UP), send(side_down1, DOWN)
    hidden = units(
        hidden, [(side_up1, (1, -1)), (side_down1, (1, 1)), (up2, (0, -2)), (down2, (0, 2))]
    )
    up4, down4 = send(up3[:HALF], UP), send(down3[HALF:], DOWN)
    three = send(jnp.concatenate([up3, down3], 0), ACROSS)
    hidden = units(
        hidden, [(side_up2, (1, -2)), (side_down2, (1, 2)), (up3, (0, -3)), (down3, (0, 3))]
    )
    four = jnp.concatenate([up4, down4], 0)
    other_four = send(four, ACROSS)
    hidden = units(
        hidden, [(three[:ROWS], (1, -3)), (three[ROWS:], (1, 3)), (four, (0, 4)), (other_four, (1, 4))]
    )
    return (normed, hidden)


def solution(mesh):
    in_specs = (
        P("dp", "tensor"),
        P(("dp", "tensor"), None),
        P("tensor", None),
        P(),
        P(),
        P(),
        P(None, "tensor"),
        P(None, "tensor"),
    )
    out_specs = (P(("dp", "tensor"), None), P("dp", "tensor"))
    return jax.shard_map(shards, mesh=mesh, in_specs=in_specs, out_specs=out_specs, check_vma=False)
```

time: 192 us -> 129 us (0.67)
  waiting for transfers between devices: 157 us -> 47.4 us
  starting transfers between devices: 0.08 us -> 51.8 us
  between operations: 14.1 us -> 1.25 us
  matrix products: 15.2 us -> 24.2 us
  other arithmetic: 4.16 us -> 1.03 us
    reduce_scatter x1 -> x0, waiting for transfers between devices: 83.6 us -> none  [shards(): lax.psum_scatter(jnp.dot(context, out_weight, preferred_element_type=jnp....]
    all_gather x1 -> x0, waiting for transfers between devices: 73.2 us -> none  [shards(): lax.all_gather(normed, 'tensor', axis=0, tiled=True)]
    ppermute x0 -> x30, starting transfers between devices: none -> 51.8 us  [send(): return lax.ppermute(value, 'tensor', pairs)]
    ppermute x0 -> x30, waiting for transfers between devices: none -> 47.4 us  [send(): return lax.ppermute(value, 'tensor', pairs)]
    dot_general x3 -> x23, matrix products: 15.2 us -> 24.2 us  [the longest x15 16.3 us: partial(): return jnp.dot(rows, out_weight, preferred_element_type=jnp.float32)]
  transfers between devices with their start and end apart: 2 -> 30, of which waited for: 2 -> 18; matrix products, arithmetic and copies ran while one was open for 0% -> 12% of each run, Pallas kernels for 0% -> 0%
where the time goes in v1:
time: 129 us
  starting transfers between devices  51.8 us (40%)
  waiting for transfers between devices  47.4 us (37%)
  matrix products  24.2 us (19%)
  local copies, waits for them, and re-layouts  2.85 us (2%)
    ppermute x30, starting transfers between devices, send(): return lax.ppermute(value, 'tensor', pairs)  51.8 us
    ppermute x30, waiting for transfers between devices, send(): return lax.ppermute(value, 'tensor', pairs)  47.4 us
    dot_general x15, matrix products, partial(): return jnp.dot(rows, out_weight, preferred_element_type=jnp.float32)  16.3 us
    dot_general x4, matrix products, units(): up = jnp.dot(rows, up_weight, preferred_element_type=jnp.float32)  4.86 us
    dot_general x4, matrix products, units(): gate = jnp.dot(rows, gate_weight, preferred_element_type=jnp.float32)  3.05 us
  transfers between devices with their start and end apart: 30, of which 18 were waited for; matrix products, arithmetic and copies ran while one was open for 12% of the time, Pallas kernels for 0%

profile of v1, /device:TPU:6, one launch (start us, length us, event | category | flops | bytes accessed | tf_op | source)
XLA Modules:
  0.0 128.5 jit_solution(8776104468231729486)
XLA Ops:
  7.9 5.9 %collective-permute-start.2 = (bf16[32,4096]{1,0:T(8,128)(2,1)}, bf16[32,4096]{1,0:T(8,128)(2,1)}, u32[]{:S(2)}, u32[]{:S(2)}) collective-permute-start(bf16[32,4096]{1,0:T(8,128)(2,1)} %convolution_convert_fusion.2), channel_id=1, source_target_pairs={{0,7},{1,0},{2,1},{3,2},{4,3},{5,4},{6,5},{7,6},{8,15},{9,8},{10,9... | collective-permute-start | bytes 786440 | tf_op jit(solution)/shard_map/ppermute | solution.py:24
  18.9 4.2 %collective-permute-done.6 = bf16[32,4096]{1,0:T(8,128)(2,1)} collective-permute-done((bf16[32,4096]{1,0:T(8,128)(2,1)}, bf16[32,4096]{1,0:T(8,128)(2,1)}, u32[]{:S(2)}, u32[]{:S(2)}) %collective-permute-start.6) | collective-permute-done | bytes 262176 | tf_op jit(solution)/shard_map/ppermute | solution.py:24
  24.6 5.9 %collective-permute-start.11 = (bf16[16,4096]{1,0:T(8,128)(2,1)S(1)}, bf16[16,4096]{1,0:T(8,128)(2,1)S(1)}, u32[]{:S(2)}, u32[]{:S(2)}) collective-permute-start(bf16[16,4096]{1,0:T(8,128)(2,1)S(1)} %get-tuple-element.5), channel_id=1, source_target_pairs={{0,7},{1,0},{2,1},{3,2},{4,3},{5,4},{6,5},{7,6},{8,15},{9,8},{10,9... | collective-permute-start | bytes 393224 | tf_op jit(solution)/shard_map/ppermute | solution.py:24
  31.9 3.3 %collective-permute-start.3 = (bf16[32,4096]{1,0:T(8,128)(2,1)S(1)}, bf16[32,4096]{1,0:T(8,128)(2,1)S(1)}, u32[]{:S(2)}, u32[]{:S(2)}) collective-permute-start(bf16[32,4096]{1,0:T(8,128)(2,1)S(1)} %add_convert_fusion.9), channel_id=1, source_target_pairs={{0,7},{1,0},{2,1},{3,2},{4,3},{5,4},{6,5},{7,6},{8,15},{9,8},{10,9... | collective-permute-start | bytes 786440 | tf_op jit(solution)/shard_map/ppermute | solution.py:24
  38.3 3.3 %collective-permute-start.12 = (bf16[32,4096]{1,0:T(8,128)(2,1)S(1)}, bf16[32,4096]{1,0:T(8,128)(2,1)S(1)}, u32[]{:S(2)}, u32[]{:S(2)}) collective-permute-start(bf16[32,4096]{1,0:T(8,128)(2,1)S(1)} %add_convert_fusion.3), channel_id=1, source_target_pairs={{0,7},{1,0},{2,1},{3,2},{4,3},{5,4},{6,5},{7,6},{8,15},{9,8},{10,9... | collective-permute-start | bytes 786440 | tf_op jit(solution)/shard_map/ppermute | solution.py:24
  46.1 3.1 %collective-permute-start.13 = (bf16[32,4096]{1,0:T(8,128)(2,1)S(1)}, bf16[32,4096]{1,0:T(8,128)(2,1)S(1)}, u32[]{:S(2)}, u32[]{:S(2)}) collective-permute-start(bf16[32,4096]{1,0:T(8,128)(2,1)S(1)} %add_convert_fusion.2), channel_id=1, source_target_pairs={{0,7},{1,0},{2,1},{3,2},{4,3},{5,4},{6,5},{7,6},{8,15},{9,8},{10,9... | collective-permute-start | bytes 786440 | tf_op jit(solution)/shard_map/ppermute | solution.py:24
  51.0 2.6 %collective-permute-done.13 = bf16[32,4096]{1,0:T(8,128)(2,1)S(1)} collective-permute-done((bf16[32,4096]{1,0:T(8,128)(2,1)S(1)}, bf16[32,4096]{1,0:T(8,128)(2,1)S(1)}, u32[]{:S(2)}, u32[]{:S(2)}) %collective-permute-start.13) | collective-permute-done | bytes 262176 | tf_op jit(solution)/shard_map/ppermute | solution.py:24
  53.6 3.8 %collective-permute-start.14 = (bf16[32,4096]{1,0:T(8,128)(2,1)S(1)}, bf16[32,4096]{1,0:T(8,128)(2,1)S(1)}, u32[]{:S(2)}, u32[]{:S(2)}) collective-permute-start(bf16[32,4096]{1,0:T(8,128)(2,1)S(1)} %add_convert_fusion.1), channel_id=1, source_target_pairs={{0,7},{1,0},{2,1},{3,2},{4,3},{5,4},{6,5},{7,6},{8,15},{9,8},{10,9... | collective-permute-start | bytes 786440 | tf_op jit(solution)/shard_map/ppermute | solution.py:24
  57.4 1.8 %collective-permute-done.9 = bf16[32,4096]{1,0:T(8,128)(2,1)S(1)} collective-permute-done((bf16[32,4096]{1,0:T(8,128)(2,1)S(1)}, bf16[32,4096]{1,0:T(8,128)(2,1)S(1)}, u32[]{:S(2)}, u32[]{:S(2)}) %collective-permute-start.9) | collective-permute-done | bytes 262176 | tf_op jit(solution)/shard_map/ppermute | solution.py:24
  61.3 6.7 %collective-permute-done.10 = bf16[32,4096]{1,0:T(8,128)(2,1)S(1)} collective-permute-done((bf16[32,4096]{1,0:T(8,128)(2,1)S(1)}, bf16[32,4096]{1,0:T(8,128)(2,1)S(1)}, u32[]{:S(2)}, u32[]{:S(2)}) %collective-permute-start.10) | collective-permute-done | bytes 262176 | tf_op jit(solution)/shard_map/ppermute | solution.py:24
  68.8 2.0 %collective-permute-start.16 = (bf16[32,4096]{1,0:T(8,128)(2,1)S(1)}, bf16[32,4096]{1,0:T(8,128)(2,1)S(1)}, u32[]{:S(2)}, u32[]{:S(2)}) collective-permute-start(bf16[32,4096]{1,0:T(8,128)(2,1)S(1)} %add_convert_fusion), channel_id=1, source_target_pairs={{0,1},{1,2},{2,3},{3,4},{4,5},{5,6},{6,7},{7,0},{8,9},{9,10},{10,1... | collective-permute-start | bytes 786440 | tf_op jit(solution)/shard_map/ppermute | solution.py:24
  72.4 3.5 %collective-permute-done.17 = bf16[32,4096]{1,0:T(8,128)(2,1)S(1)} collective-permute-done((bf16[32,4096]{1,0:T(8,128)(2,1)S(1)}, bf16[32,4096]{1,0:T(8,128)(2,1)S(1)}, u32[]{:S(2)}, u32[]{:S(2)}) %collective-permute-start.17) | collective-permute-done | bytes 262176 | tf_op jit(solution)/shard_map/ppermute | solution.py:24
  79.5 2.5 %collective-permute-start.18 = (bf16[32,4096]{1,0:T(8,128)(2,1)S(1)}, bf16[32,4096]{1,0:T(8,128)(2,1)S(1)}, u32[]{:S(2)}, u32[]{:S(2)}) collective-permute-start(bf16[32,4096]{1,0:T(8,128)(2,1)S(1)} %collective-permute-done.15), channel_id=1, source_target_pairs={{0,1},{1,2},{2,3},{3,4},{4,5},{5,6},{6,7},{7,0},{8,9},{9,10},{10,1... | collective-permute-start | bytes 786440 | tf_op jit(solution)/shard_map/ppermute | solution.py:24
  84.0 2.0 %collective-permute-start.21 = (bf16[32,4096]{1,0:T(8,128)(2,1)S(1)}, bf16[32,4096]{1,0:T(8,128)(2,1)S(1)}, u32[]{:S(2)}, u32[]{:S(2)}) collective-permute-start(bf16[32,4096]{1,0:T(8,128)(2,1)S(1)} %collective-permute-done.17), channel_id=1, source_target_pairs={{0,7},{1,0},{2,1},{3,2},{4,3},{5,4},{6,5},{7,6},{8,15},{9,8},{10,9... | collective-permute-start | bytes 786440 | tf_op jit(solution)/shard_map/ppermute | solution.py:24
  87.2 2.3 %collective-permute-done.19 = bf16[32,4096]{1,0:T(8,128)(2,1)S(1)} collective-permute-done((bf16[32,4096]{1,0:T(8,128)(2,1)S(1)}, bf16[32,4096]{1,0:T(8,128)(2,1)S(1)}, u32[]{:S(2)}, u32[]{:S(2)}) %collective-permute-start.19) | collective-permute-done | bytes 262176 | tf_op jit(solution)/shard_map/ppermute | solution.py:24
  89.5 3.4 %collective-permute-done.20 = bf16[32,4096]{1,0:T(8,128)(2,1)S(1)} collective-permute-done((bf16[32,4096]{1,0:T(8,128)(2,1)S(1)}, bf16[32,4096]{1,0:T(8,128)(2,1)S(1)}, u32[]{:S(2)}, u32[]{:S(2)}) %collective-permute-start.20) | collective-permute-done | bytes 262176 | tf_op jit(solution)/shard_map/ppermute | solution.py:24
  92.9 2.2 %collective-permute-done.21 = bf16[32,4096]{1,0:T(8,128)(2,1)S(1)} collective-permute-done((bf16[32,4096]{1,0:T(8,128)(2,1)S(1)}, bf16[32,4096]{1,0:T(8,128)(2,1)S(1)}, u32[]{:S(2)}, u32[]{:S(2)}) %collective-permute-start.21) | collective-permute-done | bytes 262176 | tf_op jit(solution)/shard_map/ppermute | solution.py:24
  97.3 3.2 %collective-permute-start.23 = (bf16[32,4096]{1,0:T(8,128)(2,1)S(1)}, bf16[32,4096]{1,0:T(8,128)(2,1)S(1)}, u32[]{:S(2)}, u32[]{:S(2)}) collective-permute-start(bf16[32,4096]{1,0:T(8,128)(2,1)S(1)} %collective-permute-done.19), channel_id=1, source_target_pairs={{0,7},{1,0},{2,1},{3,2},{4,3},{5,4},{6,5},{7,6},{8,15},{9,8},{10,9... | collective-permute-start | bytes 786440 | tf_op jit(solution)/shard_map/ppermute | solution.py:24
  100.5 3.2 %collective-permute-start.25 = (bf16[32,4096]{1,0:T(8,128)(2,1)S(1)}, bf16[32,4096]{1,0:T(8,128)(2,1)S(1)}, u32[]{:S(2)}, u32[]{:S(2)}) collective-permute-start(bf16[32,4096]{1,0:T(8,128)(2,1)S(1)} %collective-permute-done.21), channel_id=1, source_target_pairs={{0,7},{1,0},{2,1},{3,2},{4,3},{5,4},{6,5},{7,6},{8,15},{9,8},{10,9... | collective-permute-start | bytes 786440 | tf_op jit(solution)/shard_map/ppermute | solution.py:24
  103.7 1.9 %collective-permute-done.22 = bf16[32,4096]{1,0:T(8,128)(2,1)S(1)} collective-permute-done((bf16[32,4096]{1,0:T(8,128)(2,1)S(1)}, bf16[32,4096]{1,0:T(8,128)(2,1)S(1)}, u32[]{:S(2)}, u32[]{:S(2)}) %collective-permute-start.22) | collective-permute-done | bytes 262176 | tf_op jit(solution)/shard_map/ppermute | solution.py:24
  105.7 3.4 %collective-permute-done.24 = bf16[32,4096]{1,0:T(8,128)(2,1)S(1)} collective-permute-done((bf16[32,4096]{1,0:T(8,128)(2,1)S(1)}, bf16[32,4096]{1,0:T(8,128)(2,1)S(1)}, u32[]{:S(2)}, u32[]{:S(2)}) %collective-permute-start.24) | collective-permute-done | bytes 262176 | tf_op jit(solution)/shard_map/ppermute | solution.py:24
  113.0 3.3 %collective-permute-start.28 = (bf16[16,4096]{1,0:T(8,128)(2,1)S(1)}, bf16[16,4096]{1,0:T(8,128)(2,1)S(1)}, u32[]{:S(2)}, u32[]{:S(2)}) collective-permute-start(bf16[16,4096]{1,0:T(8,128)(2,1)S(1)} %slice.108), channel_id=1, source_target_pairs={{0,7},{1,0},{2,1},{3,2},{4,3},{5,4},{6,5},{7,6},{8,15},{9,8},{10,9... | collective-permute-start | bytes 393224 | tf_op jit(solution)/shard_map/ppermute | solution.py:24
  116.3 2.8 %collective-permute-done.27 = bf16[16,4096]{1,0:T(8,128)(2,1)S(1)} collective-permute-done((bf16[16,4096]{1,0:T(8,128)(2,1)S(1)}, bf16[16,4096]{1,0:T(8,128)(2,1)S(1)}, u32[]{:S(2)}, u32[]{:S(2)}) %collective-permute-start.27) | collective-permute-done | bytes 131104 | tf_op jit(solution)/shard_map/ppermute | solution.py:24
  120.6 5.0 %collective-permute-done.29 = bf16[32,4096]{1,0:T(8,128)(2,1)S(1)} collective-permute-done((bf16[32,4096]{1,0:T(8,128)(2,1)S(1)}, bf16[32,4096]{1,0:T(8,128)(2,1)S(1)}, u32[]{:S(2)}, u32[]{:S(2)}) %collective-permute-start.29) | collective-permute-done | bytes 262176 | tf_op jit(solution)/shard_map/ppermute | solution.py:24
  (128 shorter events, 45.8 us)
Async XLA Ops:
  3.5 33.3 %collective-permute-start.5 = (bf16[64,4096]{1,0:T(8,128)(2,1)}, bf16[64,4096]{1,0:T(8,128)(2,1)}, u32[]{:S(2)}, u32[]{:S(2)}) collective-permute-start(bf16[64,4096]{1,0:T(8,128)(2,1)} %convolution_convert_fusion), channel_id=1, source_target_pairs={{0,8},{1,9},{2,10},{3,11},{4,12},{5,13},{6,14},{7,15},{8,0},{9,1},... | collective-permute-start | bytes 1572872 | tf_op jit(solution)/shard_map/ppermute | solution.py:24
  6.3 16.8 %collective-permute-start.6 = (bf16[32,4096]{1,0:T(8,128)(2,1)}, bf16[32,4096]{1,0:T(8,128)(2,1)}, u32[]{:S(2)}, u32[]{:S(2)}) collective-permute-start(bf16[32,4096]{1,0:T(8,128)(2,1)} %convolution_convert_fusion.1), channel_id=1, source_target_pairs={{0,8},{1,9},{2,10},{3,11},{4,12},{5,13},{6,14},{7,15},{8,0},{9,1},... | collective-permute-start | bytes 786440 | tf_op jit(solution)/shard_map/ppermute | solution.py:24
  7.9 22.6 %collective-permute-start.2 = (bf16[32,4096]{1,0:T(8,128)(2,1)}, bf16[32,4096]{1,0:T(8,128)(2,1)}, u32[]{:S(2)}, u32[]{:S(2)}) collective-permute-start(bf16[32,4096]{1,0:T(8,128)(2,1)} %convolution_convert_fusion.2), channel_id=1, source_target_pairs={{0,7},{1,0},{2,1},{3,2},{4,3},{5,4},{6,5},{7,6},{8,15},{9,8},{10,9... | collective-permute-start | bytes 786440 | tf_op jit(solution)/shard_map/ppermute | solution.py:24
  15.0 20.3 %collective-permute-start = (bf16[32,4096]{1,0:T(8,128)(2,1)}, bf16[32,4096]{1,0:T(8,128)(2,1)}, u32[]{:S(2)}, u32[]{:S(2)}) collective-permute-start(bf16[32,4096]{1,0:T(8,128)(2,1)} %convolution_convert_fusion.3), channel_id=1, source_target_pairs={{0,1},{1,2},{2,3},{3,4},{4,5},{5,6},{6,7},{7,0},{8,9},{9,10},{10,1... | collective-permute-start | bytes 786440 | tf_op jit(solution)/shard_map/ppermute | solution.py:24
  24.6 12.2 %collective-permute-start.11 = (bf16[16,4096]{1,0:T(8,128)(2,1)S(1)}, bf16[16,4096]{1,0:T(8,128)(2,1)S(1)}, u32[]{:S(2)}, u32[]{:S(2)}) collective-permute-start(bf16[16,4096]{1,0:T(8,128)(2,1)S(1)} %get-tuple-element.5), channel_id=1, source_target_pairs={{0,7},{1,0},{2,1},{3,2},{4,3},{5,4},{6,5},{7,6},{8,15},{9,8},{10,9... | collective-permute-start | bytes 393224 | tf_op jit(solution)/shard_map/ppermute | solution.py:24
  30.5 11.0 %collective-permute-start.7 = (bf16[16,4096]{1,0:T(8,128)(2,1)S(1)}, bf16[16,4096]{1,0:T(8,128)(2,1)S(1)}, u32[]{:S(2)}, u32[]{:S(2)}) collective-permute-start(bf16[16,4096]{1,0:T(8,128)(2,1)S(1)} %get-tuple-element.4), channel_id=1, source_target_pairs={{0,1},{1,2},{2,3},{3,4},{4,5},{5,6},{6,7},{7,0},{8,9},{9,10},{10,1... | collective-permute-start | bytes 393224 | tf_op jit(solution)/shard_map/ppermute | solution.py:24
  31.9 11.3 %collective-permute-start.3 = (bf16[32,4096]{1,0:T(8,128)(2,1)S(1)}, bf16[32,4096]{1,0:T(8,128)(2,1)S(1)}, u32[]{:S(2)}, u32[]{:S(2)}) collective-permute-start(bf16[32,4096]{1,0:T(8,128)(2,1)S(1)} %add_convert_fusion.9), channel_id=1, source_target_pairs={{0,7},{1,0},{2,1},{3,2},{4,3},{5,4},{6,5},{7,6},{8,15},{9,8},{10,9... | collective-permute-start | bytes 786440 | tf_op jit(solution)/shard_map/ppermute | solution.py:24
  36.7 7.7 %collective-permute-start.1 = (bf16[32,4096]{1,0:T(8,128)(2,1)S(1)}, bf16[32,4096]{1,0:T(8,128)(2,1)S(1)}, u32[]{:S(2)}, u32[]{:S(2)}) collective-permute-start(bf16[32,4096]{1,0:T(8,128)(2,1)S(1)} %add_convert_fusion.10), channel_id=1, source_target_pairs={{0,1},{1,2},{2,3},{3,4},{4,5},{5,6},{6,7},{7,0},{8,9},{9,10},{10,1... | collective-permute-start | bytes 786440 | tf_op jit(solution)/shard_map/ppermute | solution.py:24
  38.3 7.8 %collective-permute-start.12 = (bf16[32,4096]{1,0:T(8,128)(2,1)S(1)}, bf16[32,4096]{1,0:T(8,128)(2,1)S(1)}, u32[]{:S(2)}, u32[]{:S(2)}) collective-permute-start(bf16[32,4096]{1,0:T(8,128)(2,1)S(1)} %add_convert_fusion.3), channel_id=1, source_target_pairs={{0,7},{1,0},{2,1},{3,2},{4,3},{5,4},{6,5},{7,6},{8,15},{9,8},{10,9... | collective-permute-start | bytes 786440 | tf_op jit(solution)/shard_map/ppermute | solution.py:24
  43.0 7.8 %collective-permute-start.8 = (bf16[32,4096]{1,0:T(8,128)(2,1)S(1)}, bf16[32,4096]{1,0:T(8,128)(2,1)S(1)}, u32[]{:S(2)}, u32[]{:S(2)}) collective-permute-start(bf16[32,4096]{1,0:T(8,128)(2,1)S(1)} %add_convert_fusion.6), channel_id=1, source_target_pairs={{0,1},{1,2},{2,3},{3,4},{4,5},{5,6},{6,7},{7,0},{8,9},{9,10},{10,1... | collective-permute-start | bytes 786440 | tf_op jit(solution)/shard_map/ppermute | solution.py:24
  44.4 15.5 %collective-permute-start.4 = (bf16[32,4096]{1,0:T(8,128)(2,1)S(1)}, bf16[32,4096]{1,0:T(8,128)(2,1)S(1)}, u32[]{:S(2)}, u32[]{:S(2)}) collective-permute-start(bf16[32,4096]{1,0:T(8,128)(2,1)S(1)} %add_convert_fusion.8), channel_id=1, source_target_pairs={{0,8},{1,9},{2,10},{3,11},{4,12},{5,13},{6,14},{7,15},{8,0},{9,1},... | collective-permute-start | bytes 786440 | tf_op jit(solution)/shard_map/ppermute | solution.py:24
  50.9 8.4 %collective-permute-start.9 = (bf16[32,4096]{1,0:T(8,128)(2,1)S(1)}, bf16[32,4096]{1,0:T(8,128)(2,1)S(1)}, u32[]{:S(2)}, u32[]{:S(2)}) collective-permute-start(bf16[32,4096]{1,0:T(8,128)(2,1)S(1)} %add_convert_fusion.5), channel_id=1, source_target_pairs={{0,1},{1,2},{2,3},{3,4},{4,5},{5,6},{6,7},{7,0},{8,9},{9,10},{10,1... | collective-permute-start | bytes 786440 | tf_op jit(solution)/shard_map/ppermute | solution.py:24
  53.6 7.7 %collective-permute-start.14 = (bf16[32,4096]{1,0:T(8,128)(2,1)S(1)}, bf16[32,4096]{1,0:T(8,128)(2,1)S(1)}, u32[]{:S(2)}, u32[]{:S(2)}) collective-permute-start(bf16[32,4096]{1,0:T(8,128)(2,1)S(1)} %add_convert_fusion.1), channel_id=1, source_target_pairs={{0,7},{1,0},{2,1},{3,2},{4,3},{5,4},{6,5},{7,6},{8,15},{9,8},{10,9... | collective-permute-start | bytes 786440 | tf_op jit(solution)/shard_map/ppermute | solution.py:24
  59.3 8.7 %collective-permute-start.10 = (bf16[32,4096]{1,0:T(8,128)(2,1)S(1)}, bf16[32,4096]{1,0:T(8,128)(2,1)S(1)}, u32[]{:S(2)}, u32[]{:S(2)}) collective-permute-start(bf16[32,4096]{1,0:T(8,128)(2,1)S(1)} %add_convert_fusion.4), channel_id=1, source_target_pairs={{0,1},{1,2},{2,3},{3,4},{4,5},{5,6},{6,7},{7,0},{8,9},{9,10},{10,1... | collective-permute-start | bytes 786440 | tf_op jit(solution)/shard_map/ppermute | solution.py:24
  68.8 8.6 %collective-permute-start.16 = (bf16[32,4096]{1,0:T(8,128)(2,1)S(1)}, bf16[32,4096]{1,0:T(8,128)(2,1)S(1)}, u32[]{:S(2)}, u32[]{:S(2)}) collective-permute-start(bf16[32,4096]{1,0:T(8,128)(2,1)S(1)} %add_convert_fusion), channel_id=1, source_target_pairs={{0,1},{1,2},{2,3},{3,4},{4,5},{5,6},{6,7},{7,0},{8,9},{9,10},{10,1... | collective-permute-start | bytes 786440 | tf_op jit(solution)/shard_map/ppermute | solution.py:24
  79.5 7.7 %collective-permute-start.18 = (bf16[32,4096]{1,0:T(8,128)(2,1)S(1)}, bf16[32,4096]{1,0:T(8,128)(2,1)S(1)}, u32[]{:S(2)}, u32[]{:S(2)}) collective-permute-start(bf16[32,4096]{1,0:T(8,128)(2,1)S(1)} %collective-permute-done.15), channel_id=1, source_target_pairs={{0,1},{1,2},{2,3},{3,4},{4,5},{5,6},{6,7},{7,0},{8,9},{9,10},{10,1... | collective-permute-start | bytes 786440 | tf_op jit(solution)/shard_map/ppermute | solution.py:24
  82.0 7.5 %collective-permute-start.19 = (bf16[32,4096]{1,0:T(8,128)(2,1)S(1)}, bf16[32,4096]{1,0:T(8,128)(2,1)S(1)}, u32[]{:S(2)}, u32[]{:S(2)}) collective-permute-start(bf16[32,4096]{1,0:T(8,128)(2,1)S(1)} %collective-permute-done.15), channel_id=1, source_target_pairs={{0,7},{1,0},{2,1},{3,2},{4,3},{5,4},{6,5},{7,6},{8,15},{9,8},{10,9... | collective-permute-start | bytes 786440 | tf_op jit(solution)/shard_map/ppermute | solution.py:24
  82.8 10.1 %collective-permute-start.20 = (bf16[32,4096]{1,0:T(8,128)(2,1)S(1)}, bf16[32,4096]{1,0:T(8,128)(2,1)S(1)}, u32[]{:S(2)}, u32[]{:S(2)}) collective-permute-start(bf16[32,4096]{1,0:T(8,128)(2,1)S(1)} %collective-permute-done.16), channel_id=1, source_target_pairs={{0,1},{1,2},{2,3},{3,4},{4,5},{5,6},{6,7},{7,0},{8,9},{9,10},{10,1... | collective-permute-start | bytes 786440 | tf_op jit(solution)/shard_map/ppermute | solution.py:24
  84.0 11.1 %collective-permute-start.21 = (bf16[32,4096]{1,0:T(8,128)(2,1)S(1)}, bf16[32,4096]{1,0:T(8,128)(2,1)S(1)}, u32[]{:S(2)}, u32[]{:S(2)}) collective-permute-start(bf16[32,4096]{1,0:T(8,128)(2,1)S(1)} %collective-permute-done.17), channel_id=1, source_target_pairs={{0,7},{1,0},{2,1},{3,2},{4,3},{5,4},{6,5},{7,6},{8,15},{9,8},{10,9... | collective-permute-start | bytes 786440 | tf_op jit(solution)/shard_map/ppermute | solution.py:24
  97.2 8.4 %collective-permute-start.22 = (bf16[32,4096]{1,0:T(8,128)(2,1)S(1)}, bf16[32,4096]{1,0:T(8,128)(2,1)S(1)}, u32[]{:S(2)}, u32[]{:S(2)}) collective-permute-start(bf16[32,4096]{1,0:T(8,128)(2,1)S(1)} %collective-permute-done.18), channel_id=1, source_target_pairs={{0,1},{1,2},{2,3},{3,4},{4,5},{5,6},{6,7},{7,0},{8,9},{9,10},{10,1... | collective-permute-start | bytes 786440 | tf_op jit(solution)/shard_map/ppermute | solution.py:24
  97.3 8.3 %collective-permute-start.23 = (bf16[32,4096]{1,0:T(8,128)(2,1)S(1)}, bf16[32,4096]{1,0:T(8,128)(2,1)S(1)}, u32[]{:S(2)}, u32[]{:S(2)}) collective-permute-start(bf16[32,4096]{1,0:T(8,128)(2,1)S(1)} %collective-permute-done.19), channel_id=1, source_target_pairs={{0,7},{1,0},{2,1},{3,2},{4,3},{5,4},{6,5},{7,6},{8,15},{9,8},{10,9... | collective-permute-start | bytes 786440 | tf_op jit(solution)/shard_map/ppermute | solution.py:24
  100.5 8.6 %collective-permute-start.24 = (bf16[32,4096]{1,0:T(8,128)(2,1)S(1)}, bf16[32,4096]{1,0:T(8,128)(2,1)S(1)}, u32[]{:S(2)}, u32[]{:S(2)}) collective-permute-start(bf16[32,4096]{1,0:T(8,128)(2,1)S(1)} %collective-permute-done.20), channel_id=1, source_target_pairs={{0,1},{1,2},{2,3},{3,4},{4,5},{5,6},{6,7},{7,0},{8,9},{9,10},{10,1... | collective-permute-start | bytes 786440 | tf_op jit(solution)/shard_map/ppermute | solution.py:24
  100.5 8.6 %collective-permute-start.25 = (bf16[32,4096]{1,0:T(8,128)(2,1)S(1)}, bf16[32,4096]{1,0:T(8,128)(2,1)S(1)}, u32[]{:S(2)}, u32[]{:S(2)}) collective-permute-start(bf16[32,4096]{1,0:T(8,128)(2,1)S(1)} %collective-permute-done.21), channel_id=1, source_target_pairs={{0,7},{1,0},{2,1},{3,2},{4,3},{5,4},{6,5},{7,6},{8,15},{9,8},{10,9... | collective-permute-start | bytes 786440 | tf_op jit(solution)/shard_map/ppermute | solution.py:24
  111.2 9.3 %collective-permute-start.26 = (bf16[64,4096]{1,0:T(8,128)(2,1)S(1)}, bf16[64,4096]{1,0:T(8,128)(2,1)S(1)}, u32[]{:S(2)}, u32[]{:S(2)}) collective-permute-start(bf16[64,4096]{1,0:T(8,128)(2,1)S(1)} %pad_maximum_fusion.1), channel_id=1, source_target_pairs={{0,8},{1,9},{2,10},{3,11},{4,12},{5,13},{6,14},{7,15},{8,0},{9,1},... | collective-permute-start | bytes 1572872 | tf_op jit(solution)/shard_map/ppermute | solution.py:24
  (18 other events, 151.7 us)

commit v2 on v1

v2 whole, which is shorter than its diff:
```python
import jax
import jax.numpy as jnp
from jax import lax
from jax.sharding import PartitionSpec as P

ROWS = 32
RING = 8
HALF = ROWS // 2


def index_of(y, z):
    return (y % 2) * RING + z % RING


def ring_pairs(step):
    return [(index_of(y, z), index_of(y, z + step)) for y in range(2) for z in range(RING)]


UP, DOWN = ring_pairs(1), ring_pairs(-1)
ACROSS = [(index_of(y, z), index_of(y + 1, z)) for y in range(2) for z in range(RING)]


def send(value, pairs):
    return lax.ppermute(value, "tensor", pairs)


def hold(values):
    return lax.optimization_barrier(values)


def shards(
    context, residual_in, out_weight, out_bias, norm_gain, norm_bias, gate_weight, up_weight
):
    me = lax.axis_index("tensor")
    y, z = me // RING, me % RING

    def start_of(other, dz):
        return (jnp.bitwise_xor(y, other) * RING + lax.rem(z + dz + RING, RING)) * ROWS

    def bf(value):
        return value.astype(jnp.bfloat16)

    def f32(value):
        return value.astype(jnp.float32)

    ring = context.reshape(2, RING, ROWS, -1)
    ring = lax.dynamic_slice_in_dim(jnp.concatenate([ring, ring], 1), z, RING, 1)
    ring = jnp.where(y == 0, ring, ring[::-1])

    def product(*blocks):
        rows = [ring[other, dz % RING] for other, dz in blocks]
        rows = jnp.concatenate(rows, 0) if len(rows) > 1 else rows[0]
        return bf(jnp.dot(rows, out_weight, preferred_element_type=jnp.float32))

    far = product((1, 4))
    far, ring = hold((far, ring))
    far = send(far, ACROSS)
    rest = product((1, 1), (1, -1), (1, 3), (1, -3), (1, 2), (1, -2))
    side_up = send(rest[:ROWS], UP)
    side_down = send(rest[ROWS : 2 * ROWS], DOWN)
    three = send(rest[2 * ROWS : 4 * ROWS], ACROSS)
    two = send(rest[4 * ROWS :], ACROSS)
    ring, rest = hold((ring, rest))
    own4, own0, side0 = product((0, 4)), product((0, 0)), product((1, 0))
    own3, own2, own1 = (product((0, dz), (0, -dz)) for dz in (3, 2, 1))

    far, own4, own3, own2, own1, own0, side0 = hold((far, own4, own3, own2, own1, own0, side0))
    total = bf(f32(own4) + f32(far))
    up, down = send(total[:HALF], UP), send(total[HALF:], DOWN)

    up, down, three, side_up, side_down, own3, side0 = hold(
        (up, down, three, side_up, side_down, own3, side0)
    )
    pad = jnp.zeros((HALF, up.shape[1]), jnp.bfloat16)
    own3 = f32(own3) + f32(three)
    up = send(bf(own3[:ROWS] + f32(jnp.concatenate([up, pad], 0))), UP)
    down = send(bf(own3[ROWS:] + f32(jnp.concatenate([pad, down], 0))), DOWN)
    side = send(bf(f32(side0) + f32(side_up) + f32(side_down)), ACROSS)

    up, down, two, own2 = hold((up, down, two, own2))
    own2 = f32(own2) + f32(two)
    up = send(bf(own2[:ROWS] + f32(up)), UP)
    down = send(bf(own2[ROWS:] + f32(down)), DOWN)

    up, down, own1 = hold((up, down, own1))
    up = send(bf(f32(own1[:ROWS]) + f32(up)), UP)
    down = send(bf(f32(own1[ROWS:]) + f32(down)), DOWN)

    attended = f32(own0) + f32(side) + f32(up) + f32(down)

    stream = f32(residual_in) + attended + out_bias
    center = jnp.mean(stream, axis=1, keepdims=True)
    spread = jnp.mean((stream - center) ** 2, axis=1, keepdims=True)
    normed = bf((stream - center) / jnp.sqrt(spread + 1e-05) * norm_gain + norm_bias)

    hidden = jnp.zeros((context.shape[0], gate_weight.shape[1]), jnp.bfloat16)

    def units(hidden, blocks):
        rows = jnp.concatenate([rows for rows, _ in blocks], 0)
        gate = jnp.dot(rows, gate_weight, preferred_element_type=jnp.float32)
        up = jnp.dot(rows, up_weight, preferred_element_type=jnp.float32)
        out = bf(jax.nn.gelu(gate, approximate=False) * up)
        for i, (_, block) in enumerate(blocks):
            hidden = lax.dynamic_update_slice_in_dim(
                hidden, out[i * ROWS : (i + 1) * ROWS], start_of(*block), 0
            )
        return hidden

    up1, down1 = send(normed, UP), send(normed, DOWN)
    other = send(normed, ACROSS)
    up1, down1, other, normed = hold((up1, down1, other, normed))

    up2, down2 = send(up1, UP), send(down1, DOWN)
    side_up1, side_down1 = send(other, UP), send(other, DOWN)
    up2, down2, up1, down1, other, normed = hold((up2, down2, up1, down1, other, normed))

    up3, down3 = send(up2, UP), send(down2, DOWN)
    two = send(jnp.concatenate([up2, down2], 0), ACROSS)
    hidden = units(
        hidden, [(normed, (0, 0)), (other, (1, 0)), (up1, (0, -1)), (down1, (0, 1))]
    )
    up3, down3, side_up1, side_down1, up2, down2, hidden, normed = hold(
        (up3, down3, side_up1, side_down1, up2, down2, hidden, normed)
    )

    up4, down4 = send(up3[:HALF], UP), send(down3[HALF:], DOWN)
    three = send(jnp.concatenate([up3, down3], 0), ACROSS)
    hidden = units(
        hidden, [(side_up1, (1, -1)), (side_down1, (1, 1)), (up2, (0, -2)), (down2, (0, 2))]
    )
    up4, down4, up3, down3, hidden = hold((up4, down4, up3, down3, hidden))

    four = jnp.concatenate([up4, down4], 0)
    other_four = send(four, ACROSS)
    two, up3, down3, hidden = hold((two, up3, down3, hidden))
    hidden = units(
        hidden, [(two[:ROWS], (1, -2)), (two[ROWS:], (1, 2)), (up3, (0, -3)), (down3, (0, 3))]
    )
    hidden = units(
        hidden, [(three[:ROWS], (1, -3)), (three[ROWS:], (1, 3)), (four, (0, 4)), (other_four, (1, 4))]
    )
    return (normed, hidden)


def solution(mesh):
    in_specs = (
        P("dp", "tensor"),
        P(("dp", "tensor"), None),
        P("tensor", None),
        P(),
        P(),
        P(),
        P(None, "tensor"),
        P(None, "tensor"),
    )
    out_specs = (P(("dp", "tensor"), None), P("dp", "tensor"))
    return jax.shard_map(shards, mesh=mesh, in_specs=in_specs, out_specs=out_specs, check_vma=False)
```

time: 129 us -> 107 us (0.83)
  waiting for transfers between devices: 47.4 us -> 33.3 us
  matrix products: 24.2 us -> 13.9 us
  local copies, waits for them, and re-layouts: 2.85 us -> 4.97 us
  other arithmetic: 1.03 us -> 2.72 us
    ppermute x30 -> x28, waiting for transfers between devices: 47.4 us -> 33.3 us  [send(): return lax.ppermute(value, 'tensor', pairs)]
    dot_general x15 -> x8, matrix products: 16.3 us -> 3.92 us  [product(): return bf(jnp.dot(rows, out_weight, preferred_element_type=jnp.float32))]
    dot_general x4, matrix products: 3.05 us -> 5.25 us  [units(): gate = jnp.dot(rows, gate_weight, preferred_element_type=jnp.float32)]
    unnamed x33 -> x34, local copies, waits for them, and re-layouts: 1.68 us -> 3.58 us
    ppermute x30 -> x28, starting transfers between devices: 51.8 us -> 50.8 us  [send(): return lax.ppermute(value, 'tensor', pairs)]
  transfers between devices with their start and end apart: 30 -> 28, of which waited for: 18 -> 14; matrix products, arithmetic and copies ran while one was open for 12% -> 13% of each run, Pallas kernels for 0% -> 0%
where the time goes in v2:
time: 107 us
  starting transfers between devices  50.8 us (47%)
  waiting for transfers between devices  33.3 us (31%)
  matrix products  13.9 us (13%)
  local copies, waits for them, and re-layouts  4.97 us (5%)
  other arithmetic  2.72 us (3%)
  between operations  1.29 us (1%)
    ppermute x28, starting transfers between devices, send(): return lax.ppermute(value, 'tensor', pairs)  50.8 us
    ppermute x28, waiting for transfers between devices, send(): return lax.ppermute(value, 'tensor', pairs)  33.3 us
    dot_general x4, matrix products, units(): gate = jnp.dot(rows, gate_weight, preferred_element_type=jnp.float32)  5.25 us
    dot_general x4, matrix products, units(): up = jnp.dot(rows, up_weight, preferred_element_type=jnp.float32)  4.68 us
    dot_general x8, matrix products, product(): return bf(jnp.dot(rows, out_weight, preferred_element_type=jnp.float32))  3.92 us
    unnamed x34, local copies, waits for them, and re-layouts  3.58 us
  transfers between devices with their start and end apart: 28, of which 14 were waited for; matrix products, arithmetic and copies ran while one was open for 13% of the time, Pallas kernels for 0%

profile of v2, /device:TPU:6, one launch (start us, length us, event | category | flops | bytes accessed | tf_op | source)
XLA Modules:
  0.0 106.9 jit_solution(6279512840547191584)
XLA Ops:
  5.7 2.0 %collective-permute-start.4 = (bf16[32,4096]{1,0:T(8,128)(2,1)S(1)}, bf16[32,4096]{1,0:T(8,128)(2,1)S(1)}, u32[]{:S(2)}, u32[]{:S(2)}) collective-permute-start(bf16[32,4096]{1,0:T(8,128)(2,1)S(1)} %get-tuple-element.109), channel_id=1, source_target_pairs={{0,1},{1,2},{2,3},{3,4},{4,5},{5,6},{6,7},{7,0},{8,9},{9,10},{10,1... | collective-permute-start | bytes 786440 | tf_op jit(solution)/shard_map/ppermute | solution.py:24
  7.8 4.0 %collective-permute-start.5 = (bf16[32,4096]{1,0:T(8,128)(2,1)S(1)}, bf16[32,4096]{1,0:T(8,128)(2,1)S(1)}, u32[]{:S(2)}, u32[]{:S(2)}) collective-permute-start(bf16[32,4096]{1,0:T(8,128)(2,1)S(1)} %get-tuple-element.108), channel_id=1, source_target_pairs={{0,7},{1,0},{2,1},{3,2},{4,3},{5,4},{6,5},{7,6},{8,15},{9,8},{10,9... | collective-permute-start | bytes 786440 | tf_op jit(solution)/shard_map/ppermute | solution.py:24
  14.9 3.3 %collective-permute-start.2 = (bf16[16,4096]{1,0:T(8,128)(2,1)S(1)}, bf16[16,4096]{1,0:T(8,128)(2,1)S(1)}, u32[]{:S(2)}, u32[]{:S(2)}) collective-permute-start(bf16[16,4096]{1,0:T(8,128)(2,1)S(1)} %get-tuple-element.116), channel_id=1, source_target_pairs={{0,7},{1,0},{2,1},{3,2},{4,3},{5,4},{6,5},{7,6},{8,15},{9,8},{10,9... | collective-permute-start | bytes 393224 | tf_op jit(solution)/shard_map/ppermute | solution.py:24
  21.1 2.2 %collective-permute-done.3 = bf16[64,4096]{1,0:T(8,128)(2,1)S(1)} collective-permute-done((bf16[64,4096]{1,0:T(8,128)(2,1)S(1)}, bf16[64,4096]{1,0:T(8,128)(2,1)S(1)}, u32[]{:S(2)}, u32[]{:S(2)}) %collective-permute-start.3) | collective-permute-done | bytes 524320 | tf_op jit(solution)/shard_map/ppermute | solution.py:24
  23.5 2.0 %collective-permute-start.7 = (bf16[32,4096]{1,0:T(8,128)(2,1)S(1)}, bf16[32,4096]{1,0:T(8,128)(2,1)S(1)}, u32[]{:S(2)}, u32[]{:S(2)}) collective-permute-start(bf16[32,4096]{1,0:T(8,128)(2,1)S(1)} %get-tuple-element.113), channel_id=1, source_target_pairs={{0,1},{1,2},{2,3},{3,4},{4,5},{5,6},{6,7},{7,0},{8,9},{9,10},{10,1... | collective-permute-start | bytes 786440 | tf_op jit(solution)/shard_map/ppermute | solution.py:24
  25.5 4.0 %collective-permute-start.8 = (bf16[32,4096]{1,0:T(8,128)(2,1)S(1)}, bf16[32,4096]{1,0:T(8,128)(2,1)S(1)}, u32[]{:S(2)}, u32[]{:S(2)}) collective-permute-start(bf16[32,4096]{1,0:T(8,128)(2,1)S(1)} %get-tuple-element.112), channel_id=1, source_target_pairs={{0,7},{1,0},{2,1},{3,2},{4,3},{5,4},{6,5},{7,6},{8,15},{9,8},{10,9... | collective-permute-start | bytes 786440 | tf_op jit(solution)/shard_map/ppermute | solution.py:24
  29.5 3.8 %collective-permute-done.9 = bf16[64,4096]{1,0:T(8,128)(2,1)S(1)} collective-permute-done((bf16[64,4096]{1,0:T(8,128)(2,1)S(1)}, bf16[64,4096]{1,0:T(8,128)(2,1)S(1)}, u32[]{:S(2)}, u32[]{:S(2)}) %collective-permute-start.9) | collective-permute-done | bytes 524320 | tf_op jit(solution)/shard_map/ppermute | solution.py:24
  35.6 4.0 %collective-permute-start.11 = (bf16[32,4096]{1,0:T(8,128)(2,1)S(1)}, bf16[32,4096]{1,0:T(8,128)(2,1)S(1)}, u32[]{:S(2)}, u32[]{:S(2)}) collective-permute-start(bf16[32,4096]{1,0:T(8,128)(2,1)S(1)} %get-tuple-element.110), channel_id=1, source_target_pairs={{0,7},{1,0},{2,1},{3,2},{4,3},{5,4},{6,5},{7,6},{8,15},{9,8},{10,9... | collective-permute-start | bytes 786440 | tf_op jit(solution)/shard_map/ppermute | solution.py:24
  39.8 1.8 %collective-permute-start.6 = (bf16[32,4096]{1,0:T(8,128)(2,1)S(1)}, bf16[32,4096]{1,0:T(8,128)(2,1)S(1)}, u32[]{:S(2)}, u32[]{:S(2)}) collective-permute-start(bf16[32,4096]{1,0:T(8,128)(2,1)S(1)} %add_convert_fusion.3), channel_id=1, source_target_pairs={{0,8},{1,9},{2,10},{3,11},{4,12},{5,13},{6,14},{7,15},{8,0},{9,1},... | collective-permute-start | bytes 786440 | tf_op jit(solution)/shard_map/ppermute | solution.py:24
  41.6 3.4 %collective-permute-done.10 = bf16[32,4096]{1,0:T(8,128)(2,1)S(1)} collective-permute-done((bf16[32,4096]{1,0:T(8,128)(2,1)S(1)}, bf16[32,4096]{1,0:T(8,128)(2,1)S(1)}, u32[]{:S(2)}, u32[]{:S(2)}) %collective-permute-start.10) | collective-permute-done | bytes 262176 | tf_op jit(solution)/shard_map/ppermute | solution.py:24
  45.2 3.2 %collective-permute-start.13 = (bf16[32,4096]{1,0:T(8,128)(2,1)S(1)}, bf16[32,4096]{1,0:T(8,128)(2,1)S(1)}, u32[]{:S(2)}, u32[]{:S(2)}) collective-permute-start(bf16[32,4096]{1,0:T(8,128)(2,1)S(1)} %get-tuple-element.115), channel_id=1, source_target_pairs={{0,7},{1,0},{2,1},{3,2},{4,3},{5,4},{6,5},{7,6},{8,15},{9,8},{10,9... | collective-permute-start | bytes 786440 | tf_op jit(solution)/shard_map/ppermute | solution.py:24
  48.5 4.5 %collective-permute-done.12 = bf16[32,4096]{1,0:T(8,128)(2,1)S(1)} collective-permute-done((bf16[32,4096]{1,0:T(8,128)(2,1)S(1)}, bf16[32,4096]{1,0:T(8,128)(2,1)S(1)}, u32[]{:S(2)}, u32[]{:S(2)}) %collective-permute-start.12) | collective-permute-done | bytes 262176 | tf_op jit(solution)/shard_map/ppermute | solution.py:24
  53.7 2.4 %collective-permute-start.14 = (bf16[32,4096]{1,0:T(8,128)(2,1)S(1)}, bf16[32,4096]{1,0:T(8,128)(2,1)S(1)}, u32[]{:S(2)}, u32[]{:S(2)}) collective-permute-start(bf16[32,4096]{1,0:T(8,128)(2,1)S(1)} %add_convert_fusion), channel_id=1, source_target_pairs={{0,1},{1,2},{2,3},{3,4},{4,5},{5,6},{6,7},{7,0},{8,9},{9,10},{10,1... | collective-permute-start | bytes 786440 | tf_op jit(solution)/shard_map/ppermute | solution.py:24
  58.6 2.8 %collective-permute-done.14 = bf16[32,4096]{1,0:T(8,128)(2,1)S(1)} collective-permute-done((bf16[32,4096]{1,0:T(8,128)(2,1)S(1)}, bf16[32,4096]{1,0:T(8,128)(2,1)S(1)}, u32[]{:S(2)}, u32[]{:S(2)}) %collective-permute-start.14) | collective-permute-done | bytes 262176 | tf_op jit(solution)/shard_map/ppermute | solution.py:24
  67.1 2.8 %collective-permute-start.22 = (bf16[32,4096]{1,0:T(8,128)(2,1)S(1)}, bf16[32,4096]{1,0:T(8,128)(2,1)S(1)}, u32[]{:S(2)}, u32[]{:S(2)}) collective-permute-start(bf16[32,4096]{1,0:T(8,128)(2,1)S(1)} %collective-permute-done.16), channel_id=1, source_target_pairs={{0,7},{1,0},{2,1},{3,2},{4,3},{5,4},{6,5},{7,6},{8,15},{9,8},{10,9... | collective-permute-start | bytes 786440 | tf_op jit(solution)/shard_map/ppermute | solution.py:24
  69.9 3.5 %collective-permute-done.17 = bf16[32,4096]{1,0:T(8,128)(2,1)S(1)} collective-permute-done((bf16[32,4096]{1,0:T(8,128)(2,1)S(1)}, bf16[32,4096]{1,0:T(8,128)(2,1)S(1)}, u32[]{:S(2)}, u32[]{:S(2)}) %collective-permute-start.17) | collective-permute-done | bytes 262176 | tf_op jit(solution)/shard_map/ppermute | solution.py:24
  74.3 2.8 %collective-permute-start.20 = (bf16[32,4096]{1,0:T(8,128)(2,1)S(1)}, bf16[32,4096]{1,0:T(8,128)(2,1)S(1)}, u32[]{:S(2)}, u32[]{:S(2)}) collective-permute-start(bf16[32,4096]{1,0:T(8,128)(2,1)S(1)} %collective-permute-done.18), channel_id=1, source_target_pairs={{0,7},{1,0},{2,1},{3,2},{4,3},{5,4},{6,5},{7,6},{8,15},{9,8},{10,9... | collective-permute-start | bytes 786440 | tf_op jit(solution)/shard_map/ppermute | solution.py:24
  77.2 1.9 %collective-permute-start.23 = (bf16[64,4096]{1,0:T(8,128)(2,1)S(1)}, bf16[64,4096]{1,0:T(8,128)(2,1)S(1)}, u32[]{:S(2)}, u32[]{:S(2)}) collective-permute-start(bf16[64,4096]{1,0:T(8,128)(2,1)S(1)} %pad_maximum_fusion), channel_id=1, source_target_pairs={{0,8},{1,9},{2,10},{3,11},{4,12},{5,13},{6,14},{7,15},{8,0},{9,1},... | collective-permute-start | bytes 1572872 | tf_op jit(solution)/shard_map/ppermute | solution.py:24
  80.1 3.1 %fusion.68 = f32[128,512]{1,0:T(8,128)S(1)} fusion(bf16[128,4096]{1,0:T(8,128)(2,1)S(1)} %constant_dynamic-update-slice_fusion.6, bf16[4096,512]{1,0:T(8,128)(2,1)} %param.14), kind=kOutput, calls=%fused_computation.180 | convolution fusion | flops 536870912 | bytes 5505024 | tf_op jit(solution)/shard_map/dot_general | solution.py:100
  85.1 1.8 %copy-done.1 = bf16[4096,512]{1,0:T(8,128)(2,1)S(1)} copy-done((bf16[4096,512]{1,0:T(8,128)(2,1)S(1)}, bf16[4096,512]{1,0:T(8,128)(2,1)}, u32[]{:S(2)}) %copy-start.1) | copy-done | bytes 4194328
  88.9 3.2 %collective-permute-start.25 = (bf16[16,4096]{1,0:T(8,128)(2,1)S(1)}, bf16[16,4096]{1,0:T(8,128)(2,1)S(1)}, u32[]{:S(2)}, u32[]{:S(2)}) collective-permute-start(bf16[16,4096]{1,0:T(8,128)(2,1)S(1)} %slice.177), channel_id=1, source_target_pairs={{0,7},{1,0},{2,1},{3,2},{4,3},{5,4},{6,5},{7,6},{8,15},{9,8},{10,9... | collective-permute-start | bytes 393224 | tf_op jit(solution)/shard_map/ppermute | solution.py:24
  92.7 2.4 %collective-permute-done.24 = bf16[16,4096]{1,0:T(8,128)(2,1)S(1)} collective-permute-done((bf16[16,4096]{1,0:T(8,128)(2,1)S(1)}, bf16[16,4096]{1,0:T(8,128)(2,1)S(1)}, u32[]{:S(2)}, u32[]{:S(2)}) %collective-permute-start.24) | collective-permute-done | bytes 131104 | tf_op jit(solution)/shard_map/ppermute | solution.py:24
  97.7 3.6 %collective-permute-done.26 = bf16[64,4096]{1,0:T(8,128)(2,1)S(1)} collective-permute-done((bf16[64,4096]{1,0:T(8,128)(2,1)S(1)}, bf16[64,4096]{1,0:T(8,128)(2,1)S(1)}, u32[]{:S(2)}, u32[]{:S(2)}) %collective-permute-start.26) | collective-permute-done | bytes 524320 | tf_op jit(solution)/shard_map/ppermute | solution.py:24
  101.4 2.7 %collective-permute-done.27 = bf16[32,4096]{1,0:T(8,128)(2,1)S(1)} collective-permute-done((bf16[32,4096]{1,0:T(8,128)(2,1)S(1)}, bf16[32,4096]{1,0:T(8,128)(2,1)S(1)}, u32[]{:S(2)}, u32[]{:S(2)}) %collective-permute-start.27) | collective-permute-done | bytes 262176 | tf_op jit(solution)/shard_map/ppermute | solution.py:24
  (127 shorter events, 34.1 us)
Async XLA Ops:
  2.8 11.9 %collective-permute-start = (bf16[32,4096]{1,0:T(8,128)(2,1)S(1)}, bf16[32,4096]{1,0:T(8,128)(2,1)S(1)}, u32[]{:S(2)}, u32[]{:S(2)}) collective-permute-start(bf16[32,4096]{1,0:T(8,128)(2,1)S(1)} %convolution_convert_fusion.7), channel_id=1, source_target_pairs={{0,8},{1,9},{2,10},{3,11},{4,12},{5,13},{6,14},{7,15},{8,0},{9,1},... | collective-permute-start | bytes 786440 | tf_op jit(solution)/shard_map/ppermute | solution.py:24
  5.2 18.1 %collective-permute-start.3 = (bf16[64,4096]{1,0:T(8,128)(2,1)S(1)}, bf16[64,4096]{1,0:T(8,128)(2,1)S(1)}, u32[]{:S(2)}, u32[]{:S(2)}) collective-permute-start(bf16[64,4096]{1,0:T(8,128)(2,1)S(1)} %get-tuple-element.107), channel_id=1, source_target_pairs={{0,8},{1,9},{2,10},{3,11},{4,12},{5,13},{6,14},{7,15},{8,0},{9,1},... | collective-permute-start | bytes 1572872 | tf_op jit(solution)/shard_map/ppermute | solution.py:24
  5.7 12.5 %collective-permute-start.4 = (bf16[32,4096]{1,0:T(8,128)(2,1)S(1)}, bf16[32,4096]{1,0:T(8,128)(2,1)S(1)}, u32[]{:S(2)}, u32[]{:S(2)}) collective-permute-start(bf16[32,4096]{1,0:T(8,128)(2,1)S(1)} %get-tuple-element.109), channel_id=1, source_target_pairs={{0,1},{1,2},{2,3},{3,4},{4,5},{5,6},{6,7},{7,0},{8,9},{9,10},{10,1... | collective-permute-start | bytes 786440 | tf_op jit(solution)/shard_map/ppermute | solution.py:24
  7.8 12.0 %collective-permute-start.5 = (bf16[32,4096]{1,0:T(8,128)(2,1)S(1)}, bf16[32,4096]{1,0:T(8,128)(2,1)S(1)}, u32[]{:S(2)}, u32[]{:S(2)}) collective-permute-start(bf16[32,4096]{1,0:T(8,128)(2,1)S(1)} %get-tuple-element.108), channel_id=1, source_target_pairs={{0,7},{1,0},{2,1},{3,2},{4,3},{5,4},{6,5},{7,6},{8,15},{9,8},{10,9... | collective-permute-start | bytes 786440 | tf_op jit(solution)/shard_map/ppermute | solution.py:24
  18.2 15.2 %collective-permute-start.9 = (bf16[64,4096]{1,0:T(8,128)(2,1)S(1)}, bf16[64,4096]{1,0:T(8,128)(2,1)S(1)}, u32[]{:S(2)}, u32[]{:S(2)}) collective-permute-start(bf16[64,4096]{1,0:T(8,128)(2,1)S(1)} %get-tuple-element.106), channel_id=1, source_target_pairs={{0,8},{1,9},{2,10},{3,11},{4,12},{5,13},{6,14},{7,15},{8,0},{9,1},... | collective-permute-start | bytes 1572872 | tf_op jit(solution)/shard_map/ppermute | solution.py:24
  23.5 10.3 %collective-permute-start.7 = (bf16[32,4096]{1,0:T(8,128)(2,1)S(1)}, bf16[32,4096]{1,0:T(8,128)(2,1)S(1)}, u32[]{:S(2)}, u32[]{:S(2)}) collective-permute-start(bf16[32,4096]{1,0:T(8,128)(2,1)S(1)} %get-tuple-element.113), channel_id=1, source_target_pairs={{0,1},{1,2},{2,3},{3,4},{4,5},{5,6},{6,7},{7,0},{8,9},{9,10},{10,1... | collective-permute-start | bytes 786440 | tf_op jit(solution)/shard_map/ppermute | solution.py:24
  25.5 8.3 %collective-permute-start.8 = (bf16[32,4096]{1,0:T(8,128)(2,1)S(1)}, bf16[32,4096]{1,0:T(8,128)(2,1)S(1)}, u32[]{:S(2)}, u32[]{:S(2)}) collective-permute-start(bf16[32,4096]{1,0:T(8,128)(2,1)S(1)} %get-tuple-element.112), channel_id=1, source_target_pairs={{0,7},{1,0},{2,1},{3,2},{4,3},{5,4},{6,5},{7,6},{8,15},{9,8},{10,9... | collective-permute-start | bytes 786440 | tf_op jit(solution)/shard_map/ppermute | solution.py:24
  34.0 11.0 %collective-permute-start.10 = (bf16[32,4096]{1,0:T(8,128)(2,1)S(1)}, bf16[32,4096]{1,0:T(8,128)(2,1)S(1)}, u32[]{:S(2)}, u32[]{:S(2)}) collective-permute-start(bf16[32,4096]{1,0:T(8,128)(2,1)S(1)} %get-tuple-element.111), channel_id=1, source_target_pairs={{0,1},{1,2},{2,3},{3,4},{4,5},{5,6},{6,7},{7,0},{8,9},{9,10},{10,1... | collective-permute-start | bytes 786440 | tf_op jit(solution)/shard_map/ppermute | solution.py:24
  35.6 9.4 %collective-permute-start.11 = (bf16[32,4096]{1,0:T(8,128)(2,1)S(1)}, bf16[32,4096]{1,0:T(8,128)(2,1)S(1)}, u32[]{:S(2)}, u32[]{:S(2)}) collective-permute-start(bf16[32,4096]{1,0:T(8,128)(2,1)S(1)} %get-tuple-element.110), channel_id=1, source_target_pairs={{0,7},{1,0},{2,1},{3,2},{4,3},{5,4},{6,5},{7,6},{8,15},{9,8},{10,9... | collective-permute-start | bytes 786440 | tf_op jit(solution)/shard_map/ppermute | solution.py:24
  39.8 8.7 %collective-permute-start.6 = (bf16[32,4096]{1,0:T(8,128)(2,1)S(1)}, bf16[32,4096]{1,0:T(8,128)(2,1)S(1)}, u32[]{:S(2)}, u32[]{:S(2)}) collective-permute-start(bf16[32,4096]{1,0:T(8,128)(2,1)S(1)} %add_convert_fusion.3), channel_id=1, source_target_pairs={{0,8},{1,9},{2,10},{3,11},{4,12},{5,13},{6,14},{7,15},{8,0},{9,1},... | collective-permute-start | bytes 786440 | tf_op jit(solution)/shard_map/ppermute | solution.py:24
  45.1 7.8 %collective-permute-start.12 = (bf16[32,4096]{1,0:T(8,128)(2,1)S(1)}, bf16[32,4096]{1,0:T(8,128)(2,1)S(1)}, u32[]{:S(2)}, u32[]{:S(2)}) collective-permute-start(bf16[32,4096]{1,0:T(8,128)(2,1)S(1)} %get-tuple-element.114), channel_id=1, source_target_pairs={{0,1},{1,2},{2,3},{3,4},{4,5},{5,6},{6,7},{7,0},{8,9},{9,10},{10,1... | collective-permute-start | bytes 786440 | tf_op jit(solution)/shard_map/ppermute | solution.py:24
  45.2 7.7 %collective-permute-start.13 = (bf16[32,4096]{1,0:T(8,128)(2,1)S(1)}, bf16[32,4096]{1,0:T(8,128)(2,1)S(1)}, u32[]{:S(2)}, u32[]{:S(2)}) collective-permute-start(bf16[32,4096]{1,0:T(8,128)(2,1)S(1)} %get-tuple-element.115), channel_id=1, source_target_pairs={{0,7},{1,0},{2,1},{3,2},{4,3},{5,4},{6,5},{7,6},{8,15},{9,8},{10,9... | collective-permute-start | bytes 786440 | tf_op jit(solution)/shard_map/ppermute | solution.py:24
  53.7 7.7 %collective-permute-start.14 = (bf16[32,4096]{1,0:T(8,128)(2,1)S(1)}, bf16[32,4096]{1,0:T(8,128)(2,1)S(1)}, u32[]{:S(2)}, u32[]{:S(2)}) collective-permute-start(bf16[32,4096]{1,0:T(8,128)(2,1)S(1)} %add_convert_fusion), channel_id=1, source_target_pairs={{0,1},{1,2},{2,3},{3,4},{4,5},{5,6},{6,7},{7,0},{8,9},{9,10},{10,1... | collective-permute-start | bytes 786440 | tf_op jit(solution)/shard_map/ppermute | solution.py:24
  56.1 6.5 %collective-permute-start.15 = (bf16[32,4096]{1,0:T(8,128)(2,1)S(1)}, bf16[32,4096]{1,0:T(8,128)(2,1)}, u32[]{:S(2)}, u32[]{:S(2)}) collective-permute-start(bf16[32,4096]{1,0:T(8,128)(2,1)S(1)} %add_convert_fusion), channel_id=1, source_target_pairs={{0,7},{1,0},{2,1},{3,2},{4,3},{5,4},{6,5},{7,6},{8,15},{9,8},{10,9... | collective-permute-start | bytes 786440 | tf_op jit(solution)/shard_map/ppermute | solution.py:24
  57.1 6.4 %collective-permute-start.16 = (bf16[32,4096]{1,0:T(8,128)(2,1)S(1)}, bf16[32,4096]{1,0:T(8,128)(2,1)S(1)}, u32[]{:S(2)}, u32[]{:S(2)}) collective-permute-start(bf16[32,4096]{1,0:T(8,128)(2,1)S(1)} %add_convert_fusion), channel_id=1, source_target_pairs={{0,8},{1,9},{2,10},{3,11},{4,12},{5,13},{6,14},{7,15},{8,0},{9,1},... | collective-permute-start | bytes 786440 | tf_op jit(solution)/shard_map/ppermute | solution.py:24
  63.4 9.9 %collective-permute-start.17 = (bf16[32,4096]{1,0:T(8,128)(2,1)S(1)}, bf16[32,4096]{1,0:T(8,128)(2,1)S(1)}, u32[]{:S(2)}, u32[]{:S(2)}) collective-permute-start(bf16[32,4096]{1,0:T(8,128)(2,1)S(1)} %collective-permute-done.14), channel_id=1, source_target_pairs={{0,1},{1,2},{2,3},{3,4},{4,5},{5,6},{6,7},{7,0},{8,9},{9,10},{10,1... | collective-permute-start | bytes 786440 | tf_op jit(solution)/shard_map/ppermute | solution.py:24
  65.1 8.8 %collective-permute-start.18 = (bf16[32,4096]{1,0:T(8,128)(2,1)}, bf16[32,4096]{1,0:T(8,128)(2,1)S(1)}, u32[]{:S(2)}, u32[]{:S(2)}) collective-permute-start(bf16[32,4096]{1,0:T(8,128)(2,1)} %collective-permute-done.15), channel_id=1, source_target_pairs={{0,7},{1,0},{2,1},{3,2},{4,3},{5,4},{6,5},{7,6},{8,15},{9,8},{10,9... | collective-permute-start | bytes 786440 | tf_op jit(solution)/shard_map/ppermute | solution.py:24
  66.7 18.2 %collective-permute-start.21 = (bf16[32,4096]{1,0:T(8,128)(2,1)S(1)}, bf16[32,4096]{1,0:T(8,128)(2,1)S(1)}, u32[]{:S(2)}, u32[]{:S(2)}) collective-permute-start(bf16[32,4096]{1,0:T(8,128)(2,1)S(1)} %collective-permute-done.16), channel_id=1, source_target_pairs={{0,1},{1,2},{2,3},{3,4},{4,5},{5,6},{6,7},{7,0},{8,9},{9,10},{10,1... | collective-permute-start | bytes 786440 | tf_op jit(solution)/shard_map/ppermute | solution.py:24
  67.1 17.8 %collective-permute-start.22 = (bf16[32,4096]{1,0:T(8,128)(2,1)S(1)}, bf16[32,4096]{1,0:T(8,128)(2,1)S(1)}, u32[]{:S(2)}, u32[]{:S(2)}) collective-permute-start(bf16[32,4096]{1,0:T(8,128)(2,1)S(1)} %collective-permute-done.16), channel_id=1, source_target_pairs={{0,7},{1,0},{2,1},{3,2},{4,3},{5,4},{6,5},{7,6},{8,15},{9,8},{10,9... | collective-permute-start | bytes 786440 | tf_op jit(solution)/shard_map/ppermute | solution.py:24
  73.9 11.0 %collective-permute-start.19 = (bf16[32,4096]{1,0:T(8,128)(2,1)S(1)}, bf16[32,4096]{1,0:T(8,128)(2,1)S(1)}, u32[]{:S(2)}, u32[]{:S(2)}) collective-permute-start(bf16[32,4096]{1,0:T(8,128)(2,1)S(1)} %collective-permute-done.17), channel_id=1, source_target_pairs={{0,1},{1,2},{2,3},{3,4},{4,5},{5,6},{6,7},{7,0},{8,9},{9,10},{10,1... | collective-permute-start | bytes 786440 | tf_op jit(solution)/shard_map/ppermute | solution.py:24
  74.3 10.6 %collective-permute-start.20 = (bf16[32,4096]{1,0:T(8,128)(2,1)S(1)}, bf16[32,4096]{1,0:T(8,128)(2,1)S(1)}, u32[]{:S(2)}, u32[]{:S(2)}) collective-permute-start(bf16[32,4096]{1,0:T(8,128)(2,1)S(1)} %collective-permute-done.18), channel_id=1, source_target_pairs={{0,7},{1,0},{2,1},{3,2},{4,3},{5,4},{6,5},{7,6},{8,15},{9,8},{10,9... | collective-permute-start | bytes 786440 | tf_op jit(solution)/shard_map/ppermute | solution.py:24
  77.2 18.4 %collective-permute-start.23 = (bf16[64,4096]{1,0:T(8,128)(2,1)S(1)}, bf16[64,4096]{1,0:T(8,128)(2,1)S(1)}, u32[]{:S(2)}, u32[]{:S(2)}) collective-permute-start(bf16[64,4096]{1,0:T(8,128)(2,1)S(1)} %pad_maximum_fusion), channel_id=1, source_target_pairs={{0,8},{1,9},{2,10},{3,11},{4,12},{5,13},{6,14},{7,15},{8,0},{9,1},... | collective-permute-start | bytes 1572872 | tf_op jit(solution)/shard_map/ppermute | solution.py:24
  92.2 9.2 %collective-permute-start.26 = (bf16[64,4096]{1,0:T(8,128)(2,1)S(1)}, bf16[64,4096]{1,0:T(8,128)(2,1)S(1)}, u32[]{:S(2)}, u32[]{:S(2)}) collective-permute-start(bf16[64,4096]{1,0:T(8,128)(2,1)S(1)} %pad_maximum_fusion.1), channel_id=1, source_target_pairs={{0,8},{1,9},{2,10},{3,11},{4,12},{5,13},{6,14},{7,15},{8,0},{9,1},... | collective-permute-start | bytes 1572872 | tf_op jit(solution)/shard_map/ppermute | solution.py:24
  95.1 9.0 %collective-permute-start.27 = (bf16[32,4096]{1,0:T(8,128)(2,1)S(1)}, bf16[32,4096]{1,0:T(8,128)(2,1)S(1)}, u32[]{:S(2)}, u32[]{:S(2)}) collective-permute-start(bf16[32,4096]{1,0:T(8,128)(2,1)S(1)} %pad_maximum_fusion.2), channel_id=1, source_target_pairs={{0,8},{1,9},{2,10},{3,11},{4,12},{5,13},{6,14},{7,15},{8,0},{9,1},... | collective-permute-start | bytes 786440 | tf_op jit(solution)/shard_map/ppermute | solution.py:24
  (13 other events, 128.2 us)

commit v3 on v2

--- a/solution.py
+++ b/solution.py
@@ -124,20 +124,19 @@
     )
 
     up4, down4 = send(up3[:HALF], UP), send(down3[HALF:], DOWN)
-    three = send(jnp.concatenate([up3, down3], 0), ACROSS)
+    up4, down4, two, up2, hidden = hold((up4, down4, two, up2, hidden))
+
+    four = jnp.concatenate([up4, down4], 0)
+    other_four = send(four, ACROSS)
+    side_up3, side_down3 = send(two[:ROWS], UP), send(two[ROWS:], DOWN)
     hidden = units(
         hidden, [(side_up1, (1, -1)), (side_down1, (1, 1)), (up2, (0, -2)), (down2, (0, 2))]
     )
-    up4, down4, up3, down3, hidden = hold((up4, down4, up3, down3, hidden))
-
-    four = jnp.concatenate([up4, down4], 0)
-    other_four = send(four, ACROSS)
-    two, up3, down3, hidden = hold((two, up3, down3, hidden))
     hidden = units(
         hidden, [(two[:ROWS], (1, -2)), (two[ROWS:], (1, 2)), (up3, (0, -3)), (down3, (0, 3))]
     )
     hidden = units(
-        hidden, [(three[:ROWS], (1, -3)), (three[ROWS:], (1, 3)), (four, (0, 4)), (other_four, (1, 4))]
+        hidden, [(side_up3, (1, -3)), (side_down3, (1, 3)), (four, (0, 4)), (other_four, (1, 4))]
     )
     return (normed, hidden)
 

time: 107 us -> 105 us (0.981)
  waiting for transfers between devices: 33.3 us -> 29.1 us
  starting transfers between devices: 50.8 us -> 54.3 us
  local copies, waits for them, and re-layouts: 4.97 us -> 3.2 us
    ppermute x28 -> x29, waiting for transfers between devices: 33.3 us -> 29.1 us  [send(): return lax.ppermute(value, 'tensor', pairs)]
    ppermute x28 -> x29, starting transfers between devices: 50.8 us -> 54.3 us  [send(): return lax.ppermute(value, 'tensor', pairs)]
    unnamed x34 -> x35, local copies, waits for them, and re-layouts: 3.58 us -> 1.75 us
  transfers between devices with their start and end apart: 28 -> 29, of which waited for: 14 -> 14; matrix products, arithmetic and copies ran while one was open for 13% -> 13% of each run, Pallas kernels for 0% -> 0%
where the time goes in v3:
time: 105 us; the launch traced here: 104 us
  starting transfers between devices  54.3 us (52%)
  waiting for transfers between devices  29.1 us (28%)
  matrix products  13.9 us (13%)
  local copies, waits for them, and re-layouts  3.2 us (3%)
  other arithmetic  2.68 us (3%)
  between operations  1.29 us (1%)
    ppermute x29, starting transfers between devices, send(): return lax.ppermute(value, 'tensor', pairs)  54.3 us
    ppermute x29, waiting for transfers between devices, send(): return lax.ppermute(value, 'tensor', pairs)  29.1 us
    dot_general x4, matrix products, units(): gate = jnp.dot(rows, gate_weight, preferred_element_type=jnp.float32)  5.25 us
    dot_general x4, matrix products, units(): up = jnp.dot(rows, up_weight, preferred_element_type=jnp.float32)  4.68 us
    dot_general x8, matrix products, product(): return bf(jnp.dot(rows, out_weight, preferred_element_type=jnp.float32))  3.92 us
  transfers between devices with their start and end apart: 29, of which 14 were waited for; matrix products, arithmetic and copies ran while one was open for 13% of the time, Pallas kernels for 0%

profile of v3, /device:TPU:6, one launch (start us, length us, event | category | flops | bytes accessed | tf_op | source)
XLA Modules:
  0.0 104.4 jit_solution(18132333245515042648)
XLA Ops:
  2.8 1.6 %collective-permute-start = (bf16[32,4096]{1,0:T(8,128)(2,1)S(1)}, bf16[32,4096]{1,0:T(8,128)(2,1)S(1)}, u32[]{:S(2)}, u32[]{:S(2)}) collective-permute-start(bf16[32,4096]{1,0:T(8,128)(2,1)S(1)} %convolution_convert_fusion.7), channel_id=1, source_target_pairs={{0,8},{1,9},{2,10},{3,11},{4,12},{5,13},{6,14},{7,15},{8,0},{9,1},... | collective-permute-start | bytes 786440 | tf_op jit(solution)/shard_map/ppermute | solution.py:24
  5.7 2.0 %collective-permute-start.4 = (bf16[32,4096]{1,0:T(8,128)(2,1)S(1)}, bf16[32,4096]{1,0:T(8,128)(2,1)S(1)}, u32[]{:S(2)}, u32[]{:S(2)}) collective-permute-start(bf16[32,4096]{1,0:T(8,128)(2,1)S(1)} %get-tuple-element.101), channel_id=1, source_target_pairs={{0,1},{1,2},{2,3},{3,4},{4,5},{5,6},{6,7},{7,0},{8,9},{9,10},{10,1... | collective-permute-start | bytes 786440 | tf_op jit(solution)/shard_map/ppermute | solution.py:24
  7.8 4.0 %collective-permute-start.5 = (bf16[32,4096]{1,0:T(8,128)(2,1)S(1)}, bf16[32,4096]{1,0:T(8,128)(2,1)S(1)}, u32[]{:S(2)}, u32[]{:S(2)}) collective-permute-start(bf16[32,4096]{1,0:T(8,128)(2,1)S(1)} %get-tuple-element.100), channel_id=1, source_target_pairs={{0,7},{1,0},{2,1},{3,2},{4,3},{5,4},{6,5},{7,6},{8,15},{9,8},{10,9... | collective-permute-start | bytes 786440 | tf_op jit(solution)/shard_map/ppermute | solution.py:24
  14.9 3.3 %collective-permute-start.2 = (bf16[16,4096]{1,0:T(8,128)(2,1)S(1)}, bf16[16,4096]{1,0:T(8,128)(2,1)S(1)}, u32[]{:S(2)}, u32[]{:S(2)}) collective-permute-start(bf16[16,4096]{1,0:T(8,128)(2,1)S(1)} %get-tuple-element.110), channel_id=1, source_target_pairs={{0,7},{1,0},{2,1},{3,2},{4,3},{5,4},{6,5},{7,6},{8,15},{9,8},{10,9... | collective-permute-start | bytes 393224 | tf_op jit(solution)/shard_map/ppermute | solution.py:24
  21.1 2.2 %collective-permute-done.3 = bf16[64,4096]{1,0:T(8,128)(2,1)S(1)} collective-permute-done((bf16[64,4096]{1,0:T(8,128)(2,1)S(1)}, bf16[64,4096]{1,0:T(8,128)(2,1)S(1)}, u32[]{:S(2)}, u32[]{:S(2)}) %collective-permute-start.3) | collective-permute-done | bytes 524320 | tf_op jit(solution)/shard_map/ppermute | solution.py:24
  23.5 2.0 %collective-permute-start.7 = (bf16[32,4096]{1,0:T(8,128)(2,1)S(1)}, bf16[32,4096]{1,0:T(8,128)(2,1)S(1)}, u32[]{:S(2)}, u32[]{:S(2)}) collective-permute-start(bf16[32,4096]{1,0:T(8,128)(2,1)S(1)} %get-tuple-element.105), channel_id=1, source_target_pairs={{0,1},{1,2},{2,3},{3,4},{4,5},{5,6},{6,7},{7,0},{8,9},{9,10},{10,1... | collective-permute-start | bytes 786440 | tf_op jit(solution)/shard_map/ppermute | solution.py:24
  25.5 4.0 %collective-permute-start.8 = (bf16[32,4096]{1,0:T(8,128)(2,1)S(1)}, bf16[32,4096]{1,0:T(8,128)(2,1)S(1)}, u32[]{:S(2)}, u32[]{:S(2)}) collective-permute-start(bf16[32,4096]{1,0:T(8,128)(2,1)S(1)} %get-tuple-element.104), channel_id=1, source_target_pairs={{0,7},{1,0},{2,1},{3,2},{4,3},{5,4},{6,5},{7,6},{8,15},{9,8},{10,9... | collective-permute-start | bytes 786440 | tf_op jit(solution)/shard_map/ppermute | solution.py:24
  29.5 3.8 %collective-permute-done.9 = bf16[64,4096]{1,0:T(8,128)(2,1)S(1)} collective-permute-done((bf16[64,4096]{1,0:T(8,128)(2,1)S(1)}, bf16[64,4096]{1,0:T(8,128)(2,1)S(1)}, u32[]{:S(2)}, u32[]{:S(2)}) %collective-permute-start.9) | collective-permute-done | bytes 524320 | tf_op jit(solution)/shard_map/ppermute | solution.py:24
  34.0 1.6 %collective-permute-start.10 = (bf16[32,4096]{1,0:T(8,128)(2,1)S(1)}, bf16[32,4096]{1,0:T(8,128)(2,1)S(1)}, u32[]{:S(2)}, u32[]{:S(2)}) collective-permute-start(bf16[32,4096]{1,0:T(8,128)(2,1)S(1)} %get-tuple-element.103), channel_id=1, source_target_pairs={{0,1},{1,2},{2,3},{3,4},{4,5},{5,6},{6,7},{7,0},{8,9},{9,10},{10,1... | collective-permute-start | bytes 786440 | tf_op jit(solution)/shard_map/ppermute | solution.py:24
  35.6 4.0 %collective-permute-start.11 = (bf16[32,4096]{1,0:T(8,128)(2,1)S(1)}, bf16[32,4096]{1,0:T(8,128)(2,1)S(1)}, u32[]{:S(2)}, u32[]{:S(2)}) collective-permute-start(bf16[32,4096]{1,0:T(8,128)(2,1)S(1)} %get-tuple-element.102), channel_id=1, source_target_pairs={{0,7},{1,0},{2,1},{3,2},{4,3},{5,4},{6,5},{7,6},{8,15},{9,8},{10,9... | collective-permute-start | bytes 786440 | tf_op jit(solution)/shard_map/ppermute | solution.py:24
  39.8 1.8 %collective-permute-start.6 = (bf16[32,4096]{1,0:T(8,128)(2,1)S(1)}, bf16[32,4096]{1,0:T(8,128)(2,1)S(1)}, u32[]{:S(2)}, u32[]{:S(2)}) collective-permute-start(bf16[32,4096]{1,0:T(8,128)(2,1)S(1)} %add_convert_fusion.3), channel_id=1, source_target_pairs={{0,8},{1,9},{2,10},{3,11},{4,12},{5,13},{6,14},{7,15},{8,0},{9,1},... | collective-permute-start | bytes 786440 | tf_op jit(solution)/shard_map/ppermute | solution.py:24
  41.6 3.4 %collective-permute-done.10 = bf16[32,4096]{1,0:T(8,128)(2,1)S(1)} collective-permute-done((bf16[32,4096]{1,0:T(8,128)(2,1)S(1)}, bf16[32,4096]{1,0:T(8,128)(2,1)S(1)}, u32[]{:S(2)}, u32[]{:S(2)}) %collective-permute-start.10) | collective-permute-done | bytes 262176 | tf_op jit(solution)/shard_map/ppermute | solution.py:24
  45.2 3.2 %collective-permute-start.13 = (bf16[32,4096]{1,0:T(8,128)(2,1)S(1)}, bf16[32,4096]{1,0:T(8,128)(2,1)S(1)}, u32[]{:S(2)}, u32[]{:S(2)}) collective-permute-start(bf16[32,4096]{1,0:T(8,128)(2,1)S(1)} %get-tuple-element.109), channel_id=1, source_target_pairs={{0,7},{1,0},{2,1},{3,2},{4,3},{5,4},{6,5},{7,6},{8,15},{9,8},{10,9... | collective-permute-start | bytes 786440 | tf_op jit(solution)/shard_map/ppermute | solution.py:24
  48.5 4.5 %collective-permute-done.12 = bf16[32,4096]{1,0:T(8,128)(2,1)S(1)} collective-permute-done((bf16[32,4096]{1,0:T(8,128)(2,1)S(1)}, bf16[32,4096]{1,0:T(8,128)(2,1)S(1)}, u32[]{:S(2)}, u32[]{:S(2)}) %collective-permute-start.12) | collective-permute-done | bytes 262176 | tf_op jit(solution)/shard_map/ppermute | solution.py:24
  53.7 2.4 %collective-permute-start.14 = (bf16[32,4096]{1,0:T(8,128)(2,1)S(1)}, bf16[32,4096]{1,0:T(8,128)(2,1)S(1)}, u32[]{:S(2)}, u32[]{:S(2)}) collective-permute-start(bf16[32,4096]{1,0:T(8,128)(2,1)S(1)} %add_convert_fusion), channel_id=1, source_target_pairs={{0,1},{1,2},{2,3},{3,4},{4,5},{5,6},{6,7},{7,0},{8,9},{9,10},{10,1... | collective-permute-start | bytes 786440 | tf_op jit(solution)/shard_map/ppermute | solution.py:24
  58.6 2.8 %collective-permute-done.14 = bf16[32,4096]{1,0:T(8,128)(2,1)S(1)} collective-permute-done((bf16[32,4096]{1,0:T(8,128)(2,1)S(1)}, bf16[32,4096]{1,0:T(8,128)(2,1)S(1)}, u32[]{:S(2)}, u32[]{:S(2)}) %collective-permute-start.14) | collective-permute-done | bytes 262176 | tf_op jit(solution)/shard_map/ppermute | solution.py:24
  63.4 1.6 %collective-permute-start.17 = (bf16[32,4096]{1,0:T(8,128)(2,1)S(1)}, bf16[32,4096]{1,0:T(8,128)(2,1)S(1)}, u32[]{:S(2)}, u32[]{:S(2)}) collective-permute-start(bf16[32,4096]{1,0:T(8,128)(2,1)S(1)} %collective-permute-done.14), channel_id=1, source_target_pairs={{0,1},{1,2},{2,3},{3,4},{4,5},{5,6},{6,7},{7,0},{8,9},{9,10},{10,1... | collective-permute-start | bytes 786440 | tf_op jit(solution)/shard_map/ppermute | solution.py:24
  67.1 2.8 %collective-permute-start.22 = (bf16[32,4096]{1,0:T(8,128)(2,1)S(1)}, bf16[32,4096]{1,0:T(8,128)(2,1)S(1)}, u32[]{:S(2)}, u32[]{:S(2)}) collective-permute-start(bf16[32,4096]{1,0:T(8,128)(2,1)S(1)} %collective-permute-done.16), channel_id=1, source_target_pairs={{0,7},{1,0},{2,1},{3,2},{4,3},{5,4},{6,5},{7,6},{8,15},{9,8},{10,9... | collective-permute-start | bytes 786440 | tf_op jit(solution)/shard_map/ppermute | solution.py:24
  69.9 3.5 %collective-permute-done.17 = bf16[32,4096]{1,0:T(8,128)(2,1)S(1)} collective-permute-done((bf16[32,4096]{1,0:T(8,128)(2,1)S(1)}, bf16[32,4096]{1,0:T(8,128)(2,1)S(1)}, u32[]{:S(2)}, u32[]{:S(2)}) %collective-permute-start.17) | collective-permute-done | bytes 262176 | tf_op jit(solution)/shard_map/ppermute | solution.py:24
  74.2 2.9 %collective-permute-start.20 = (bf16[32,4096]{1,0:T(8,128)(2,1)S(1)}, bf16[32,4096]{1,0:T(8,128)(2,1)S(1)}, u32[]{:S(2)}, u32[]{:S(2)}) collective-permute-start(bf16[32,4096]{1,0:T(8,128)(2,1)S(1)} %collective-permute-done.18), channel_id=1, source_target_pairs={{0,7},{1,0},{2,1},{3,2},{4,3},{5,4},{6,5},{7,6},{8,15},{9,8},{10,9... | collective-permute-start | bytes 786440 | tf_op jit(solution)/shard_map/ppermute | solution.py:24
  79.8 3.1 %fusion.69 = f32[128,512]{1,0:T(8,128)S(1)} fusion(bf16[128,4096]{1,0:T(8,128)(2,1)S(1)} %constant_dynamic-update-slice_fusion.6, bf16[4096,512]{1,0:T(8,128)(2,1)} %param.14), kind=kOutput, calls=%fused_computation.181 | convolution fusion | flops 536870912 | bytes 5505024 | tf_op jit(solution)/shard_map/dot_general | solution.py:100
  84.9 3.3 %collective-permute-start.24 = (bf16[16,4096]{1,0:T(8,128)(2,1)S(1)}, bf16[16,4096]{1,0:T(8,128)(2,1)S(1)}, u32[]{:S(2)}, u32[]{:S(2)}) collective-permute-start(bf16[16,4096]{1,0:T(8,128)(2,1)S(1)} %slice.180), channel_id=1, source_target_pairs={{0,7},{1,0},{2,1},{3,2},{4,3},{5,4},{6,5},{7,6},{8,15},{9,8},{10,9... | collective-permute-start | bytes 393224 | tf_op jit(solution)/shard_map/ppermute | solution.py:24
  88.2 4.0 %collective-permute-done.23 = bf16[16,4096]{1,0:T(8,128)(2,1)S(1)} collective-permute-done((bf16[16,4096]{1,0:T(8,128)(2,1)S(1)}, bf16[16,4096]{1,0:T(8,128)(2,1)S(1)}, u32[]{:S(2)}, u32[]{:S(2)}) %collective-permute-start.23) | collective-permute-done | bytes 131104 | tf_op jit(solution)/shard_map/ppermute | solution.py:24
  93.5 1.7 %collective-permute-start.26 = (bf16[32,4096]{1,0:T(8,128)(2,1)S(1)}, bf16[32,4096]{1,0:T(8,128)(2,1)S(1)}, u32[]{:S(2)}, u32[]{:S(2)}) collective-permute-start(bf16[32,4096]{1,0:T(8,128)(2,1)S(1)} %get-tuple-element.107), channel_id=1, source_target_pairs={{0,1},{1,2},{2,3},{3,4},{4,5},{5,6},{6,7},{7,0},{8,9},{9,10},{10,1... | collective-permute-start | bytes 786440 | tf_op jit(solution)/shard_map/ppermute | solution.py:24
  (129 shorter events, 33.3 us)
Async XLA Ops:
  2.8 11.9 %collective-permute-start = (bf16[32,4096]{1,0:T(8,128)(2,1)S(1)}, bf16[32,4096]{1,0:T(8,128)(2,1)S(1)}, u32[]{:S(2)}, u32[]{:S(2)}) collective-permute-start(bf16[32,4096]{1,0:T(8,128)(2,1)S(1)} %convolution_convert_fusion.7), channel_id=1, source_target_pairs={{0,8},{1,9},{2,10},{3,11},{4,12},{5,13},{6,14},{7,15},{8,0},{9,1},... | collective-permute-start | bytes 786440 | tf_op jit(solution)/shard_map/ppermute | solution.py:24
  5.2 18.1 %collective-permute-start.3 = (bf16[64,4096]{1,0:T(8,128)(2,1)S(1)}, bf16[64,4096]{1,0:T(8,128)(2,1)S(1)}, u32[]{:S(2)}, u32[]{:S(2)}) collective-permute-start(bf16[64,4096]{1,0:T(8,128)(2,1)S(1)} %get-tuple-element.99), channel_id=1, source_target_pairs={{0,8},{1,9},{2,10},{3,11},{4,12},{5,13},{6,14},{7,15},{8,0},{9,1},... | collective-permute-start | bytes 1572872 | tf_op jit(solution)/shard_map/ppermute | solution.py:24
  5.7 12.5 %collective-permute-start.4 = (bf16[32,4096]{1,0:T(8,128)(2,1)S(1)}, bf16[32,4096]{1,0:T(8,128)(2,1)S(1)}, u32[]{:S(2)}, u32[]{:S(2)}) collective-permute-start(bf16[32,4096]{1,0:T(8,128)(2,1)S(1)} %get-tuple-element.101), channel_id=1, source_target_pairs={{0,1},{1,2},{2,3},{3,4},{4,5},{5,6},{6,7},{7,0},{8,9},{9,10},{10,1... | collective-permute-start | bytes 786440 | tf_op jit(solution)/shard_map/ppermute | solution.py:24
  7.8 12.0 %collective-permute-start.5 = (bf16[32,4096]{1,0:T(8,128)(2,1)S(1)}, bf16[32,4096]{1,0:T(8,128)(2,1)S(1)}, u32[]{:S(2)}, u32[]{:S(2)}) collective-permute-start(bf16[32,4096]{1,0:T(8,128)(2,1)S(1)} %get-tuple-element.100), channel_id=1, source_target_pairs={{0,7},{1,0},{2,1},{3,2},{4,3},{5,4},{6,5},{7,6},{8,15},{9,8},{10,9... | collective-permute-start | bytes 786440 | tf_op jit(solution)/shard_map/ppermute | solution.py:24
  18.2 15.2 %collective-permute-start.9 = (bf16[64,4096]{1,0:T(8,128)(2,1)S(1)}, bf16[64,4096]{1,0:T(8,128)(2,1)S(1)}, u32[]{:S(2)}, u32[]{:S(2)}) collective-permute-start(bf16[64,4096]{1,0:T(8,128)(2,1)S(1)} %get-tuple-element.98), channel_id=1, source_target_pairs={{0,8},{1,9},{2,10},{3,11},{4,12},{5,13},{6,14},{7,15},{8,0},{9,1},... | collective-permute-start | bytes 1572872 | tf_op jit(solution)/shard_map/ppermute | solution.py:24
  23.5 10.3 %collective-permute-start.7 = (bf16[32,4096]{1,0:T(8,128)(2,1)S(1)}, bf16[32,4096]{1,0:T(8,128)(2,1)S(1)}, u32[]{:S(2)}, u32[]{:S(2)}) collective-permute-start(bf16[32,4096]{1,0:T(8,128)(2,1)S(1)} %get-tuple-element.105), channel_id=1, source_target_pairs={{0,1},{1,2},{2,3},{3,4},{4,5},{5,6},{6,7},{7,0},{8,9},{9,10},{10,1... | collective-permute-start | bytes 786440 | tf_op jit(solution)/shard_map/ppermute | solution.py:24
  25.5 8.3 %collective-permute-start.8 = (bf16[32,4096]{1,0:T(8,128)(2,1)S(1)}, bf16[32,4096]{1,0:T(8,128)(2,1)S(1)}, u32[]{:S(2)}, u32[]{:S(2)}) collective-permute-start(bf16[32,4096]{1,0:T(8,128)(2,1)S(1)} %get-tuple-element.104), channel_id=1, source_target_pairs={{0,7},{1,0},{2,1},{3,2},{4,3},{5,4},{6,5},{7,6},{8,15},{9,8},{10,9... | collective-permute-start | bytes 786440 | tf_op jit(solution)/shard_map/ppermute | solution.py:24
  34.0 11.0 %collective-permute-start.10 = (bf16[32,4096]{1,0:T(8,128)(2,1)S(1)}, bf16[32,4096]{1,0:T(8,128)(2,1)S(1)}, u32[]{:S(2)}, u32[]{:S(2)}) collective-permute-start(bf16[32,4096]{1,0:T(8,128)(2,1)S(1)} %get-tuple-element.103), channel_id=1, source_target_pairs={{0,1},{1,2},{2,3},{3,4},{4,5},{5,6},{6,7},{7,0},{8,9},{9,10},{10,1... | collective-permute-start | bytes 786440 | tf_op jit(solution)/shard_map/ppermute | solution.py:24
  35.6 9.4 %collective-permute-start.11 = (bf16[32,4096]{1,0:T(8,128)(2,1)S(1)}, bf16[32,4096]{1,0:T(8,128)(2,1)S(1)}, u32[]{:S(2)}, u32[]{:S(2)}) collective-permute-start(bf16[32,4096]{1,0:T(8,128)(2,1)S(1)} %get-tuple-element.102), channel_id=1, source_target_pairs={{0,7},{1,0},{2,1},{3,2},{4,3},{5,4},{6,5},{7,6},{8,15},{9,8},{10,9... | collective-permute-start | bytes 786440 | tf_op jit(solution)/shard_map/ppermute | solution.py:24
  39.8 8.7 %collective-permute-start.6 = (bf16[32,4096]{1,0:T(8,128)(2,1)S(1)}, bf16[32,4096]{1,0:T(8,128)(2,1)S(1)}, u32[]{:S(2)}, u32[]{:S(2)}) collective-permute-start(bf16[32,4096]{1,0:T(8,128)(2,1)S(1)} %add_convert_fusion.3), channel_id=1, source_target_pairs={{0,8},{1,9},{2,10},{3,11},{4,12},{5,13},{6,14},{7,15},{8,0},{9,1},... | collective-permute-start | bytes 786440 | tf_op jit(solution)/shard_map/ppermute | solution.py:24
  45.1 7.8 %collective-permute-start.12 = (bf16[32,4096]{1,0:T(8,128)(2,1)S(1)}, bf16[32,4096]{1,0:T(8,128)(2,1)S(1)}, u32[]{:S(2)}, u32[]{:S(2)}) collective-permute-start(bf16[32,4096]{1,0:T(8,128)(2,1)S(1)} %get-tuple-element.108), channel_id=1, source_target_pairs={{0,1},{1,2},{2,3},{3,4},{4,5},{5,6},{6,7},{7,0},{8,9},{9,10},{10,1... | collective-permute-start | bytes 786440 | tf_op jit(solution)/shard_map/ppermute | solution.py:24
  45.2 7.7 %collective-permute-start.13 = (bf16[32,4096]{1,0:T(8,128)(2,1)S(1)}, bf16[32,4096]{1,0:T(8,128)(2,1)S(1)}, u32[]{:S(2)}, u32[]{:S(2)}) collective-permute-start(bf16[32,4096]{1,0:T(8,128)(2,1)S(1)} %get-tuple-element.109), channel_id=1, source_target_pairs={{0,7},{1,0},{2,1},{3,2},{4,3},{5,4},{6,5},{7,6},{8,15},{9,8},{10,9... | collective-permute-start | bytes 786440 | tf_op jit(solution)/shard_map/ppermute | solution.py:24
  53.7 7.7 %collective-permute-start.14 = (bf16[32,4096]{1,0:T(8,128)(2,1)S(1)}, bf16[32,4096]{1,0:T(8,128)(2,1)S(1)}, u32[]{:S(2)}, u32[]{:S(2)}) collective-permute-start(bf16[32,4096]{1,0:T(8,128)(2,1)S(1)} %add_convert_fusion), channel_id=1, source_target_pairs={{0,1},{1,2},{2,3},{3,4},{4,5},{5,6},{6,7},{7,0},{8,9},{9,10},{10,1... | collective-permute-start | bytes 786440 | tf_op jit(solution)/shard_map/ppermute | solution.py:24
  63.4 9.9 %collective-permute-start.17 = (bf16[32,4096]{1,0:T(8,128)(2,1)S(1)}, bf16[32,4096]{1,0:T(8,128)(2,1)S(1)}, u32[]{:S(2)}, u32[]{:S(2)}) collective-permute-start(bf16[32,4096]{1,0:T(8,128)(2,1)S(1)} %collective-permute-done.14), channel_id=1, source_target_pairs={{0,1},{1,2},{2,3},{3,4},{4,5},{5,6},{6,7},{7,0},{8,9},{9,10},{10,1... | collective-permute-start | bytes 786440 | tf_op jit(solution)/shard_map/ppermute | solution.py:24
  65.1 8.7 %collective-permute-start.18 = (bf16[32,4096]{1,0:T(8,128)(2,1)}, bf16[32,4096]{1,0:T(8,128)(2,1)S(1)}, u32[]{:S(2)}, u32[]{:S(2)}) collective-permute-start(bf16[32,4096]{1,0:T(8,128)(2,1)} %collective-permute-done.15), channel_id=1, source_target_pairs={{0,7},{1,0},{2,1},{3,2},{4,3},{5,4},{6,5},{7,6},{8,15},{9,8},{10,9... | collective-permute-start | bytes 786440 | tf_op jit(solution)/shard_map/ppermute | solution.py:24
  66.7 17.9 %collective-permute-start.21 = (bf16[32,4096]{1,0:T(8,128)(2,1)S(1)}, bf16[32,4096]{1,0:T(8,128)(2,1)S(1)}, u32[]{:S(2)}, u32[]{:S(2)}) collective-permute-start(bf16[32,4096]{1,0:T(8,128)(2,1)S(1)} %collective-permute-done.16), channel_id=1, source_target_pairs={{0,1},{1,2},{2,3},{3,4},{4,5},{5,6},{6,7},{7,0},{8,9},{9,10},{10,1... | collective-permute-start | bytes 786440 | tf_op jit(solution)/shard_map/ppermute | solution.py:24
  67.1 17.4 %collective-permute-start.22 = (bf16[32,4096]{1,0:T(8,128)(2,1)S(1)}, bf16[32,4096]{1,0:T(8,128)(2,1)S(1)}, u32[]{:S(2)}, u32[]{:S(2)}) collective-permute-start(bf16[32,4096]{1,0:T(8,128)(2,1)S(1)} %collective-permute-done.16), channel_id=1, source_target_pairs={{0,7},{1,0},{2,1},{3,2},{4,3},{5,4},{6,5},{7,6},{8,15},{9,8},{10,9... | collective-permute-start | bytes 786440 | tf_op jit(solution)/shard_map/ppermute | solution.py:24
  73.8 10.7 %collective-permute-start.19 = (bf16[32,4096]{1,0:T(8,128)(2,1)S(1)}, bf16[32,4096]{1,0:T(8,128)(2,1)S(1)}, u32[]{:S(2)}, u32[]{:S(2)}) collective-permute-start(bf16[32,4096]{1,0:T(8,128)(2,1)S(1)} %collective-permute-done.17), channel_id=1, source_target_pairs={{0,1},{1,2},{2,3},{3,4},{4,5},{5,6},{6,7},{7,0},{8,9},{9,10},{10,1... | collective-permute-start | bytes 786440 | tf_op jit(solution)/shard_map/ppermute | solution.py:24
  74.2 10.3 %collective-permute-start.20 = (bf16[32,4096]{1,0:T(8,128)(2,1)S(1)}, bf16[32,4096]{1,0:T(8,128)(2,1)S(1)}, u32[]{:S(2)}, u32[]{:S(2)}) collective-permute-start(bf16[32,4096]{1,0:T(8,128)(2,1)S(1)} %collective-permute-done.18), channel_id=1, source_target_pairs={{0,7},{1,0},{2,1},{3,2},{4,3},{5,4},{6,5},{7,6},{8,15},{9,8},{10,9... | collective-permute-start | bytes 786440 | tf_op jit(solution)/shard_map/ppermute | solution.py:24
  77.1 15.1 %collective-permute-start.25 = (bf16[64,4096]{1,0:T(8,128)(2,1)S(1)}, bf16[64,4096]{1,0:T(8,128)(2,1)S(1)}, u32[]{:S(2)}, u32[]{:S(2)}) collective-permute-start(bf16[64,4096]{1,0:T(8,128)(2,1)S(1)} %pad_maximum_fusion), channel_id=1, source_target_pairs={{0,8},{1,9},{2,10},{3,11},{4,12},{5,13},{6,14},{7,15},{8,0},{9,1},... | collective-permute-start | bytes 1572872 | tf_op jit(solution)/shard_map/ppermute | solution.py:24
  84.6 7.7 %collective-permute-start.23 = (bf16[16,4096]{1,0:T(8,128)(2,1)S(1)}, bf16[16,4096]{1,0:T(8,128)(2,1)S(1)}, u32[]{:S(2)}, u32[]{:S(2)}) collective-permute-start(bf16[16,4096]{1,0:T(8,128)(2,1)S(1)} %slice.179), channel_id=1, source_target_pairs={{0,1},{1,2},{2,3},{3,4},{4,5},{5,6},{6,7},{7,0},{8,9},{9,10},{10,1... | collective-permute-start | bytes 393224 | tf_op jit(solution)/shard_map/ppermute | solution.py:24
  84.9 7.4 %collective-permute-start.24 = (bf16[16,4096]{1,0:T(8,128)(2,1)S(1)}, bf16[16,4096]{1,0:T(8,128)(2,1)S(1)}, u32[]{:S(2)}, u32[]{:S(2)}) collective-permute-start(bf16[16,4096]{1,0:T(8,128)(2,1)S(1)} %slice.180), channel_id=1, source_target_pairs={{0,7},{1,0},{2,1},{3,2},{4,3},{5,4},{6,5},{7,6},{8,15},{9,8},{10,9... | collective-permute-start | bytes 393224 | tf_op jit(solution)/shard_map/ppermute | solution.py:24
  92.4 9.2 %collective-permute-start.28 = (bf16[32,4096]{1,0:T(8,128)(2,1)S(1)}, bf16[32,4096]{1,0:T(8,128)(2,1)S(1)}, u32[]{:S(2)}, u32[]{:S(2)}) collective-permute-start(bf16[32,4096]{1,0:T(8,128)(2,1)S(1)} %pad_maximum_fusion.1), channel_id=1, source_target_pairs={{0,8},{1,9},{2,10},{3,11},{4,12},{5,13},{6,14},{7,15},{8,0},{9,1},... | collective-permute-start | bytes 786440 | tf_op jit(solution)/shard_map/ppermute | solution.py:24
  93.5 7.6 %collective-permute-start.26 = (bf16[32,4096]{1,0:T(8,128)(2,1)S(1)}, bf16[32,4096]{1,0:T(8,128)(2,1)S(1)}, u32[]{:S(2)}, u32[]{:S(2)}) collective-permute-start(bf16[32,4096]{1,0:T(8,128)(2,1)S(1)} %get-tuple-element.107), channel_id=1, source_target_pairs={{0,1},{1,2},{2,3},{3,4},{4,5},{5,6},{6,7},{7,0},{8,9},{9,10},{10,1... | collective-permute-start | bytes 786440 | tf_op jit(solution)/shard_map/ppermute | solution.py:24
  (14 other events, 137.0 us)

commit v4 on v3

--- a/solution.py
+++ b/solution.py
@@ -55,38 +55,42 @@
     far = product((1, 4))
     far, ring = hold((far, ring))
     far = send(far, ACROSS)
-    rest = product((1, 1), (1, -1), (1, 3), (1, -3), (1, 2), (1, -2))
+    rest = product((1, 2), (1, -2), (1, 3), (1, -3))
     side_up = send(rest[:ROWS], UP)
     side_down = send(rest[ROWS : 2 * ROWS], DOWN)
-    three = send(rest[2 * ROWS : 4 * ROWS], ACROSS)
-    two = send(rest[4 * ROWS :], ACROSS)
+    three = send(rest[2 * ROWS :], ACROSS)
     ring, rest = hold((ring, rest))
-    own4, own0, side0 = product((0, 4)), product((0, 0)), product((1, 0))
+    own4, own0, side1, side0 = (
+        product((0, 4)), product((0, 0)), product((1, 1), (1, -1)), product((1, 0))
+    )
     own3, own2, own1 = (product((0, dz), (0, -dz)) for dz in (3, 2, 1))
 
-    far, own4, own3, own2, own1, own0, side0 = hold((far, own4, own3, own2, own1, own0, side0))
+    far, own4, own3, own2, own1, own0, side1, side0 = hold(
+        (far, own4, own3, own2, own1, own0, side1, side0)
+    )
     total = bf(f32(own4) + f32(far))
     up, down = send(total[:HALF], UP), send(total[HALF:], DOWN)
 
-    up, down, three, side_up, side_down, own3, side0 = hold(
-        (up, down, three, side_up, side_down, own3, side0)
+    up, down, three, side_up, side_down, own3, side1, side0 = hold(
+        (up, down, three, side_up, side_down, own3, side1, side0)
     )
+    one = send(bf(f32(side1) + jnp.concatenate([f32(side_up), f32(side_down)], 0)), ACROSS)
     pad = jnp.zeros((HALF, up.shape[1]), jnp.bfloat16)
     own3 = f32(own3) + f32(three)
     up = send(bf(own3[:ROWS] + f32(jnp.concatenate([up, pad], 0))), UP)
     down = send(bf(own3[ROWS:] + f32(jnp.concatenate([pad, down], 0))), DOWN)
-    side = send(bf(f32(side0) + f32(side_up) + f32(side_down)), ACROSS)
 
-    up, down, two, own2 = hold((up, down, two, own2))
-    own2 = f32(own2) + f32(two)
-    up = send(bf(own2[:ROWS] + f32(up)), UP)
-    down = send(bf(own2[ROWS:] + f32(down)), DOWN)
+    up, down, own2, side0 = hold((up, down, own2, side0))
+    zero = send(side0, ACROSS)
+    up = send(bf(f32(own2[:ROWS]) + f32(up)), UP)
+    down = send(bf(f32(own2[ROWS:]) + f32(down)), DOWN)
 
-    up, down, own1 = hold((up, down, own1))
-    up = send(bf(f32(own1[:ROWS]) + f32(up)), UP)
-    down = send(bf(f32(own1[ROWS:]) + f32(down)), DOWN)
+    up, down, own1, one = hold((up, down, own1, one))
+    own1 = f32(own1) + f32(one)
+    up = send(bf(own1[:ROWS] + f32(up)), UP)
+    down = send(bf(own1[ROWS:] + f32(down)), DOWN)
 
-    attended = f32(own0) + f32(side) + f32(up) + f32(down)
+    attended = f32(own0) + f32(zero) + f32(up) + f32(down)
 
     stream = f32(residual_in) + attended + out_bias
     center = jnp.mean(stream, axis=1, keepdims=True)

time: 105 us -> 103 us (0.981)
  starting transfers between devices: 54.3 us -> 51.1 us
  waiting for transfers between devices: 29.1 us -> 30.9 us
    ppermute x29, starting transfers between devices: 54.3 us -> 51.1 us  [send(): return lax.ppermute(value, 'tensor', pairs)]
    ppermute x29, waiting for transfers between devices: 29.1 us -> 30.9 us  [send(): return lax.ppermute(value, 'tensor', pairs)]
    dot_general x8 -> x9, matrix products: 3.92 us -> 4.25 us  [product(): return bf(jnp.dot(rows, out_weight, preferred_element_type=jnp.float32))]
  transfers between devices with their start and end apart: 29 -> 29, of which waited for: 14 -> 12; matrix products, arithmetic and copies ran while one was open for 13% -> 13% of each run, Pallas kernels for 0% -> 0%
where the time goes in v4:
time: 103 us
  starting transfers between devices  51.1 us (50%)
  waiting for transfers between devices  30.9 us (30%)
  matrix products  14.2 us (14%)
  local copies, waits for them, and re-layouts  3.12 us (3%)
  other arithmetic  2.7 us (3%)
  between operations  1.28 us (1%)
    ppermute x29, starting transfers between devices, send(): return lax.ppermute(value, 'tensor', pairs)  51.1 us
    ppermute x29, waiting for transfers between devices, send(): return lax.ppermute(value, 'tensor', pairs)  30.9 us
    dot_general x4, matrix products, units(): gate = jnp.dot(rows, gate_weight, preferred_element_type=jnp.float32)  5.27 us
    dot_general x4, matrix products, units(): up = jnp.dot(rows, up_weight, preferred_element_type=jnp.float32)  4.67 us
    dot_general x9, matrix products, product(): return bf(jnp.dot(rows, out_weight, preferred_element_type=jnp.float32))  4.25 us
  transfers between devices with their start and end apart: 29, of which 12 were waited for; matrix products, arithmetic and copies ran while one was open for 13% of the time, Pallas kernels for 0%

profile of v4, /device:TPU:6, one launch (start us, length us, event | category | flops | bytes accessed | tf_op | source)
XLA Modules:
  0.0 103.3 jit_solution(9692583938202401740)
XLA Ops:
  2.8 1.6 %collective-permute-start = (bf16[32,4096]{1,0:T(8,128)(2,1)S(1)}, bf16[32,4096]{1,0:T(8,128)(2,1)S(1)}, u32[]{:S(2)}, u32[]{:S(2)}) collective-permute-start(bf16[32,4096]{1,0:T(8,128)(2,1)S(1)} %convolution_convert_fusion.8), channel_id=1, source_target_pairs={{0,8},{1,9},{2,10},{3,11},{4,12},{5,13},{6,14},{7,15},{8,0},{9,1},... | collective-permute-start | bytes 786440 | tf_op jit(solution)/shard_map/ppermute | solution.py:24
  5.5 2.0 %collective-permute-start.4 = (bf16[32,4096]{1,0:T(8,128)(2,1)S(1)}, bf16[32,4096]{1,0:T(8,128)(2,1)S(1)}, u32[]{:S(2)}, u32[]{:S(2)}) collective-permute-start(bf16[32,4096]{1,0:T(8,128)(2,1)S(1)} %get-tuple-element.109), channel_id=1, source_target_pairs={{0,1},{1,2},{2,3},{3,4},{4,5},{5,6},{6,7},{7,0},{8,9},{9,10},{10,1... | collective-permute-start | bytes 786440 | tf_op jit(solution)/shard_map/ppermute | solution.py:24
  7.5 4.0 %collective-permute-start.5 = (bf16[32,4096]{1,0:T(8,128)(2,1)S(1)}, bf16[32,4096]{1,0:T(8,128)(2,1)S(1)}, u32[]{:S(2)}, u32[]{:S(2)}) collective-permute-start(bf16[32,4096]{1,0:T(8,128)(2,1)S(1)} %get-tuple-element.108), channel_id=1, source_target_pairs={{0,7},{1,0},{2,1},{3,2},{4,3},{5,4},{6,5},{7,6},{8,15},{9,8},{10,9... | collective-permute-start | bytes 786440 | tf_op jit(solution)/shard_map/ppermute | solution.py:24
  15.1 3.2 %collective-permute-start.2 = (bf16[16,4096]{1,0:T(8,128)(2,1)S(1)}, bf16[16,4096]{1,0:T(8,128)(2,1)S(1)}, u32[]{:S(2)}, u32[]{:S(2)}) collective-permute-start(bf16[16,4096]{1,0:T(8,128)(2,1)S(1)} %get-tuple-element.114), channel_id=1, source_target_pairs={{0,7},{1,0},{2,1},{3,2},{4,3},{5,4},{6,5},{7,6},{8,15},{9,8},{10,9... | collective-permute-start | bytes 393224 | tf_op jit(solution)/shard_map/ppermute | solution.py:24
  18.4 2.9 %collective-permute-done.1 = bf16[16,4096]{1,0:T(8,128)(2,1)S(1)} collective-permute-done((bf16[16,4096]{1,0:T(8,128)(2,1)S(1)}, bf16[16,4096]{1,0:T(8,128)(2,1)S(1)}, u32[]{:S(2)}, u32[]{:S(2)}) %collective-permute-start.1) | collective-permute-done | bytes 131104 | tf_op jit(solution)/shard_map/ppermute | solution.py:24
  22.3 2.0 %collective-permute-start.6 = (bf16[32,4096]{1,0:T(8,128)(2,1)S(1)}, bf16[32,4096]{1,0:T(8,128)(2,1)S(1)}, u32[]{:S(2)}, u32[]{:S(2)}) collective-permute-start(bf16[32,4096]{1,0:T(8,128)(2,1)S(1)} %get-tuple-element.107), channel_id=1, source_target_pairs={{0,1},{1,2},{2,3},{3,4},{4,5},{5,6},{6,7},{7,0},{8,9},{9,10},{10,1... | collective-permute-start | bytes 786440 | tf_op jit(solution)/shard_map/ppermute | solution.py:24
  24.4 4.0 %collective-permute-start.7 = (bf16[32,4096]{1,0:T(8,128)(2,1)S(1)}, bf16[32,4096]{1,0:T(8,128)(2,1)S(1)}, u32[]{:S(2)}, u32[]{:S(2)}) collective-permute-start(bf16[32,4096]{1,0:T(8,128)(2,1)S(1)} %get-tuple-element.106), channel_id=1, source_target_pairs={{0,7},{1,0},{2,1},{3,2},{4,3},{5,4},{6,5},{7,6},{8,15},{9,8},{10,9... | collective-permute-start | bytes 786440 | tf_op jit(solution)/shard_map/ppermute | solution.py:24
  28.5 1.7 %collective-permute-start.11 = (bf16[64,4096]{1,0:T(8,128)(2,1)S(1)}, bf16[64,4096]{1,0:T(8,128)(2,1)S(1)}, u32[]{:S(2)}, u32[]{:S(2)}) collective-permute-start(bf16[64,4096]{1,0:T(8,128)(2,1)S(1)} %add_convert_fusion), channel_id=1, source_target_pairs={{0,8},{1,9},{2,10},{3,11},{4,12},{5,13},{6,14},{7,15},{8,0},{9,1},... | collective-permute-start | bytes 1572872 | tf_op jit(solution)/shard_map/ppermute | solution.py:24
  30.2 3.6 %collective-permute-done.6 = bf16[32,4096]{1,0:T(8,128)(2,1)S(1)} collective-permute-done((bf16[32,4096]{1,0:T(8,128)(2,1)S(1)}, bf16[32,4096]{1,0:T(8,128)(2,1)S(1)}, u32[]{:S(2)}, u32[]{:S(2)}) %collective-permute-start.6) | collective-permute-done | bytes 262176 | tf_op jit(solution)/shard_map/ppermute | solution.py:24
  33.9 3.1 %collective-permute-start.10 = (bf16[32,4096]{1,0:T(8,128)(2,1)S(1)}, bf16[32,4096]{1,0:T(8,128)(2,1)S(1)}, u32[]{:S(2)}, u32[]{:S(2)}) collective-permute-start(bf16[32,4096]{1,0:T(8,128)(2,1)S(1)} %get-tuple-element.112), channel_id=1, source_target_pairs={{0,7},{1,0},{2,1},{3,2},{4,3},{5,4},{6,5},{7,6},{8,15},{9,8},{10,9... | collective-permute-start | bytes 786440 | tf_op jit(solution)/shard_map/ppermute | solution.py:24
  38.6 4.9 %collective-permute-done.11 = bf16[64,4096]{1,0:T(8,128)(2,1)S(1)} collective-permute-done((bf16[64,4096]{1,0:T(8,128)(2,1)S(1)}, bf16[64,4096]{1,0:T(8,128)(2,1)S(1)}, u32[]{:S(2)}, u32[]{:S(2)}) %collective-permute-start.11) | collective-permute-done | bytes 524320 | tf_op jit(solution)/shard_map/ppermute | solution.py:24
  44.9 3.2 %collective-permute-start.13 = (bf16[32,4096]{1,0:T(8,128)(2,1)S(1)}, bf16[32,4096]{1,0:T(8,128)(2,1)S(1)}, u32[]{:S(2)}, u32[]{:S(2)}) collective-permute-start(bf16[32,4096]{1,0:T(8,128)(2,1)S(1)} %get-tuple-element.105), channel_id=1, source_target_pairs={{0,7},{1,0},{2,1},{3,2},{4,3},{5,4},{6,5},{7,6},{8,15},{9,8},{10,9... | collective-permute-start | bytes 786440 | tf_op jit(solution)/shard_map/ppermute | solution.py:24
  48.1 4.3 %collective-permute-done.12 = bf16[32,4096]{1,0:T(8,128)(2,1)S(1)} collective-permute-done((bf16[32,4096]{1,0:T(8,128)(2,1)S(1)}, bf16[32,4096]{1,0:T(8,128)(2,1)S(1)}, u32[]{:S(2)}, u32[]{:S(2)}) %collective-permute-start.12) | collective-permute-done | bytes 262176 | tf_op jit(solution)/shard_map/ppermute | solution.py:24
  53.3 3.3 %collective-permute-start.15 = (bf16[32,4096]{1,0:T(8,128)(2,1)S(1)}, bf16[32,4096]{1,0:T(8,128)(2,1)}, u32[]{:S(2)}, u32[]{:S(2)}) collective-permute-start(bf16[32,4096]{1,0:T(8,128)(2,1)S(1)} %add_convert_fusion.1), channel_id=1, source_target_pairs={{0,7},{1,0},{2,1},{3,2},{4,3},{5,4},{6,5},{7,6},{8,15},{9,8},{10,9... | collective-permute-start | bytes 786440 | tf_op jit(solution)/shard_map/ppermute | solution.py:24
  58.2 3.0 %collective-permute-done.14 = bf16[32,4096]{1,0:T(8,128)(2,1)S(1)} collective-permute-done((bf16[32,4096]{1,0:T(8,128)(2,1)S(1)}, bf16[32,4096]{1,0:T(8,128)(2,1)S(1)}, u32[]{:S(2)}, u32[]{:S(2)}) %collective-permute-start.14) | collective-permute-done | bytes 262176 | tf_op jit(solution)/shard_map/ppermute | solution.py:24
  61.2 1.8 %collective-permute-done.16 = bf16[32,4096]{1,0:T(8,128)(2,1)S(1)} collective-permute-done((bf16[32,4096]{1,0:T(8,128)(2,1)S(1)}, bf16[32,4096]{1,0:T(8,128)(2,1)S(1)}, u32[]{:S(2)}, u32[]{:S(2)}) %collective-permute-start.16) | collective-permute-done | bytes 262176 | tf_op jit(solution)/shard_map/ppermute | solution.py:24
  63.0 2.9 %collective-permute-start.17 = (bf16[32,4096]{1,0:T(8,128)(2,1)S(1)}, bf16[32,4096]{1,0:T(8,128)(2,1)S(1)}, u32[]{:S(2)}, u32[]{:S(2)}) collective-permute-start(bf16[32,4096]{1,0:T(8,128)(2,1)S(1)} %collective-permute-done.14), channel_id=1, source_target_pairs={{0,1},{1,2},{2,3},{3,4},{4,5},{5,6},{6,7},{7,0},{8,9},{9,10},{10,1... | collective-permute-start | bytes 786440 | tf_op jit(solution)/shard_map/ppermute | solution.py:24
  66.2 2.0 %collective-permute-start.21 = (bf16[32,4096]{1,0:T(8,128)(2,1)S(1)}, bf16[32,4096]{1,0:T(8,128)(2,1)S(1)}, u32[]{:S(2)}, u32[]{:S(2)}) collective-permute-start(bf16[32,4096]{1,0:T(8,128)(2,1)S(1)} %collective-permute-done.16), channel_id=1, source_target_pairs={{0,1},{1,2},{2,3},{3,4},{4,5},{5,6},{6,7},{7,0},{8,9},{9,10},{10,1... | collective-permute-start | bytes 786440 | tf_op jit(solution)/shard_map/ppermute | solution.py:24
  69.5 3.8 %collective-permute-done.17 = bf16[32,4096]{1,0:T(8,128)(2,1)S(1)} collective-permute-done((bf16[32,4096]{1,0:T(8,128)(2,1)S(1)}, bf16[32,4096]{1,0:T(8,128)(2,1)S(1)}, u32[]{:S(2)}, u32[]{:S(2)}) %collective-permute-start.17) | collective-permute-done | bytes 262176 | tf_op jit(solution)/shard_map/ppermute | solution.py:24
  74.8 1.7 %collective-permute-start.19 = (bf16[32,4096]{1,0:T(8,128)(2,1)S(1)}, bf16[32,4096]{1,0:T(8,128)(2,1)S(1)}, u32[]{:S(2)}, u32[]{:S(2)}) collective-permute-start(bf16[32,4096]{1,0:T(8,128)(2,1)S(1)} %collective-permute-done.17), channel_id=1, source_target_pairs={{0,1},{1,2},{2,3},{3,4},{4,5},{5,6},{6,7},{7,0},{8,9},{9,10},{10,1... | collective-permute-start | bytes 786440 | tf_op jit(solution)/shard_map/ppermute | solution.py:24
  80.8 3.1 %fusion.80 = f32[128,512]{1,0:T(8,128)S(1)} fusion(bf16[128,4096]{1,0:T(8,128)(2,1)S(1)} %constant_dynamic-update-slice_fusion, bf16[4096,512]{1,0:T(8,128)(2,1)} %param.14), kind=kOutput, calls=%fused_computation.193 | convolution fusion | flops 536870912 | bytes 5505024 | tf_op jit(solution)/shard_map/dot_general | solution.py:104
  86.4 2.8 %collective-permute-start.24 = (bf16[16,4096]{1,0:T(8,128)(2,1)S(1)}, bf16[16,4096]{1,0:T(8,128)(2,1)S(1)}, u32[]{:S(2)}, u32[]{:S(2)}) collective-permute-start(bf16[16,4096]{1,0:T(8,128)(2,1)S(1)} %slice.176), channel_id=1, source_target_pairs={{0,7},{1,0},{2,1},{3,2},{4,3},{5,4},{6,5},{7,6},{8,15},{9,8},{10,9... | collective-permute-start | bytes 393224 | tf_op jit(solution)/shard_map/ppermute | solution.py:24
  89.2 2.8 %collective-permute-done.23 = bf16[16,4096]{1,0:T(8,128)(2,1)S(1)} collective-permute-done((bf16[16,4096]{1,0:T(8,128)(2,1)S(1)}, bf16[16,4096]{1,0:T(8,128)(2,1)S(1)}, u32[]{:S(2)}, u32[]{:S(2)}) %collective-permute-start.23) | collective-permute-done | bytes 131104 | tf_op jit(solution)/shard_map/ppermute | solution.py:24
  93.4 2.6 %collective-permute-start.27 = (bf16[32,4096]{1,0:T(8,128)(2,1)S(1)}, bf16[32,4096]{1,0:T(8,128)(2,1)S(1)}, u32[]{:S(2)}, u32[]{:S(2)}) collective-permute-start(bf16[32,4096]{1,0:T(8,128)(2,1)S(1)} %get-tuple-element.110), channel_id=1, source_target_pairs={{0,7},{1,0},{2,1},{3,2},{4,3},{5,4},{6,5},{7,6},{8,15},{9,8},{10,9... | collective-permute-start | bytes 786440 | tf_op jit(solution)/shard_map/ppermute | solution.py:24
  (125 shorter events, 31.3 us)
Async XLA Ops:
  2.8 12.2 %collective-permute-start = (bf16[32,4096]{1,0:T(8,128)(2,1)S(1)}, bf16[32,4096]{1,0:T(8,128)(2,1)S(1)}, u32[]{:S(2)}, u32[]{:S(2)}) collective-permute-start(bf16[32,4096]{1,0:T(8,128)(2,1)S(1)} %convolution_convert_fusion.8), channel_id=1, source_target_pairs={{0,8},{1,9},{2,10},{3,11},{4,12},{5,13},{6,14},{7,15},{8,0},{9,1},... | collective-permute-start | bytes 786440 | tf_op jit(solution)/shard_map/ppermute | solution.py:24
  4.9 17.2 %collective-permute-start.3 = (bf16[64,4096]{1,0:T(8,128)(2,1)S(1)}, bf16[64,4096]{1,0:T(8,128)(2,1)S(1)}, u32[]{:S(2)}, u32[]{:S(2)}) collective-permute-start(bf16[64,4096]{1,0:T(8,128)(2,1)S(1)} %slice.194), channel_id=1, source_target_pairs={{0,8},{1,9},{2,10},{3,11},{4,12},{5,13},{6,14},{7,15},{8,0},{9,1},... | collective-permute-start | bytes 1572872 | tf_op jit(solution)/shard_map/ppermute | solution.py:24
  5.5 12.9 %collective-permute-start.4 = (bf16[32,4096]{1,0:T(8,128)(2,1)S(1)}, bf16[32,4096]{1,0:T(8,128)(2,1)S(1)}, u32[]{:S(2)}, u32[]{:S(2)}) collective-permute-start(bf16[32,4096]{1,0:T(8,128)(2,1)S(1)} %get-tuple-element.109), channel_id=1, source_target_pairs={{0,1},{1,2},{2,3},{3,4},{4,5},{5,6},{6,7},{7,0},{8,9},{9,10},{10,1... | collective-permute-start | bytes 786440 | tf_op jit(solution)/shard_map/ppermute | solution.py:24
  7.5 10.8 %collective-permute-start.5 = (bf16[32,4096]{1,0:T(8,128)(2,1)S(1)}, bf16[32,4096]{1,0:T(8,128)(2,1)S(1)}, u32[]{:S(2)}, u32[]{:S(2)}) collective-permute-start(bf16[32,4096]{1,0:T(8,128)(2,1)S(1)} %get-tuple-element.108), channel_id=1, source_target_pairs={{0,7},{1,0},{2,1},{3,2},{4,3},{5,4},{6,5},{7,6},{8,15},{9,8},{10,9... | collective-permute-start | bytes 786440 | tf_op jit(solution)/shard_map/ppermute | solution.py:24
  22.3 11.4 %collective-permute-start.6 = (bf16[32,4096]{1,0:T(8,128)(2,1)S(1)}, bf16[32,4096]{1,0:T(8,128)(2,1)S(1)}, u32[]{:S(2)}, u32[]{:S(2)}) collective-permute-start(bf16[32,4096]{1,0:T(8,128)(2,1)S(1)} %get-tuple-element.107), channel_id=1, source_target_pairs={{0,1},{1,2},{2,3},{3,4},{4,5},{5,6},{6,7},{7,0},{8,9},{9,10},{10,1... | collective-permute-start | bytes 786440 | tf_op jit(solution)/shard_map/ppermute | solution.py:24
  24.4 9.4 %collective-permute-start.7 = (bf16[32,4096]{1,0:T(8,128)(2,1)S(1)}, bf16[32,4096]{1,0:T(8,128)(2,1)S(1)}, u32[]{:S(2)}, u32[]{:S(2)}) collective-permute-start(bf16[32,4096]{1,0:T(8,128)(2,1)S(1)} %get-tuple-element.106), channel_id=1, source_target_pairs={{0,7},{1,0},{2,1},{3,2},{4,3},{5,4},{6,5},{7,6},{8,15},{9,8},{10,9... | collective-permute-start | bytes 786440 | tf_op jit(solution)/shard_map/ppermute | solution.py:24
  28.5 14.9 %collective-permute-start.11 = (bf16[64,4096]{1,0:T(8,128)(2,1)S(1)}, bf16[64,4096]{1,0:T(8,128)(2,1)S(1)}, u32[]{:S(2)}, u32[]{:S(2)}) collective-permute-start(bf16[64,4096]{1,0:T(8,128)(2,1)S(1)} %add_convert_fusion), channel_id=1, source_target_pairs={{0,8},{1,9},{2,10},{3,11},{4,12},{5,13},{6,14},{7,15},{8,0},{9,1},... | collective-permute-start | bytes 1572872 | tf_op jit(solution)/shard_map/ppermute | solution.py:24
  33.9 9.6 %collective-permute-start.10 = (bf16[32,4096]{1,0:T(8,128)(2,1)S(1)}, bf16[32,4096]{1,0:T(8,128)(2,1)S(1)}, u32[]{:S(2)}, u32[]{:S(2)}) collective-permute-start(bf16[32,4096]{1,0:T(8,128)(2,1)S(1)} %get-tuple-element.112), channel_id=1, source_target_pairs={{0,7},{1,0},{2,1},{3,2},{4,3},{5,4},{6,5},{7,6},{8,15},{9,8},{10,9... | collective-permute-start | bytes 786440 | tf_op jit(solution)/shard_map/ppermute | solution.py:24
  37.0 7.6 %collective-permute-start.9 = (bf16[32,4096]{1,0:T(8,128)(2,1)S(1)}, bf16[32,4096]{1,0:T(8,128)(2,1)S(1)}, u32[]{:S(2)}, u32[]{:S(2)}) collective-permute-start(bf16[32,4096]{1,0:T(8,128)(2,1)S(1)} %get-tuple-element.113), channel_id=1, source_target_pairs={{0,1},{1,2},{2,3},{3,4},{4,5},{5,6},{6,7},{7,0},{8,9},{9,10},{10,1... | collective-permute-start | bytes 786440 | tf_op jit(solution)/shard_map/ppermute | solution.py:24
  37.0 11.1 %collective-permute-start.8 = (bf16[32,4096]{1,0:T(8,128)(2,1)S(1)}, bf16[32,4096]{1,0:T(8,128)(2,1)S(1)}, u32[]{:S(2)}, u32[]{:S(2)}) collective-permute-start(bf16[32,4096]{1,0:T(8,128)(2,1)S(1)} %convolution_convert_fusion.5), channel_id=1, source_target_pairs={{0,8},{1,9},{2,10},{3,11},{4,12},{5,13},{6,14},{7,15},{8,0},{9,1},... | collective-permute-start | bytes 786440 | tf_op jit(solution)/shard_map/ppermute | solution.py:24
  44.8 7.7 %collective-permute-start.12 = (bf16[32,4096]{1,0:T(8,128)(2,1)S(1)}, bf16[32,4096]{1,0:T(8,128)(2,1)S(1)}, u32[]{:S(2)}, u32[]{:S(2)}) collective-permute-start(bf16[32,4096]{1,0:T(8,128)(2,1)S(1)} %get-tuple-element.104), channel_id=1, source_target_pairs={{0,1},{1,2},{2,3},{3,4},{4,5},{5,6},{6,7},{7,0},{8,9},{9,10},{10,1... | collective-permute-start | bytes 786440 | tf_op jit(solution)/shard_map/ppermute | solution.py:24
  44.9 7.6 %collective-permute-start.13 = (bf16[32,4096]{1,0:T(8,128)(2,1)S(1)}, bf16[32,4096]{1,0:T(8,128)(2,1)S(1)}, u32[]{:S(2)}, u32[]{:S(2)}) collective-permute-start(bf16[32,4096]{1,0:T(8,128)(2,1)S(1)} %get-tuple-element.105), channel_id=1, source_target_pairs={{0,7},{1,0},{2,1},{3,2},{4,3},{5,4},{6,5},{7,6},{8,15},{9,8},{10,9... | collective-permute-start | bytes 786440 | tf_op jit(solution)/shard_map/ppermute | solution.py:24
  53.2 8.0 %collective-permute-start.14 = (bf16[32,4096]{1,0:T(8,128)(2,1)S(1)}, bf16[32,4096]{1,0:T(8,128)(2,1)S(1)}, u32[]{:S(2)}, u32[]{:S(2)}) collective-permute-start(bf16[32,4096]{1,0:T(8,128)(2,1)S(1)} %add_convert_fusion.1), channel_id=1, source_target_pairs={{0,1},{1,2},{2,3},{3,4},{4,5},{5,6},{6,7},{7,0},{8,9},{9,10},{10,1... | collective-permute-start | bytes 786440 | tf_op jit(solution)/shard_map/ppermute | solution.py:24
  53.3 7.9 %collective-permute-start.15 = (bf16[32,4096]{1,0:T(8,128)(2,1)S(1)}, bf16[32,4096]{1,0:T(8,128)(2,1)}, u32[]{:S(2)}, u32[]{:S(2)}) collective-permute-start(bf16[32,4096]{1,0:T(8,128)(2,1)S(1)} %add_convert_fusion.1), channel_id=1, source_target_pairs={{0,7},{1,0},{2,1},{3,2},{4,3},{5,4},{6,5},{7,6},{8,15},{9,8},{10,9... | collective-permute-start | bytes 786440 | tf_op jit(solution)/shard_map/ppermute | solution.py:24
  63.0 10.3 %collective-permute-start.17 = (bf16[32,4096]{1,0:T(8,128)(2,1)S(1)}, bf16[32,4096]{1,0:T(8,128)(2,1)S(1)}, u32[]{:S(2)}, u32[]{:S(2)}) collective-permute-start(bf16[32,4096]{1,0:T(8,128)(2,1)S(1)} %collective-permute-done.14), channel_id=1, source_target_pairs={{0,1},{1,2},{2,3},{3,4},{4,5},{5,6},{6,7},{7,0},{8,9},{9,10},{10,1... | collective-permute-start | bytes 786440 | tf_op jit(solution)/shard_map/ppermute | solution.py:24
  65.9 8.9 %collective-permute-start.18 = (bf16[32,4096]{1,0:T(8,128)(2,1)}, bf16[32,4096]{1,0:T(8,128)(2,1)S(1)}, u32[]{:S(2)}, u32[]{:S(2)}) collective-permute-start(bf16[32,4096]{1,0:T(8,128)(2,1)} %collective-permute-done.15), channel_id=1, source_target_pairs={{0,7},{1,0},{2,1},{3,2},{4,3},{5,4},{6,5},{7,6},{8,15},{9,8},{10,9... | collective-permute-start | bytes 786440 | tf_op jit(solution)/shard_map/ppermute | solution.py:24
  66.2 19.3 %collective-permute-start.21 = (bf16[32,4096]{1,0:T(8,128)(2,1)S(1)}, bf16[32,4096]{1,0:T(8,128)(2,1)S(1)}, u32[]{:S(2)}, u32[]{:S(2)}) collective-permute-start(bf16[32,4096]{1,0:T(8,128)(2,1)S(1)} %collective-permute-done.16), channel_id=1, source_target_pairs={{0,1},{1,2},{2,3},{3,4},{4,5},{5,6},{6,7},{7,0},{8,9},{9,10},{10,1... | collective-permute-start | bytes 786440 | tf_op jit(solution)/shard_map/ppermute | solution.py:24
  68.3 17.2 %collective-permute-start.22 = (bf16[32,4096]{1,0:T(8,128)(2,1)S(1)}, bf16[32,4096]{1,0:T(8,128)(2,1)S(1)}, u32[]{:S(2)}, u32[]{:S(2)}) collective-permute-start(bf16[32,4096]{1,0:T(8,128)(2,1)S(1)} %collective-permute-done.16), channel_id=1, source_target_pairs={{0,7},{1,0},{2,1},{3,2},{4,3},{5,4},{6,5},{7,6},{8,15},{9,8},{10,9... | collective-permute-start | bytes 786440 | tf_op jit(solution)/shard_map/ppermute | solution.py:24
  74.8 10.7 %collective-permute-start.19 = (bf16[32,4096]{1,0:T(8,128)(2,1)S(1)}, bf16[32,4096]{1,0:T(8,128)(2,1)S(1)}, u32[]{:S(2)}, u32[]{:S(2)}) collective-permute-start(bf16[32,4096]{1,0:T(8,128)(2,1)S(1)} %collective-permute-done.17), channel_id=1, source_target_pairs={{0,1},{1,2},{2,3},{3,4},{4,5},{5,6},{6,7},{7,0},{8,9},{9,10},{10,1... | collective-permute-start | bytes 786440 | tf_op jit(solution)/shard_map/ppermute | solution.py:24
  76.6 9.0 %collective-permute-start.20 = (bf16[32,4096]{1,0:T(8,128)(2,1)S(1)}, bf16[32,4096]{1,0:T(8,128)(2,1)S(1)}, u32[]{:S(2)}, u32[]{:S(2)}) collective-permute-start(bf16[32,4096]{1,0:T(8,128)(2,1)S(1)} %collective-permute-done.18), channel_id=1, source_target_pairs={{0,7},{1,0},{2,1},{3,2},{4,3},{5,4},{6,5},{7,6},{8,15},{9,8},{10,9... | collective-permute-start | bytes 786440 | tf_op jit(solution)/shard_map/ppermute | solution.py:24
  78.1 13.9 %collective-permute-start.25 = (bf16[64,4096]{1,0:T(8,128)(2,1)S(1)}, bf16[64,4096]{1,0:T(8,128)(2,1)S(1)}, u32[]{:S(2)}, u32[]{:S(2)}) collective-permute-start(bf16[64,4096]{1,0:T(8,128)(2,1)S(1)} %pad_maximum_fusion), channel_id=1, source_target_pairs={{0,8},{1,9},{2,10},{3,11},{4,12},{5,13},{6,14},{7,15},{8,0},{9,1},... | collective-permute-start | bytes 1572872 | tf_op jit(solution)/shard_map/ppermute | solution.py:24
  92.2 8.3 %collective-permute-start.28 = (bf16[32,4096]{1,0:T(8,128)(2,1)S(1)}, bf16[32,4096]{1,0:T(8,128)(2,1)S(1)}, u32[]{:S(2)}, u32[]{:S(2)}) collective-permute-start(bf16[32,4096]{1,0:T(8,128)(2,1)S(1)} %pad_maximum_fusion.1), channel_id=1, source_target_pairs={{0,8},{1,9},{2,10},{3,11},{4,12},{5,13},{6,14},{7,15},{8,0},{9,1},... | collective-permute-start | bytes 786440 | tf_op jit(solution)/shard_map/ppermute | solution.py:24
  92.7 7.7 %collective-permute-start.26 = (bf16[32,4096]{1,0:T(8,128)(2,1)S(1)}, bf16[32,4096]{1,0:T(8,128)(2,1)S(1)}, u32[]{:S(2)}, u32[]{:S(2)}) collective-permute-start(bf16[32,4096]{1,0:T(8,128)(2,1)S(1)} %get-tuple-element.111), channel_id=1, source_target_pairs={{0,1},{1,2},{2,3},{3,4},{4,5},{5,6},{6,7},{7,0},{8,9},{9,10},{10,1... | collective-permute-start | bytes 786440 | tf_op jit(solution)/shard_map/ppermute | solution.py:24
  93.4 7.0 %collective-permute-start.27 = (bf16[32,4096]{1,0:T(8,128)(2,1)S(1)}, bf16[32,4096]{1,0:T(8,128)(2,1)S(1)}, u32[]{:S(2)}, u32[]{:S(2)}) collective-permute-start(bf16[32,4096]{1,0:T(8,128)(2,1)S(1)} %get-tuple-element.110), channel_id=1, source_target_pairs={{0,7},{1,0},{2,1},{3,2},{4,3},{5,4},{6,5},{7,6},{8,15},{9,8},{10,9... | collective-permute-start | bytes 786440 | tf_op jit(solution)/shard_map/ppermute | solution.py:24
  (14 other events, 119.3 us)

commit v5 on v4

--- a/solution.py
+++ b/solution.py
@@ -60,19 +60,15 @@
     side_down = send(rest[ROWS : 2 * ROWS], DOWN)
     three = send(rest[2 * ROWS :], ACROSS)
     ring, rest = hold((ring, rest))
-    own4, own0, side1, side0 = (
-        product((0, 4)), product((0, 0)), product((1, 1), (1, -1)), product((1, 0))
-    )
+    own4 = product((0, 4))
+    far, own4, ring = hold((far, own4, ring))
+    total = bf(f32(own4) + f32(far))
+    up, down = send(total[:HALF], UP), send(total[HALF:], DOWN)
+    own0, side1, side0 = product((0, 0)), product((1, 1), (1, -1)), product((1, 0))
     own3, own2, own1 = (product((0, dz), (0, -dz)) for dz in (3, 2, 1))
 
-    far, own4, own3, own2, own1, own0, side1, side0 = hold(
-        (far, own4, own3, own2, own1, own0, side1, side0)
-    )
-    total = bf(f32(own4) + f32(far))
-    up, down = send(total[:HALF], UP), send(total[HALF:], DOWN)
-
-    up, down, three, side_up, side_down, own3, side1, side0 = hold(
-        (up, down, three, side_up, side_down, own3, side1, side0)
+    up, down, three, side_up, side_down, own3, own2, own1, own0, side1, side0 = hold(
+        (up, down, three, side_up, side_down, own3, own2, own1, own0, side1, side0)
     )
     one = send(bf(f32(side1) + jnp.concatenate([f32(side_up), f32(side_down)], 0)), ACROSS)
     pad = jnp.zeros((HALF, up.shape[1]), jnp.bfloat16)

time: 103 us -> 103 us (level)
  starting transfers between devices: 51.1 us -> 53.9 us
  waiting for transfers between devices: 30.9 us -> 28.1 us
    ppermute x29, waiting for transfers between devices: 30.9 us -> 28.1 us  [send(): return lax.ppermute(value, 'tensor', pairs)]
    ppermute x29, starting transfers between devices: 51.1 us -> 53.9 us  [send(): return lax.ppermute(value, 'tensor', pairs)]
  transfers between devices with their start and end apart: 29 -> 29, of which waited for: 12 -> 11; matrix products, arithmetic and copies ran while one was open for 13% -> 13% of each run, Pallas kernels for 0% -> 0%
where the time goes in v5:
time: 103 us
  starting transfers between devices  53.9 us (52%)
  waiting for transfers between devices  28.1 us (27%)
  matrix products  14.2 us (14%)
  local copies, waits for them, and re-layouts  3.12 us (3%)
  other arithmetic  2.7 us (3%)
  between operations  1.3 us (1%)
    ppermute x29, starting transfers between devices, send(): return lax.ppermute(value, 'tensor', pairs)  53.9 us
    ppermute x29, waiting for transfers between devices, send(): return lax.ppermute(value, 'tensor', pairs)  28.1 us
    dot_general x4, matrix products, units(): gate = jnp.dot(rows, gate_weight, preferred_element_type=jnp.float32)  5.27 us
    dot_general x4, matrix products, units(): up = jnp.dot(rows, up_weight, preferred_element_type=jnp.float32)  4.67 us
    dot_general x9, matrix products, product(): return bf(jnp.dot(rows, out_weight, preferred_element_type=jnp.float32))  4.23 us
  transfers between devices with their start and end apart: 29, of which 11 were waited for; matrix products, arithmetic and copies ran while one was open for 13% of the time, Pallas kernels for 0%

profile of v5, /device:TPU:6, one launch (start us, length us, event | category | flops | bytes accessed | tf_op | source)
XLA Modules:
  0.0 103.3 jit_solution(14293673736294429899)
XLA Ops:
  2.8 1.6 %collective-permute-start = (bf16[32,4096]{1,0:T(8,128)(2,1)S(1)}, bf16[32,4096]{1,0:T(8,128)(2,1)S(1)}, u32[]{:S(2)}, u32[]{:S(2)}) collective-permute-start(bf16[32,4096]{1,0:T(8,128)(2,1)S(1)} %convolution_convert_fusion.8), channel_id=1, source_target_pairs={{0,8},{1,9},{2,10},{3,11},{4,12},{5,13},{6,14},{7,15},{8,0},{9,1},... | collective-permute-start | bytes 786440 | tf_op jit(solution)/shard_map/ppermute | solution.py:24
  5.5 2.0 %collective-permute-start.4 = (bf16[32,4096]{1,0:T(8,128)(2,1)S(1)}, bf16[32,4096]{1,0:T(8,128)(2,1)S(1)}, u32[]{:S(2)}, u32[]{:S(2)}) collective-permute-start(bf16[32,4096]{1,0:T(8,128)(2,1)S(1)} %get-tuple-element.105), channel_id=1, source_target_pairs={{0,1},{1,2},{2,3},{3,4},{4,5},{5,6},{6,7},{7,0},{8,9},{9,10},{10,1... | collective-permute-start | bytes 786440 | tf_op jit(solution)/shard_map/ppermute | solution.py:24
  7.5 4.0 %collective-permute-start.5 = (bf16[32,4096]{1,0:T(8,128)(2,1)S(1)}, bf16[32,4096]{1,0:T(8,128)(2,1)S(1)}, u32[]{:S(2)}, u32[]{:S(2)}) collective-permute-start(bf16[32,4096]{1,0:T(8,128)(2,1)S(1)} %get-tuple-element.104), channel_id=1, source_target_pairs={{0,7},{1,0},{2,1},{3,2},{4,3},{5,4},{6,5},{7,6},{8,15},{9,8},{10,9... | collective-permute-start | bytes 786440 | tf_op jit(solution)/shard_map/ppermute | solution.py:24
  12.2 2.0 %collective-permute-start.1 = (bf16[16,4096]{1,0:T(8,128)(2,1)S(1)}, bf16[16,4096]{1,0:T(8,128)(2,1)S(1)}, u32[]{:S(2)}, u32[]{:S(2)}) collective-permute-start(bf16[16,4096]{1,0:T(8,128)(2,1)S(1)} %get-tuple-element.119), channel_id=1, source_target_pairs={{0,1},{1,2},{2,3},{3,4},{4,5},{5,6},{6,7},{7,0},{8,9},{9,10},{10,1... | collective-permute-start | bytes 393224 | tf_op jit(solution)/shard_map/ppermute | solution.py:24
  14.2 4.0 %collective-permute-start.2 = (bf16[16,4096]{1,0:T(8,128)(2,1)S(1)}, bf16[16,4096]{1,0:T(8,128)(2,1)S(1)}, u32[]{:S(2)}, u32[]{:S(2)}) collective-permute-start(bf16[16,4096]{1,0:T(8,128)(2,1)S(1)} %get-tuple-element.118), channel_id=1, source_target_pairs={{0,7},{1,0},{2,1},{3,2},{4,3},{5,4},{6,5},{7,6},{8,15},{9,8},{10,9... | collective-permute-start | bytes 393224 | tf_op jit(solution)/shard_map/ppermute | solution.py:24
  22.3 2.0 %collective-permute-start.6 = (bf16[32,4096]{1,0:T(8,128)(2,1)S(1)}, bf16[32,4096]{1,0:T(8,128)(2,1)S(1)}, u32[]{:S(2)}, u32[]{:S(2)}) collective-permute-start(bf16[32,4096]{1,0:T(8,128)(2,1)S(1)} %get-tuple-element.103), channel_id=1, source_target_pairs={{0,1},{1,2},{2,3},{3,4},{4,5},{5,6},{6,7},{7,0},{8,9},{9,10},{10,1... | collective-permute-start | bytes 786440 | tf_op jit(solution)/shard_map/ppermute | solution.py:24
  24.4 4.0 %collective-permute-start.7 = (bf16[32,4096]{1,0:T(8,128)(2,1)S(1)}, bf16[32,4096]{1,0:T(8,128)(2,1)S(1)}, u32[]{:S(2)}, u32[]{:S(2)}) collective-permute-start(bf16[32,4096]{1,0:T(8,128)(2,1)S(1)} %get-tuple-element.102), channel_id=1, source_target_pairs={{0,7},{1,0},{2,1},{3,2},{4,3},{5,4},{6,5},{7,6},{8,15},{9,8},{10,9... | collective-permute-start | bytes 786440 | tf_op jit(solution)/shard_map/ppermute | solution.py:24
  28.5 1.7 %collective-permute-start.11 = (bf16[64,4096]{1,0:T(8,128)(2,1)S(1)}, bf16[64,4096]{1,0:T(8,128)(2,1)S(1)}, u32[]{:S(2)}, u32[]{:S(2)}) collective-permute-start(bf16[64,4096]{1,0:T(8,128)(2,1)S(1)} %add_convert_fusion), channel_id=1, source_target_pairs={{0,8},{1,9},{2,10},{3,11},{4,12},{5,13},{6,14},{7,15},{8,0},{9,1},... | collective-permute-start | bytes 1572872 | tf_op jit(solution)/shard_map/ppermute | solution.py:24
  30.2 3.6 %collective-permute-done.6 = bf16[32,4096]{1,0:T(8,128)(2,1)S(1)} collective-permute-done((bf16[32,4096]{1,0:T(8,128)(2,1)S(1)}, bf16[32,4096]{1,0:T(8,128)(2,1)S(1)}, u32[]{:S(2)}, u32[]{:S(2)}) %collective-permute-start.6) | collective-permute-done | bytes 262176 | tf_op jit(solution)/shard_map/ppermute | solution.py:24
  33.9 3.1 %collective-permute-start.10 = (bf16[32,4096]{1,0:T(8,128)(2,1)S(1)}, bf16[32,4096]{1,0:T(8,128)(2,1)S(1)}, u32[]{:S(2)}, u32[]{:S(2)}) collective-permute-start(bf16[32,4096]{1,0:T(8,128)(2,1)S(1)} %get-tuple-element.108), channel_id=1, source_target_pairs={{0,7},{1,0},{2,1},{3,2},{4,3},{5,4},{6,5},{7,6},{8,15},{9,8},{10,9... | collective-permute-start | bytes 786440 | tf_op jit(solution)/shard_map/ppermute | solution.py:24
  38.6 4.9 %collective-permute-done.11 = bf16[64,4096]{1,0:T(8,128)(2,1)S(1)} collective-permute-done((bf16[64,4096]{1,0:T(8,128)(2,1)S(1)}, bf16[64,4096]{1,0:T(8,128)(2,1)S(1)}, u32[]{:S(2)}, u32[]{:S(2)}) %collective-permute-start.11) | collective-permute-done | bytes 524320 | tf_op jit(solution)/shard_map/ppermute | solution.py:24
  44.9 3.2 %collective-permute-start.13 = (bf16[32,4096]{1,0:T(8,128)(2,1)S(1)}, bf16[32,4096]{1,0:T(8,128)(2,1)S(1)}, u32[]{:S(2)}, u32[]{:S(2)}) collective-permute-start(bf16[32,4096]{1,0:T(8,128)(2,1)S(1)} %get-tuple-element.101), channel_id=1, source_target_pairs={{0,7},{1,0},{2,1},{3,2},{4,3},{5,4},{6,5},{7,6},{8,15},{9,8},{10,9... | collective-permute-start | bytes 786440 | tf_op jit(solution)/shard_map/ppermute | solution.py:24
  48.1 4.3 %collective-permute-done.12 = bf16[32,4096]{1,0:T(8,128)(2,1)S(1)} collective-permute-done((bf16[32,4096]{1,0:T(8,128)(2,1)S(1)}, bf16[32,4096]{1,0:T(8,128)(2,1)S(1)}, u32[]{:S(2)}, u32[]{:S(2)}) %collective-permute-start.12) | collective-permute-done | bytes 262176 | tf_op jit(solution)/shard_map/ppermute | solution.py:24
  53.3 3.3 %collective-permute-start.15 = (bf16[32,4096]{1,0:T(8,128)(2,1)S(1)}, bf16[32,4096]{1,0:T(8,128)(2,1)}, u32[]{:S(2)}, u32[]{:S(2)}) collective-permute-start(bf16[32,4096]{1,0:T(8,128)(2,1)S(1)} %add_convert_fusion.1), channel_id=1, source_target_pairs={{0,7},{1,0},{2,1},{3,2},{4,3},{5,4},{6,5},{7,6},{8,15},{9,8},{10,9... | collective-permute-start | bytes 786440 | tf_op jit(solution)/shard_map/ppermute | solution.py:24
  58.2 3.0 %collective-permute-done.14 = bf16[32,4096]{1,0:T(8,128)(2,1)S(1)} collective-permute-done((bf16[32,4096]{1,0:T(8,128)(2,1)S(1)}, bf16[32,4096]{1,0:T(8,128)(2,1)S(1)}, u32[]{:S(2)}, u32[]{:S(2)}) %collective-permute-start.14) | collective-permute-done | bytes 262176 | tf_op jit(solution)/shard_map/ppermute | solution.py:24
  61.2 1.8 %collective-permute-done.16 = bf16[32,4096]{1,0:T(8,128)(2,1)S(1)} collective-permute-done((bf16[32,4096]{1,0:T(8,128)(2,1)S(1)}, bf16[32,4096]{1,0:T(8,128)(2,1)S(1)}, u32[]{:S(2)}, u32[]{:S(2)}) %collective-permute-start.16) | collective-permute-done | bytes 262176 | tf_op jit(solution)/shard_map/ppermute | solution.py:24
  63.0 2.9 %collective-permute-start.17 = (bf16[32,4096]{1,0:T(8,128)(2,1)S(1)}, bf16[32,4096]{1,0:T(8,128)(2,1)S(1)}, u32[]{:S(2)}, u32[]{:S(2)}) collective-permute-start(bf16[32,4096]{1,0:T(8,128)(2,1)S(1)} %collective-permute-done.14), channel_id=1, source_target_pairs={{0,1},{1,2},{2,3},{3,4},{4,5},{5,6},{6,7},{7,0},{8,9},{9,10},{10,1... | collective-permute-start | bytes 786440 | tf_op jit(solution)/shard_map/ppermute | solution.py:24
  66.2 2.0 %collective-permute-start.21 = (bf16[32,4096]{1,0:T(8,128)(2,1)S(1)}, bf16[32,4096]{1,0:T(8,128)(2,1)S(1)}, u32[]{:S(2)}, u32[]{:S(2)}) collective-permute-start(bf16[32,4096]{1,0:T(8,128)(2,1)S(1)} %collective-permute-done.16), channel_id=1, source_target_pairs={{0,1},{1,2},{2,3},{3,4},{4,5},{5,6},{6,7},{7,0},{8,9},{9,10},{10,1... | collective-permute-start | bytes 786440 | tf_op jit(solution)/shard_map/ppermute | solution.py:24
  69.5 3.8 %collective-permute-done.17 = bf16[32,4096]{1,0:T(8,128)(2,1)S(1)} collective-permute-done((bf16[32,4096]{1,0:T(8,128)(2,1)S(1)}, bf16[32,4096]{1,0:T(8,128)(2,1)S(1)}, u32[]{:S(2)}, u32[]{:S(2)}) %collective-permute-start.17) | collective-permute-done | bytes 262176 | tf_op jit(solution)/shard_map/ppermute | solution.py:24
  74.8 1.7 %collective-permute-start.19 = (bf16[32,4096]{1,0:T(8,128)(2,1)S(1)}, bf16[32,4096]{1,0:T(8,128)(2,1)S(1)}, u32[]{:S(2)}, u32[]{:S(2)}) collective-permute-start(bf16[32,4096]{1,0:T(8,128)(2,1)S(1)} %collective-permute-done.17), channel_id=1, source_target_pairs={{0,1},{1,2},{2,3},{3,4},{4,5},{5,6},{6,7},{7,0},{8,9},{9,10},{10,1... | collective-permute-start | bytes 786440 | tf_op jit(solution)/shard_map/ppermute | solution.py:24
  80.8 3.1 %fusion.80 = f32[128,512]{1,0:T(8,128)S(1)} fusion(bf16[128,4096]{1,0:T(8,128)(2,1)S(1)} %constant_dynamic-update-slice_fusion, bf16[4096,512]{1,0:T(8,128)(2,1)} %param.14), kind=kOutput, calls=%fused_computation.193 | convolution fusion | flops 536870912 | bytes 5505024 | tf_op jit(solution)/shard_map/dot_general | solution.py:100
  86.4 2.8 %collective-permute-start.24 = (bf16[16,4096]{1,0:T(8,128)(2,1)S(1)}, bf16[16,4096]{1,0:T(8,128)(2,1)S(1)}, u32[]{:S(2)}, u32[]{:S(2)}) collective-permute-start(bf16[16,4096]{1,0:T(8,128)(2,1)S(1)} %slice.176), channel_id=1, source_target_pairs={{0,7},{1,0},{2,1},{3,2},{4,3},{5,4},{6,5},{7,6},{8,15},{9,8},{10,9... | collective-permute-start | bytes 393224 | tf_op jit(solution)/shard_map/ppermute | solution.py:24
  89.2 2.8 %collective-permute-done.23 = bf16[16,4096]{1,0:T(8,128)(2,1)S(1)} collective-permute-done((bf16[16,4096]{1,0:T(8,128)(2,1)S(1)}, bf16[16,4096]{1,0:T(8,128)(2,1)S(1)}, u32[]{:S(2)}, u32[]{:S(2)}) %collective-permute-start.23) | collective-permute-done | bytes 131104 | tf_op jit(solution)/shard_map/ppermute | solution.py:24
  93.4 2.6 %collective-permute-start.27 = (bf16[32,4096]{1,0:T(8,128)(2,1)S(1)}, bf16[32,4096]{1,0:T(8,128)(2,1)S(1)}, u32[]{:S(2)}, u32[]{:S(2)}) collective-permute-start(bf16[32,4096]{1,0:T(8,128)(2,1)S(1)} %get-tuple-element.106), channel_id=1, source_target_pairs={{0,7},{1,0},{2,1},{3,2},{4,3},{5,4},{6,5},{7,6},{8,15},{9,8},{10,9... | collective-permute-start | bytes 786440 | tf_op jit(solution)/shard_map/ppermute | solution.py:24
  (125 shorter events, 31.3 us)
Async XLA Ops:
  2.8 9.3 %collective-permute-start = (bf16[32,4096]{1,0:T(8,128)(2,1)S(1)}, bf16[32,4096]{1,0:T(8,128)(2,1)S(1)}, u32[]{:S(2)}, u32[]{:S(2)}) collective-permute-start(bf16[32,4096]{1,0:T(8,128)(2,1)S(1)} %convolution_convert_fusion.8), channel_id=1, source_target_pairs={{0,8},{1,9},{2,10},{3,11},{4,12},{5,13},{6,14},{7,15},{8,0},{9,1},... | collective-permute-start | bytes 786440 | tf_op jit(solution)/shard_map/ppermute | solution.py:24
  4.9 17.2 %collective-permute-start.3 = (bf16[64,4096]{1,0:T(8,128)(2,1)S(1)}, bf16[64,4096]{1,0:T(8,128)(2,1)S(1)}, u32[]{:S(2)}, u32[]{:S(2)}) collective-permute-start(bf16[64,4096]{1,0:T(8,128)(2,1)S(1)} %slice.194), channel_id=1, source_target_pairs={{0,8},{1,9},{2,10},{3,11},{4,12},{5,13},{6,14},{7,15},{8,0},{9,1},... | collective-permute-start | bytes 1572872 | tf_op jit(solution)/shard_map/ppermute | solution.py:24
  5.5 15.6 %collective-permute-start.4 = (bf16[32,4096]{1,0:T(8,128)(2,1)S(1)}, bf16[32,4096]{1,0:T(8,128)(2,1)S(1)}, u32[]{:S(2)}, u32[]{:S(2)}) collective-permute-start(bf16[32,4096]{1,0:T(8,128)(2,1)S(1)} %get-tuple-element.105), channel_id=1, source_target_pairs={{0,1},{1,2},{2,3},{3,4},{4,5},{5,6},{6,7},{7,0},{8,9},{9,10},{10,1... | collective-permute-start | bytes 786440 | tf_op jit(solution)/shard_map/ppermute | solution.py:24
  7.5 13.6 %collective-permute-start.5 = (bf16[32,4096]{1,0:T(8,128)(2,1)S(1)}, bf16[32,4096]{1,0:T(8,128)(2,1)S(1)}, u32[]{:S(2)}, u32[]{:S(2)}) collective-permute-start(bf16[32,4096]{1,0:T(8,128)(2,1)S(1)} %get-tuple-element.104), channel_id=1, source_target_pairs={{0,7},{1,0},{2,1},{3,2},{4,3},{5,4},{6,5},{7,6},{8,15},{9,8},{10,9... | collective-permute-start | bytes 786440 | tf_op jit(solution)/shard_map/ppermute | solution.py:24
  12.2 9.0 %collective-permute-start.1 = (bf16[16,4096]{1,0:T(8,128)(2,1)S(1)}, bf16[16,4096]{1,0:T(8,128)(2,1)S(1)}, u32[]{:S(2)}, u32[]{:S(2)}) collective-permute-start(bf16[16,4096]{1,0:T(8,128)(2,1)S(1)} %get-tuple-element.119), channel_id=1, source_target_pairs={{0,1},{1,2},{2,3},{3,4},{4,5},{5,6},{6,7},{7,0},{8,9},{9,10},{10,1... | collective-permute-start | bytes 393224 | tf_op jit(solution)/shard_map/ppermute | solution.py:24
  22.3 11.4 %collective-permute-start.6 = (bf16[32,4096]{1,0:T(8,128)(2,1)S(1)}, bf16[32,4096]{1,0:T(8,128)(2,1)S(1)}, u32[]{:S(2)}, u32[]{:S(2)}) collective-permute-start(bf16[32,4096]{1,0:T(8,128)(2,1)S(1)} %get-tuple-element.103), channel_id=1, source_target_pairs={{0,1},{1,2},{2,3},{3,4},{4,5},{5,6},{6,7},{7,0},{8,9},{9,10},{10,1... | collective-permute-start | bytes 786440 | tf_op jit(solution)/shard_map/ppermute | solution.py:24
  24.4 9.4 %collective-permute-start.7 = (bf16[32,4096]{1,0:T(8,128)(2,1)S(1)}, bf16[32,4096]{1,0:T(8,128)(2,1)S(1)}, u32[]{:S(2)}, u32[]{:S(2)}) collective-permute-start(bf16[32,4096]{1,0:T(8,128)(2,1)S(1)} %get-tuple-element.102), channel_id=1, source_target_pairs={{0,7},{1,0},{2,1},{3,2},{4,3},{5,4},{6,5},{7,6},{8,15},{9,8},{10,9... | collective-permute-start | bytes 786440 | tf_op jit(solution)/shard_map/ppermute | solution.py:24
  28.5 14.9 %collective-permute-start.11 = (bf16[64,4096]{1,0:T(8,128)(2,1)S(1)}, bf16[64,4096]{1,0:T(8,128)(2,1)S(1)}, u32[]{:S(2)}, u32[]{:S(2)}) collective-permute-start(bf16[64,4096]{1,0:T(8,128)(2,1)S(1)} %add_convert_fusion), channel_id=1, source_target_pairs={{0,8},{1,9},{2,10},{3,11},{4,12},{5,13},{6,14},{7,15},{8,0},{9,1},... | collective-permute-start | bytes 1572872 | tf_op jit(solution)/shard_map/ppermute | solution.py:24
  33.9 9.6 %collective-permute-start.10 = (bf16[32,4096]{1,0:T(8,128)(2,1)S(1)}, bf16[32,4096]{1,0:T(8,128)(2,1)S(1)}, u32[]{:S(2)}, u32[]{:S(2)}) collective-permute-start(bf16[32,4096]{1,0:T(8,128)(2,1)S(1)} %get-tuple-element.108), channel_id=1, source_target_pairs={{0,7},{1,0},{2,1},{3,2},{4,3},{5,4},{6,5},{7,6},{8,15},{9,8},{10,9... | collective-permute-start | bytes 786440 | tf_op jit(solution)/shard_map/ppermute | solution.py:24
  37.0 7.6 %collective-permute-start.9 = (bf16[32,4096]{1,0:T(8,128)(2,1)S(1)}, bf16[32,4096]{1,0:T(8,128)(2,1)S(1)}, u32[]{:S(2)}, u32[]{:S(2)}) collective-permute-start(bf16[32,4096]{1,0:T(8,128)(2,1)S(1)} %get-tuple-element.109), channel_id=1, source_target_pairs={{0,1},{1,2},{2,3},{3,4},{4,5},{5,6},{6,7},{7,0},{8,9},{9,10},{10,1... | collective-permute-start | bytes 786440 | tf_op jit(solution)/shard_map/ppermute | solution.py:24
  37.0 11.1 %collective-permute-start.8 = (bf16[32,4096]{1,0:T(8,128)(2,1)S(1)}, bf16[32,4096]{1,0:T(8,128)(2,1)S(1)}, u32[]{:S(2)}, u32[]{:S(2)}) collective-permute-start(bf16[32,4096]{1,0:T(8,128)(2,1)S(1)} %convolution_convert_fusion.5), channel_id=1, source_target_pairs={{0,8},{1,9},{2,10},{3,11},{4,12},{5,13},{6,14},{7,15},{8,0},{9,1},... | collective-permute-start | bytes 786440 | tf_op jit(solution)/shard_map/ppermute | solution.py:24
  44.8 7.7 %collective-permute-start.12 = (bf16[32,4096]{1,0:T(8,128)(2,1)S(1)}, bf16[32,4096]{1,0:T(8,128)(2,1)S(1)}, u32[]{:S(2)}, u32[]{:S(2)}) collective-permute-start(bf16[32,4096]{1,0:T(8,128)(2,1)S(1)} %get-tuple-element.100), channel_id=1, source_target_pairs={{0,1},{1,2},{2,3},{3,4},{4,5},{5,6},{6,7},{7,0},{8,9},{9,10},{10,1... | collective-permute-start | bytes 786440 | tf_op jit(solution)/shard_map/ppermute | solution.py:24
  44.9 7.6 %collective-permute-start.13 = (bf16[32,4096]{1,0:T(8,128)(2,1)S(1)}, bf16[32,4096]{1,0:T(8,128)(2,1)S(1)}, u32[]{:S(2)}, u32[]{:S(2)}) collective-permute-start(bf16[32,4096]{1,0:T(8,128)(2,1)S(1)} %get-tuple-element.101), channel_id=1, source_target_pairs={{0,7},{1,0},{2,1},{3,2},{4,3},{5,4},{6,5},{7,6},{8,15},{9,8},{10,9... | collective-permute-start | bytes 786440 | tf_op jit(solution)/shard_map/ppermute | solution.py:24
  53.2 8.0 %collective-permute-start.14 = (bf16[32,4096]{1,0:T(8,128)(2,1)S(1)}, bf16[32,4096]{1,0:T(8,128)(2,1)S(1)}, u32[]{:S(2)}, u32[]{:S(2)}) collective-permute-start(bf16[32,4096]{1,0:T(8,128)(2,1)S(1)} %add_convert_fusion.1), channel_id=1, source_target_pairs={{0,1},{1,2},{2,3},{3,4},{4,5},{5,6},{6,7},{7,0},{8,9},{9,10},{10,1... | collective-permute-start | bytes 786440 | tf_op jit(solution)/shard_map/ppermute | solution.py:24
  53.3 7.9 %collective-permute-start.15 = (bf16[32,4096]{1,0:T(8,128)(2,1)S(1)}, bf16[32,4096]{1,0:T(8,128)(2,1)}, u32[]{:S(2)}, u32[]{:S(2)}) collective-permute-start(bf16[32,4096]{1,0:T(8,128)(2,1)S(1)} %add_convert_fusion.1), channel_id=1, source_target_pairs={{0,7},{1,0},{2,1},{3,2},{4,3},{5,4},{6,5},{7,6},{8,15},{9,8},{10,9... | collective-permute-start | bytes 786440 | tf_op jit(solution)/shard_map/ppermute | solution.py:24
  63.0 10.3 %collective-permute-start.17 = (bf16[32,4096]{1,0:T(8,128)(2,1)S(1)}, bf16[32,4096]{1,0:T(8,128)(2,1)S(1)}, u32[]{:S(2)}, u32[]{:S(2)}) collective-permute-start(bf16[32,4096]{1,0:T(8,128)(2,1)S(1)} %collective-permute-done.14), channel_id=1, source_target_pairs={{0,1},{1,2},{2,3},{3,4},{4,5},{5,6},{6,7},{7,0},{8,9},{9,10},{10,1... | collective-permute-start | bytes 786440 | tf_op jit(solution)/shard_map/ppermute | solution.py:24
  65.9 8.9 %collective-permute-start.18 = (bf16[32,4096]{1,0:T(8,128)(2,1)}, bf16[32,4096]{1,0:T(8,128)(2,1)S(1)}, u32[]{:S(2)}, u32[]{:S(2)}) collective-permute-start(bf16[32,4096]{1,0:T(8,128)(2,1)} %collective-permute-done.15), channel_id=1, source_target_pairs={{0,7},{1,0},{2,1},{3,2},{4,3},{5,4},{6,5},{7,6},{8,15},{9,8},{10,9... | collective-permute-start | bytes 786440 | tf_op jit(solution)/shard_map/ppermute | solution.py:24
  66.2 19.3 %collective-permute-start.21 = (bf16[32,4096]{1,0:T(8,128)(2,1)S(1)}, bf16[32,4096]{1,0:T(8,128)(2,1)S(1)}, u32[]{:S(2)}, u32[]{:S(2)}) collective-permute-start(bf16[32,4096]{1,0:T(8,128)(2,1)S(1)} %collective-permute-done.16), channel_id=1, source_target_pairs={{0,1},{1,2},{2,3},{3,4},{4,5},{5,6},{6,7},{7,0},{8,9},{9,10},{10,1... | collective-permute-start | bytes 786440 | tf_op jit(solution)/shard_map/ppermute | solution.py:24
  68.3 17.2 %collective-permute-start.22 = (bf16[32,4096]{1,0:T(8,128)(2,1)S(1)}, bf16[32,4096]{1,0:T(8,128)(2,1)S(1)}, u32[]{:S(2)}, u32[]{:S(2)}) collective-permute-start(bf16[32,4096]{1,0:T(8,128)(2,1)S(1)} %collective-permute-done.16), channel_id=1, source_target_pairs={{0,7},{1,0},{2,1},{3,2},{4,3},{5,4},{6,5},{7,6},{8,15},{9,8},{10,9... | collective-permute-start | bytes 786440 | tf_op jit(solution)/shard_map/ppermute | solution.py:24
  74.8 10.7 %collective-permute-start.19 = (bf16[32,4096]{1,0:T(8,128)(2,1)S(1)}, bf16[32,4096]{1,0:T(8,128)(2,1)S(1)}, u32[]{:S(2)}, u32[]{:S(2)}) collective-permute-start(bf16[32,4096]{1,0:T(8,128)(2,1)S(1)} %collective-permute-done.17), channel_id=1, source_target_pairs={{0,1},{1,2},{2,3},{3,4},{4,5},{5,6},{6,7},{7,0},{8,9},{9,10},{10,1... | collective-permute-start | bytes 786440 | tf_op jit(solution)/shard_map/ppermute | solution.py:24
  76.6 9.0 %collective-permute-start.20 = (bf16[32,4096]{1,0:T(8,128)(2,1)S(1)}, bf16[32,4096]{1,0:T(8,128)(2,1)S(1)}, u32[]{:S(2)}, u32[]{:S(2)}) collective-permute-start(bf16[32,4096]{1,0:T(8,128)(2,1)S(1)} %collective-permute-done.18), channel_id=1, source_target_pairs={{0,7},{1,0},{2,1},{3,2},{4,3},{5,4},{6,5},{7,6},{8,15},{9,8},{10,9... | collective-permute-start | bytes 786440 | tf_op jit(solution)/shard_map/ppermute | solution.py:24
  78.1 13.9 %collective-permute-start.25 = (bf16[64,4096]{1,0:T(8,128)(2,1)S(1)}, bf16[64,4096]{1,0:T(8,128)(2,1)S(1)}, u32[]{:S(2)}, u32[]{:S(2)}) collective-permute-start(bf16[64,4096]{1,0:T(8,128)(2,1)S(1)} %pad_maximum_fusion), channel_id=1, source_target_pairs={{0,8},{1,9},{2,10},{3,11},{4,12},{5,13},{6,14},{7,15},{8,0},{9,1},... | collective-permute-start | bytes 1572872 | tf_op jit(solution)/shard_map/ppermute | solution.py:24
  92.2 8.3 %collective-permute-start.28 = (bf16[32,4096]{1,0:T(8,128)(2,1)S(1)}, bf16[32,4096]{1,0:T(8,128)(2,1)S(1)}, u32[]{:S(2)}, u32[]{:S(2)}) collective-permute-start(bf16[32,4096]{1,0:T(8,128)(2,1)S(1)} %pad_maximum_fusion.1), channel_id=1, source_target_pairs={{0,8},{1,9},{2,10},{3,11},{4,12},{5,13},{6,14},{7,15},{8,0},{9,1},... | collective-permute-start | bytes 786440 | tf_op jit(solution)/shard_map/ppermute | solution.py:24
  92.7 7.7 %collective-permute-start.26 = (bf16[32,4096]{1,0:T(8,128)(2,1)S(1)}, bf16[32,4096]{1,0:T(8,128)(2,1)S(1)}, u32[]{:S(2)}, u32[]{:S(2)}) collective-permute-start(bf16[32,4096]{1,0:T(8,128)(2,1)S(1)} %get-tuple-element.107), channel_id=1, source_target_pairs={{0,1},{1,2},{2,3},{3,4},{4,5},{5,6},{6,7},{7,0},{8,9},{9,10},{10,1... | collective-permute-start | bytes 786440 | tf_op jit(solution)/shard_map/ppermute | solution.py:24
  (14 other events, 120.9 us)

commit v6 on v5

--- a/solution.py
+++ b/solution.py
@@ -108,7 +108,7 @@
 
     up1, down1 = send(normed, UP), send(normed, DOWN)
     other = send(normed, ACROSS)
-    up1, down1, other, normed = hold((up1, down1, other, normed))
+    up1, down1, normed = hold((up1, down1, normed))
 
     up2, down2 = send(up1, UP), send(down1, DOWN)
     side_up1, side_down1 = send(other, UP), send(other, DOWN)

time: 103 us -> 103 us (level)
  transfers between devices with their start and end apart: 29 -> 29, of which waited for: 11 -> 10; matrix products, arithmetic and copies ran while one was open for 13% -> 13% of each run, Pallas kernels for 0% -> 0%
where the time goes in v6:
time: 103 us
  starting transfers between devices  54.2 us (53%)
  waiting for transfers between devices  27.8 us (27%)
  matrix products  14.2 us (14%)
  local copies, waits for them, and re-layouts  3.12 us (3%)
  other arithmetic  2.7 us (3%)
  between operations  1.3 us (1%)
    ppermute x29, starting transfers between devices, send(): return lax.ppermute(value, 'tensor', pairs)  54.2 us
    ppermute x29, waiting for transfers between devices, send(): return lax.ppermute(value, 'tensor', pairs)  27.8 us
    dot_general x4, matrix products, units(): gate = jnp.dot(rows, gate_weight, preferred_element_type=jnp.float32)  5.27 us
    dot_general x4, matrix products, units(): up = jnp.dot(rows, up_weight, preferred_element_type=jnp.float32)  4.67 us
    dot_general x9, matrix products, product(): return bf(jnp.dot(rows, out_weight, preferred_element_type=jnp.float32))  4.23 us
  transfers between devices with their start and end apart: 29, of which 10 were waited for; matrix products, arithmetic and copies ran while one was open for 13% of the time, Pallas kernels for 0%

profile of v6, /device:TPU:6, one launch (start us, length us, event | category | flops | bytes accessed | tf_op | source)
XLA Modules:
  0.0 103.3 jit_solution(1289714483265422943)
XLA Ops:
  2.8 1.6 %collective-permute-start = (bf16[32,4096]{1,0:T(8,128)(2,1)S(1)}, bf16[32,4096]{1,0:T(8,128)(2,1)S(1)}, u32[]{:S(2)}, u32[]{:S(2)}) collective-permute-start(bf16[32,4096]{1,0:T(8,128)(2,1)S(1)} %convolution_convert_fusion.8), channel_id=1, source_target_pairs={{0,8},{1,9},{2,10},{3,11},{4,12},{5,13},{6,14},{7,15},{8,0},{9,1},... | collective-permute-start | bytes 786440 | tf_op jit(solution)/shard_map/ppermute | solution.py:24
  5.5 2.0 %collective-permute-start.4 = (bf16[32,4096]{1,0:T(8,128)(2,1)S(1)}, bf16[32,4096]{1,0:T(8,128)(2,1)S(1)}, u32[]{:S(2)}, u32[]{:S(2)}) collective-permute-start(bf16[32,4096]{1,0:T(8,128)(2,1)S(1)} %get-tuple-element.103), channel_id=1, source_target_pairs={{0,1},{1,2},{2,3},{3,4},{4,5},{5,6},{6,7},{7,0},{8,9},{9,10},{10,1... | collective-permute-start | bytes 786440 | tf_op jit(solution)/shard_map/ppermute | solution.py:24
  7.5 4.0 %collective-permute-start.5 = (bf16[32,4096]{1,0:T(8,128)(2,1)S(1)}, bf16[32,4096]{1,0:T(8,128)(2,1)S(1)}, u32[]{:S(2)}, u32[]{:S(2)}) collective-permute-start(bf16[32,4096]{1,0:T(8,128)(2,1)S(1)} %get-tuple-element.102), channel_id=1, source_target_pairs={{0,7},{1,0},{2,1},{3,2},{4,3},{5,4},{6,5},{7,6},{8,15},{9,8},{10,9... | collective-permute-start | bytes 786440 | tf_op jit(solution)/shard_map/ppermute | solution.py:24
  12.2 2.0 %collective-permute-start.1 = (bf16[16,4096]{1,0:T(8,128)(2,1)S(1)}, bf16[16,4096]{1,0:T(8,128)(2,1)S(1)}, u32[]{:S(2)}, u32[]{:S(2)}) collective-permute-start(bf16[16,4096]{1,0:T(8,128)(2,1)S(1)} %get-tuple-element.117), channel_id=1, source_target_pairs={{0,1},{1,2},{2,3},{3,4},{4,5},{5,6},{6,7},{7,0},{8,9},{9,10},{10,1... | collective-permute-start | bytes 393224 | tf_op jit(solution)/shard_map/ppermute | solution.py:24
  14.2 4.0 %collective-permute-start.2 = (bf16[16,4096]{1,0:T(8,128)(2,1)S(1)}, bf16[16,4096]{1,0:T(8,128)(2,1)S(1)}, u32[]{:S(2)}, u32[]{:S(2)}) collective-permute-start(bf16[16,4096]{1,0:T(8,128)(2,1)S(1)} %get-tuple-element.116), channel_id=1, source_target_pairs={{0,7},{1,0},{2,1},{3,2},{4,3},{5,4},{6,5},{7,6},{8,15},{9,8},{10,9... | collective-permute-start | bytes 393224 | tf_op jit(solution)/shard_map/ppermute | solution.py:24
  22.3 2.0 %collective-permute-start.6 = (bf16[32,4096]{1,0:T(8,128)(2,1)S(1)}, bf16[32,4096]{1,0:T(8,128)(2,1)S(1)}, u32[]{:S(2)}, u32[]{:S(2)}) collective-permute-start(bf16[32,4096]{1,0:T(8,128)(2,1)S(1)} %get-tuple-element.101), channel_id=1, source_target_pairs={{0,1},{1,2},{2,3},{3,4},{4,5},{5,6},{6,7},{7,0},{8,9},{9,10},{10,1... | collective-permute-start | bytes 786440 | tf_op jit(solution)/shard_map/ppermute | solution.py:24
  24.4 4.0 %collective-permute-start.7 = (bf16[32,4096]{1,0:T(8,128)(2,1)S(1)}, bf16[32,4096]{1,0:T(8,128)(2,1)S(1)}, u32[]{:S(2)}, u32[]{:S(2)}) collective-permute-start(bf16[32,4096]{1,0:T(8,128)(2,1)S(1)} %get-tuple-element.100), channel_id=1, source_target_pairs={{0,7},{1,0},{2,1},{3,2},{4,3},{5,4},{6,5},{7,6},{8,15},{9,8},{10,9... | collective-permute-start | bytes 786440 | tf_op jit(solution)/shard_map/ppermute | solution.py:24
  28.5 1.7 %collective-permute-start.11 = (bf16[64,4096]{1,0:T(8,128)(2,1)S(1)}, bf16[64,4096]{1,0:T(8,128)(2,1)S(1)}, u32[]{:S(2)}, u32[]{:S(2)}) collective-permute-start(bf16[64,4096]{1,0:T(8,128)(2,1)S(1)} %add_convert_fusion), channel_id=1, source_target_pairs={{0,8},{1,9},{2,10},{3,11},{4,12},{5,13},{6,14},{7,15},{8,0},{9,1},... | collective-permute-start | bytes 1572872 | tf_op jit(solution)/shard_map/ppermute | solution.py:24
  30.2 3.6 %collective-permute-done.6 = bf16[32,4096]{1,0:T(8,128)(2,1)S(1)} collective-permute-done((bf16[32,4096]{1,0:T(8,128)(2,1)S(1)}, bf16[32,4096]{1,0:T(8,128)(2,1)S(1)}, u32[]{:S(2)}, u32[]{:S(2)}) %collective-permute-start.6) | collective-permute-done | bytes 262176 | tf_op jit(solution)/shard_map/ppermute | solution.py:24
  33.9 3.1 %collective-permute-start.10 = (bf16[32,4096]{1,0:T(8,128)(2,1)S(1)}, bf16[32,4096]{1,0:T(8,128)(2,1)S(1)}, u32[]{:S(2)}, u32[]{:S(2)}) collective-permute-start(bf16[32,4096]{1,0:T(8,128)(2,1)S(1)} %get-tuple-element.106), channel_id=1, source_target_pairs={{0,7},{1,0},{2,1},{3,2},{4,3},{5,4},{6,5},{7,6},{8,15},{9,8},{10,9... | collective-permute-start | bytes 786440 | tf_op jit(solution)/shard_map/ppermute | solution.py:24
  38.6 4.9 %collective-permute-done.11 = bf16[64,4096]{1,0:T(8,128)(2,1)S(1)} collective-permute-done((bf16[64,4096]{1,0:T(8,128)(2,1)S(1)}, bf16[64,4096]{1,0:T(8,128)(2,1)S(1)}, u32[]{:S(2)}, u32[]{:S(2)}) %collective-permute-start.11) | collective-permute-done | bytes 524320 | tf_op jit(solution)/shard_map/ppermute | solution.py:24
  44.9 3.2 %collective-permute-start.13 = (bf16[32,4096]{1,0:T(8,128)(2,1)S(1)}, bf16[32,4096]{1,0:T(8,128)(2,1)S(1)}, u32[]{:S(2)}, u32[]{:S(2)}) collective-permute-start(bf16[32,4096]{1,0:T(8,128)(2,1)S(1)} %get-tuple-element.99), channel_id=1, source_target_pairs={{0,7},{1,0},{2,1},{3,2},{4,3},{5,4},{6,5},{7,6},{8,15},{9,8},{10,9... | collective-permute-start | bytes 786440 | tf_op jit(solution)/shard_map/ppermute | solution.py:24
  48.1 4.3 %collective-permute-done.12 = bf16[32,4096]{1,0:T(8,128)(2,1)S(1)} collective-permute-done((bf16[32,4096]{1,0:T(8,128)(2,1)S(1)}, bf16[32,4096]{1,0:T(8,128)(2,1)S(1)}, u32[]{:S(2)}, u32[]{:S(2)}) %collective-permute-start.12) | collective-permute-done | bytes 262176 | tf_op jit(solution)/shard_map/ppermute | solution.py:24
  53.3 3.3 %collective-permute-start.15 = (bf16[32,4096]{1,0:T(8,128)(2,1)S(1)}, bf16[32,4096]{1,0:T(8,128)(2,1)}, u32[]{:S(2)}, u32[]{:S(2)}) collective-permute-start(bf16[32,4096]{1,0:T(8,128)(2,1)S(1)} %add_convert_fusion.1), channel_id=1, source_target_pairs={{0,7},{1,0},{2,1},{3,2},{4,3},{5,4},{6,5},{7,6},{8,15},{9,8},{10,9... | collective-permute-start | bytes 786440 | tf_op jit(solution)/shard_map/ppermute | solution.py:24
  58.2 4.3 %collective-permute-done.14 = bf16[32,4096]{1,0:T(8,128)(2,1)S(1)} collective-permute-done((bf16[32,4096]{1,0:T(8,128)(2,1)S(1)}, bf16[32,4096]{1,0:T(8,128)(2,1)S(1)}, u32[]{:S(2)}, u32[]{:S(2)}) %collective-permute-start.14) | collective-permute-done | bytes 262176 | tf_op jit(solution)/shard_map/ppermute | solution.py:24
  62.5 3.4 %collective-permute-start.16 = (bf16[32,4096]{1,0:T(8,128)(2,1)S(1)}, bf16[32,4096]{1,0:T(8,128)(2,1)S(1)}, u32[]{:S(2)}, u32[]{:S(2)}) collective-permute-start(bf16[32,4096]{1,0:T(8,128)(2,1)S(1)} %collective-permute-done.14), channel_id=1, source_target_pairs={{0,1},{1,2},{2,3},{3,4},{4,5},{5,6},{6,7},{7,0},{8,9},{9,10},{10,1... | collective-permute-start | bytes 786440 | tf_op jit(solution)/shard_map/ppermute | solution.py:24
  66.1 2.2 %collective-permute-start.21 = (bf16[32,4096]{1,0:T(8,128)(2,1)S(1)}, bf16[32,4096]{1,0:T(8,128)(2,1)S(1)}, u32[]{:S(2)}, u32[]{:S(2)}) collective-permute-start(bf16[32,4096]{1,0:T(8,128)(2,1)S(1)} %collective-permute-done.18), channel_id=1, source_target_pairs={{0,1},{1,2},{2,3},{3,4},{4,5},{5,6},{6,7},{7,0},{8,9},{9,10},{10,1... | collective-permute-start | bytes 786440 | tf_op jit(solution)/shard_map/ppermute | solution.py:24
  69.3 3.8 %collective-permute-done.16 = bf16[32,4096]{1,0:T(8,128)(2,1)S(1)} collective-permute-done((bf16[32,4096]{1,0:T(8,128)(2,1)S(1)}, bf16[32,4096]{1,0:T(8,128)(2,1)S(1)}, u32[]{:S(2)}, u32[]{:S(2)}) %collective-permute-start.16) | collective-permute-done | bytes 262176 | tf_op jit(solution)/shard_map/ppermute | solution.py:24
  73.2 1.6 %collective-permute-done.17 = bf16[32,4096]{1,0:T(8,128)(2,1)S(1)} collective-permute-done((bf16[32,4096]{1,0:T(8,128)(2,1)}, bf16[32,4096]{1,0:T(8,128)(2,1)S(1)}, u32[]{:S(2)}, u32[]{:S(2)}) %collective-permute-start.17) | collective-permute-done | bytes 262176 | tf_op jit(solution)/shard_map/ppermute | solution.py:24
  74.8 1.7 %collective-permute-start.19 = (bf16[32,4096]{1,0:T(8,128)(2,1)S(1)}, bf16[32,4096]{1,0:T(8,128)(2,1)S(1)}, u32[]{:S(2)}, u32[]{:S(2)}) collective-permute-start(bf16[32,4096]{1,0:T(8,128)(2,1)S(1)} %collective-permute-done.16), channel_id=1, source_target_pairs={{0,1},{1,2},{2,3},{3,4},{4,5},{5,6},{6,7},{7,0},{8,9},{9,10},{10,1... | collective-permute-start | bytes 786440 | tf_op jit(solution)/shard_map/ppermute | solution.py:24
  80.8 3.1 %fusion.80 = f32[128,512]{1,0:T(8,128)S(1)} fusion(bf16[128,4096]{1,0:T(8,128)(2,1)S(1)} %constant_dynamic-update-slice_fusion, bf16[4096,512]{1,0:T(8,128)(2,1)} %param.14), kind=kOutput, calls=%fused_computation.193 | convolution fusion | flops 536870912 | bytes 5505024 | tf_op jit(solution)/shard_map/dot_general | solution.py:100
  86.4 2.8 %collective-permute-start.24 = (bf16[16,4096]{1,0:T(8,128)(2,1)S(1)}, bf16[16,4096]{1,0:T(8,128)(2,1)S(1)}, u32[]{:S(2)}, u32[]{:S(2)}) collective-permute-start(bf16[16,4096]{1,0:T(8,128)(2,1)S(1)} %slice.176), channel_id=1, source_target_pairs={{0,7},{1,0},{2,1},{3,2},{4,3},{5,4},{6,5},{7,6},{8,15},{9,8},{10,9... | collective-permute-start | bytes 393224 | tf_op jit(solution)/shard_map/ppermute | solution.py:24
  89.2 2.8 %collective-permute-done.23 = bf16[16,4096]{1,0:T(8,128)(2,1)S(1)} collective-permute-done((bf16[16,4096]{1,0:T(8,128)(2,1)S(1)}, bf16[16,4096]{1,0:T(8,128)(2,1)S(1)}, u32[]{:S(2)}, u32[]{:S(2)}) %collective-permute-start.23) | collective-permute-done | bytes 131104 | tf_op jit(solution)/shard_map/ppermute | solution.py:24
  93.4 2.6 %collective-permute-start.27 = (bf16[32,4096]{1,0:T(8,128)(2,1)S(1)}, bf16[32,4096]{1,0:T(8,128)(2,1)S(1)}, u32[]{:S(2)}, u32[]{:S(2)}) collective-permute-start(bf16[32,4096]{1,0:T(8,128)(2,1)S(1)} %get-tuple-element.104), channel_id=1, source_target_pairs={{0,7},{1,0},{2,1},{3,2},{4,3},{5,4},{6,5},{7,6},{8,15},{9,8},{10,9... | collective-permute-start | bytes 786440 | tf_op jit(solution)/shard_map/ppermute | solution.py:24
  (125 shorter events, 29.6 us)
Async XLA Ops:
  2.8 9.3 %collective-permute-start = (bf16[32,4096]{1,0:T(8,128)(2,1)S(1)}, bf16[32,4096]{1,0:T(8,128)(2,1)S(1)}, u32[]{:S(2)}, u32[]{:S(2)}) collective-permute-start(bf16[32,4096]{1,0:T(8,128)(2,1)S(1)} %convolution_convert_fusion.8), channel_id=1, source_target_pairs={{0,8},{1,9},{2,10},{3,11},{4,12},{5,13},{6,14},{7,15},{8,0},{9,1},... | collective-permute-start | bytes 786440 | tf_op jit(solution)/shard_map/ppermute | solution.py:24
  4.9 17.2 %collective-permute-start.3 = (bf16[64,4096]{1,0:T(8,128)(2,1)S(1)}, bf16[64,4096]{1,0:T(8,128)(2,1)S(1)}, u32[]{:S(2)}, u32[]{:S(2)}) collective-permute-start(bf16[64,4096]{1,0:T(8,128)(2,1)S(1)} %slice.194), channel_id=1, source_target_pairs={{0,8},{1,9},{2,10},{3,11},{4,12},{5,13},{6,14},{7,15},{8,0},{9,1},... | collective-permute-start | bytes 1572872 | tf_op jit(solution)/shard_map/ppermute | solution.py:24
  5.5 15.6 %collective-permute-start.4 = (bf16[32,4096]{1,0:T(8,128)(2,1)S(1)}, bf16[32,4096]{1,0:T(8,128)(2,1)S(1)}, u32[]{:S(2)}, u32[]{:S(2)}) collective-permute-start(bf16[32,4096]{1,0:T(8,128)(2,1)S(1)} %get-tuple-element.103), channel_id=1, source_target_pairs={{0,1},{1,2},{2,3},{3,4},{4,5},{5,6},{6,7},{7,0},{8,9},{9,10},{10,1... | collective-permute-start | bytes 786440 | tf_op jit(solution)/shard_map/ppermute | solution.py:24
  7.5 13.6 %collective-permute-start.5 = (bf16[32,4096]{1,0:T(8,128)(2,1)S(1)}, bf16[32,4096]{1,0:T(8,128)(2,1)S(1)}, u32[]{:S(2)}, u32[]{:S(2)}) collective-permute-start(bf16[32,4096]{1,0:T(8,128)(2,1)S(1)} %get-tuple-element.102), channel_id=1, source_target_pairs={{0,7},{1,0},{2,1},{3,2},{4,3},{5,4},{6,5},{7,6},{8,15},{9,8},{10,9... | collective-permute-start | bytes 786440 | tf_op jit(solution)/shard_map/ppermute | solution.py:24
  12.2 9.0 %collective-permute-start.1 = (bf16[16,4096]{1,0:T(8,128)(2,1)S(1)}, bf16[16,4096]{1,0:T(8,128)(2,1)S(1)}, u32[]{:S(2)}, u32[]{:S(2)}) collective-permute-start(bf16[16,4096]{1,0:T(8,128)(2,1)S(1)} %get-tuple-element.117), channel_id=1, source_target_pairs={{0,1},{1,2},{2,3},{3,4},{4,5},{5,6},{6,7},{7,0},{8,9},{9,10},{10,1... | collective-permute-start | bytes 393224 | tf_op jit(solution)/shard_map/ppermute | solution.py:24
  22.3 11.4 %collective-permute-start.6 = (bf16[32,4096]{1,0:T(8,128)(2,1)S(1)}, bf16[32,4096]{1,0:T(8,128)(2,1)S(1)}, u32[]{:S(2)}, u32[]{:S(2)}) collective-permute-start(bf16[32,4096]{1,0:T(8,128)(2,1)S(1)} %get-tuple-element.101), channel_id=1, source_target_pairs={{0,1},{1,2},{2,3},{3,4},{4,5},{5,6},{6,7},{7,0},{8,9},{9,10},{10,1... | collective-permute-start | bytes 786440 | tf_op jit(solution)/shard_map/ppermute | solution.py:24
  24.4 9.4 %collective-permute-start.7 = (bf16[32,4096]{1,0:T(8,128)(2,1)S(1)}, bf16[32,4096]{1,0:T(8,128)(2,1)S(1)}, u32[]{:S(2)}, u32[]{:S(2)}) collective-permute-start(bf16[32,4096]{1,0:T(8,128)(2,1)S(1)} %get-tuple-element.100), channel_id=1, source_target_pairs={{0,7},{1,0},{2,1},{3,2},{4,3},{5,4},{6,5},{7,6},{8,15},{9,8},{10,9... | collective-permute-start | bytes 786440 | tf_op jit(solution)/shard_map/ppermute | solution.py:24
  28.5 14.9 %collective-permute-start.11 = (bf16[64,4096]{1,0:T(8,128)(2,1)S(1)}, bf16[64,4096]{1,0:T(8,128)(2,1)S(1)}, u32[]{:S(2)}, u32[]{:S(2)}) collective-permute-start(bf16[64,4096]{1,0:T(8,128)(2,1)S(1)} %add_convert_fusion), channel_id=1, source_target_pairs={{0,8},{1,9},{2,10},{3,11},{4,12},{5,13},{6,14},{7,15},{8,0},{9,1},... | collective-permute-start | bytes 1572872 | tf_op jit(solution)/shard_map/ppermute | solution.py:24
  33.9 9.6 %collective-permute-start.10 = (bf16[32,4096]{1,0:T(8,128)(2,1)S(1)}, bf16[32,4096]{1,0:T(8,128)(2,1)S(1)}, u32[]{:S(2)}, u32[]{:S(2)}) collective-permute-start(bf16[32,4096]{1,0:T(8,128)(2,1)S(1)} %get-tuple-element.106), channel_id=1, source_target_pairs={{0,7},{1,0},{2,1},{3,2},{4,3},{5,4},{6,5},{7,6},{8,15},{9,8},{10,9... | collective-permute-start | bytes 786440 | tf_op jit(solution)/shard_map/ppermute | solution.py:24
  37.0 7.6 %collective-permute-start.9 = (bf16[32,4096]{1,0:T(8,128)(2,1)S(1)}, bf16[32,4096]{1,0:T(8,128)(2,1)S(1)}, u32[]{:S(2)}, u32[]{:S(2)}) collective-permute-start(bf16[32,4096]{1,0:T(8,128)(2,1)S(1)} %get-tuple-element.107), channel_id=1, source_target_pairs={{0,1},{1,2},{2,3},{3,4},{4,5},{5,6},{6,7},{7,0},{8,9},{9,10},{10,1... | collective-permute-start | bytes 786440 | tf_op jit(solution)/shard_map/ppermute | solution.py:24
  37.0 11.1 %collective-permute-start.8 = (bf16[32,4096]{1,0:T(8,128)(2,1)S(1)}, bf16[32,4096]{1,0:T(8,128)(2,1)S(1)}, u32[]{:S(2)}, u32[]{:S(2)}) collective-permute-start(bf16[32,4096]{1,0:T(8,128)(2,1)S(1)} %convolution_convert_fusion.5), channel_id=1, source_target_pairs={{0,8},{1,9},{2,10},{3,11},{4,12},{5,13},{6,14},{7,15},{8,0},{9,1},... | collective-permute-start | bytes 786440 | tf_op jit(solution)/shard_map/ppermute | solution.py:24
  44.8 7.7 %collective-permute-start.12 = (bf16[32,4096]{1,0:T(8,128)(2,1)S(1)}, bf16[32,4096]{1,0:T(8,128)(2,1)S(1)}, u32[]{:S(2)}, u32[]{:S(2)}) collective-permute-start(bf16[32,4096]{1,0:T(8,128)(2,1)S(1)} %get-tuple-element.98), channel_id=1, source_target_pairs={{0,1},{1,2},{2,3},{3,4},{4,5},{5,6},{6,7},{7,0},{8,9},{9,10},{10,1... | collective-permute-start | bytes 786440 | tf_op jit(solution)/shard_map/ppermute | solution.py:24
  53.2 9.3 %collective-permute-start.14 = (bf16[32,4096]{1,0:T(8,128)(2,1)S(1)}, bf16[32,4096]{1,0:T(8,128)(2,1)S(1)}, u32[]{:S(2)}, u32[]{:S(2)}) collective-permute-start(bf16[32,4096]{1,0:T(8,128)(2,1)S(1)} %add_convert_fusion.1), channel_id=1, source_target_pairs={{0,1},{1,2},{2,3},{3,4},{4,5},{5,6},{6,7},{7,0},{8,9},{9,10},{10,1... | collective-permute-start | bytes 786440 | tf_op jit(solution)/shard_map/ppermute | solution.py:24
  53.3 9.2 %collective-permute-start.15 = (bf16[32,4096]{1,0:T(8,128)(2,1)S(1)}, bf16[32,4096]{1,0:T(8,128)(2,1)}, u32[]{:S(2)}, u32[]{:S(2)}) collective-permute-start(bf16[32,4096]{1,0:T(8,128)(2,1)S(1)} %add_convert_fusion.1), channel_id=1, source_target_pairs={{0,7},{1,0},{2,1},{3,2},{4,3},{5,4},{6,5},{7,6},{8,15},{9,8},{10,9... | collective-permute-start | bytes 786440 | tf_op jit(solution)/shard_map/ppermute | solution.py:24
  56.6 9.5 %collective-permute-start.18 = (bf16[32,4096]{1,0:T(8,128)(2,1)S(1)}, bf16[32,4096]{1,0:T(8,128)(2,1)S(1)}, u32[]{:S(2)}, u32[]{:S(2)}) collective-permute-start(bf16[32,4096]{1,0:T(8,128)(2,1)S(1)} %add_convert_fusion.1), channel_id=1, source_target_pairs={{0,8},{1,9},{2,10},{3,11},{4,12},{5,13},{6,14},{7,15},{8,0},{9,1},... | collective-permute-start | bytes 786440 | tf_op jit(solution)/shard_map/ppermute | solution.py:24
  62.5 10.7 %collective-permute-start.16 = (bf16[32,4096]{1,0:T(8,128)(2,1)S(1)}, bf16[32,4096]{1,0:T(8,128)(2,1)S(1)}, u32[]{:S(2)}, u32[]{:S(2)}) collective-permute-start(bf16[32,4096]{1,0:T(8,128)(2,1)S(1)} %collective-permute-done.14), channel_id=1, source_target_pairs={{0,1},{1,2},{2,3},{3,4},{4,5},{5,6},{6,7},{7,0},{8,9},{9,10},{10,1... | collective-permute-start | bytes 786440 | tf_op jit(solution)/shard_map/ppermute | solution.py:24
  65.9 8.9 %collective-permute-start.17 = (bf16[32,4096]{1,0:T(8,128)(2,1)}, bf16[32,4096]{1,0:T(8,128)(2,1)S(1)}, u32[]{:S(2)}, u32[]{:S(2)}) collective-permute-start(bf16[32,4096]{1,0:T(8,128)(2,1)} %collective-permute-done.15), channel_id=1, source_target_pairs={{0,7},{1,0},{2,1},{3,2},{4,3},{5,4},{6,5},{7,6},{8,15},{9,8},{10,9... | collective-permute-start | bytes 786440 | tf_op jit(solution)/shard_map/ppermute | solution.py:24
  66.1 19.4 %collective-permute-start.21 = (bf16[32,4096]{1,0:T(8,128)(2,1)S(1)}, bf16[32,4096]{1,0:T(8,128)(2,1)S(1)}, u32[]{:S(2)}, u32[]{:S(2)}) collective-permute-start(bf16[32,4096]{1,0:T(8,128)(2,1)S(1)} %collective-permute-done.18), channel_id=1, source_target_pairs={{0,1},{1,2},{2,3},{3,4},{4,5},{5,6},{6,7},{7,0},{8,9},{9,10},{10,1... | collective-permute-start | bytes 786440 | tf_op jit(solution)/shard_map/ppermute | solution.py:24
  68.3 17.2 %collective-permute-start.22 = (bf16[32,4096]{1,0:T(8,128)(2,1)S(1)}, bf16[32,4096]{1,0:T(8,128)(2,1)S(1)}, u32[]{:S(2)}, u32[]{:S(2)}) collective-permute-start(bf16[32,4096]{1,0:T(8,128)(2,1)S(1)} %collective-permute-done.18), channel_id=1, source_target_pairs={{0,7},{1,0},{2,1},{3,2},{4,3},{5,4},{6,5},{7,6},{8,15},{9,8},{10,9... | collective-permute-start | bytes 786440 | tf_op jit(solution)/shard_map/ppermute | solution.py:24
  74.8 10.7 %collective-permute-start.19 = (bf16[32,4096]{1,0:T(8,128)(2,1)S(1)}, bf16[32,4096]{1,0:T(8,128)(2,1)S(1)}, u32[]{:S(2)}, u32[]{:S(2)}) collective-permute-start(bf16[32,4096]{1,0:T(8,128)(2,1)S(1)} %collective-permute-done.16), channel_id=1, source_target_pairs={{0,1},{1,2},{2,3},{3,4},{4,5},{5,6},{6,7},{7,0},{8,9},{9,10},{10,1... | collective-permute-start | bytes 786440 | tf_op jit(solution)/shard_map/ppermute | solution.py:24
  76.6 9.0 %collective-permute-start.20 = (bf16[32,4096]{1,0:T(8,128)(2,1)S(1)}, bf16[32,4096]{1,0:T(8,128)(2,1)S(1)}, u32[]{:S(2)}, u32[]{:S(2)}) collective-permute-start(bf16[32,4096]{1,0:T(8,128)(2,1)S(1)} %collective-permute-done.17), channel_id=1, source_target_pairs={{0,7},{1,0},{2,1},{3,2},{4,3},{5,4},{6,5},{7,6},{8,15},{9,8},{10,9... | collective-permute-start | bytes 786440 | tf_op jit(solution)/shard_map/ppermute | solution.py:24
  78.1 13.9 %collective-permute-start.25 = (bf16[64,4096]{1,0:T(8,128)(2,1)S(1)}, bf16[64,4096]{1,0:T(8,128)(2,1)S(1)}, u32[]{:S(2)}, u32[]{:S(2)}) collective-permute-start(bf16[64,4096]{1,0:T(8,128)(2,1)S(1)} %pad_maximum_fusion), channel_id=1, source_target_pairs={{0,8},{1,9},{2,10},{3,11},{4,12},{5,13},{6,14},{7,15},{8,0},{9,1},... | collective-permute-start | bytes 1572872 | tf_op jit(solution)/shard_map/ppermute | solution.py:24
  92.2 8.3 %collective-permute-start.28 = (bf16[32,4096]{1,0:T(8,128)(2,1)S(1)}, bf16[32,4096]{1,0:T(8,128)(2,1)S(1)}, u32[]{:S(2)}, u32[]{:S(2)}) collective-permute-start(bf16[32,4096]{1,0:T(8,128)(2,1)S(1)} %pad_maximum_fusion.1), channel_id=1, source_target_pairs={{0,8},{1,9},{2,10},{3,11},{4,12},{5,13},{6,14},{7,15},{8,0},{9,1},... | collective-permute-start | bytes 786440 | tf_op jit(solution)/shard_map/ppermute | solution.py:24
  92.7 7.7 %collective-permute-start.26 = (bf16[32,4096]{1,0:T(8,128)(2,1)S(1)}, bf16[32,4096]{1,0:T(8,128)(2,1)S(1)}, u32[]{:S(2)}, u32[]{:S(2)}) collective-permute-start(bf16[32,4096]{1,0:T(8,128)(2,1)S(1)} %get-tuple-element.105), channel_id=1, source_target_pairs={{0,1},{1,2},{2,3},{3,4},{4,5},{5,6},{6,7},{7,0},{8,9},{9,10},{10,1... | collective-permute-start | bytes 786440 | tf_op jit(solution)/shard_map/ppermute | solution.py:24
  (14 other events, 122.0 us)
